TPU v7x, 32 devices: a whole 2x2x4 slice. The times are simulated.
32 devices in a mesh: req: 8 (over z, x), tp: 4 (over y, core).
Axes of the slice: x: 2, y: 2, z: 4, core: 2. Of those that a mesh axis runs over, the one named last changes fastest.
Arguments:
- hidden_states: bfloat16 [2048, 2048], P('req'), may hold values from -30 to 30
- norm_gain: float32 [2048], replicated, may hold values from 0.5 to 1.5
- head: bfloat16 [2048, 24576], P(None, ('req', 'tp')), may hold values from -1 to 1
- target_ids: int32 [2048], P('req'), may hold values from 0 to 24575
- lengths: int32 [8], P('req'), may hold values from 32 to 256, as said below
Outputs:
- token_logprob: float32 [2048], P('req')
- token_entropy: float32 [2048], P('req')
- seq_mean_logprob: float32 [8], P('req')
- seq_top_logit: float32 [8], P('req')
Inputs may be any that keep to these rules, and one draw needn't show every extreme that they name: `lengths`: each completion has at least 32 and at most 256 live slots; some completion has exactly 256.
All inputs are finite; a program needn't handle non-finite values.
Results may differ from a plain program's by a relative error of at most 0.0018.
Values may be sent and summed in bfloat16 or wider, within the bound.
No kernel may reach another device: no remote copies, remote signals or barrier semaphores. Data moves between devices by JAX's collectives and lax.ppermute only.
A program may use at most 128 MiB of HBM per device.

v0:
```python
import math

import jax
import jax.numpy as jnp
from jax import lax
from jax.sharding import PartitionSpec as P


def combined_all(value, axis, combine):
    everything = jax.tree.map(lambda part: lax.all_gather(part, axis), value)
    leading = jax.tree.map(lambda part: part[0], everything)

    def turn(k, so_far):
        return combine(so_far, jax.tree.map(lambda part: part[k], everything))

    return lax.fori_loop(1, lax.axis_size(axis), turn, leading)


def combine(first, second):
    top = jnp.maximum(first[0], second[0])
    left = jnp.exp(first[0] - top)
    right = jnp.exp(second[0] - top)
    return (
        top,
        first[1] * left + second[1] * right,
        first[2] * left + second[2] * right,
        first[3] + second[3],
    )


def block_stats(block, target, matrix, vocab_ids):
    logits = jnp.dot(block, matrix, preferred_element_type=jnp.float32)
    top = jnp.max(logits, axis=-1)
    shifted = jnp.exp(logits - top[:, None])
    weight_sum = jnp.sum(shifted, axis=-1)
    weighted = jnp.sum(shifted * logits, axis=-1)
    hit = vocab_ids == target[:, None]
    picked = jnp.sum(jnp.where(hit, logits, 0.0), axis=-1)
    return (top, weight_sum, weighted, picked)


def blocked_stats(block, target, matrix, vocab_ids):
    count = block.shape[0]
    step = math.gcd(count, 512)
    stats = lax.map(
        lambda a: block_stats(a[0], a[1], matrix, vocab_ids),
        (block.reshape(count // step, step, block.shape[1]), target.reshape(count // step, step)),
    )
    return tuple((s.reshape(-1) for s in stats))


def per_device(hidden_states, norm_gain, head, target_ids, lengths):
    feats = hidden_states.astype(jnp.float32)
    scale = lax.rsqrt(jnp.mean(feats * feats, axis=-1, keepdims=True) + 1e-06)
    normed = (feats * scale * norm_gain).astype(jnp.bfloat16)
    rows = hidden_states.shape[0]
    vdev = head.shape[1]
    n_req = lax.axis_size("req")
    n_tp = lax.axis_size("tp")
    my_req = lax.axis_index("req")
    vbase = (my_req * n_tp + lax.axis_index("tp")) * vdev
    columns = lax.broadcasted_iota(jnp.int32, (1, vdev), 1)
    own_vocab = columns + vbase
    block = lax.all_gather(normed, "req", axis=0, tiled=True)
    target = lax.all_gather(target_ids, "req", axis=0, tiled=True)
    stats = blocked_stats(block, target, head, own_vocab)
    gathered = tuple((new for new in stats))
    shaped = tuple((s.reshape(n_req, rows) for s in gathered))
    arrived = (
        lax.all_to_all(shaped[0], "req", split_axis=0, concat_axis=0, tiled=True),
        lax.all_to_all(shaped[1], "req", split_axis=0, concat_axis=0, tiled=True),
        lax.all_to_all(shaped[2], "req", split_axis=0, concat_axis=0, tiled=True),
        lax.all_to_all(shaped[3], "req", split_axis=0, concat_axis=0, tiled=True),
    )
    top = jnp.max(arrived[0], axis=0)
    factor = jnp.exp(arrived[0] - top[None, :])
    own = (
        top,
        jnp.sum(arrived[1] * factor, axis=0),
        jnp.sum(arrived[2] * factor, axis=0),
        jnp.sum(arrived[3], axis=0),
    )
    merged = combined_all((own[0], own[1], own[2], own[3]), "tp", combine)
    top, weight_sum, weighted, picked = merged
    log_norm = top + jnp.log(weight_sum)
    live = jnp.arange(rows, dtype=jnp.int32) < lengths[0]
    logprob = jnp.where(live, picked - log_norm, jnp.float32(0.0))
    entropy = jnp.where(live, log_norm - weighted / weight_sum, jnp.float32(0.0))
    mean_lp = (jnp.sum(logprob) / lengths[0].astype(jnp.float32)).reshape(1)
    top_live = jnp.max(jnp.where(live, top, jnp.float32(-1e30))).reshape(1)
    return (logprob, entropy, mean_lp, top_live)


def solution(mesh):
    in_specs = (P("req", None), P(), P(None, ("req", "tp")), P("req"), P("req"))
    out_specs = (P("req"), P("req"), P("req"), P("req"))
    return jax.shard_map(
        per_device, mesh=mesh, in_specs=in_specs, out_specs=out_specs, check_vma=False
    )
```

profile of v0, /device:TPU:0, one launch (start us, length us, event | category | flops | bytes accessed | tf_op | source)
XLA Modules:
  0.0 221.0 jit_solution(7297020311215462404)
XLA Ops:
  7.2 1.7 fusion.7
  8.9 2.6 %fusion.9 = bf16[256,2048]{1,0:T(8,128)(2,1)} fusion(bf16[256,2048]{1,0:T(8,128)(2,1)} %param.9, f32[2048]{0:T(1024)} %param.10, f32[256]{0:T(256)S(1)} %add_rsqrt_fusion), kind=kLoop, calls=%fused_computation.23 | loop fusion | flops 2097152 | bytes 2106368 | tf_op jit(solution)/shard_map/convert_element_type | solution.py:55
  11.6 22.5 %all-gather.4 = s32[8,1,256]{2,1,0:T(1,128)S(1)} all-gather(s32[1,1,256]{2,1,0:T(1,128)S(1)} %bitcast.102), channel_id=1, replica_groups=mesh['req'=8,'tp'=4] {'req'}, dimensions={0}, use_global_device_ids=true | all-gather | bytes 9216 | tf_op jit(solution)/shard_map/all_gather | solution.py:65
  34.1 105.2 %all-gather.11.cloned.1.call-done = bf16[2048,2048]{1,0:T(8,128)(2,1)} async-done(((bf16[256,2048]{1,0:T(8,128)(2,1)}), bf16[2048,2048]{1,0:T(8,128)(2,1)}) %all-gather.11.cloned.1.call-update) | async-done | bytes 8388624 | tf_op jit(solution)/shard_map/all_gather | solution.py:64
  139.3 17.9 %while.39 = (s32[]{:T(128)}, f32[4,512]{1,0:T(4,128)S(1)}, f32[4,512]{1,0:T(4,128)S(1)}, f32[4,512]{1,0:T(4,128)S(1)}, f32[4,512]{1,0:T(4,128)S(1)}, /*index=5*/...) while((s32[]{:T(128)}, f32[4,512]{1,0:T(4,128)S(1)}, ...), condition=%wide.region_6.7_spmd.clone, body=%wide.region_1.6_spmd.clone.sunk | while | flops 1613757184 | bytes 8428165 | solution.py:45
  139.3 3.5 %fusion.19 = (f32[512]{0:T(512)S(1)}, f32[512,768]{1,0:T(8,128)S(1)}) fusion(bf16[2048,768]{1,0:T(8,128)(2,1)S(1)} %get-tuple-element.519, bf16[4,512,2048]{2,1,0:T(8,128)(2,1)} %get-tuple-element.518, s32[]{:T(128)} %get-tuple-element.502), kind=kOutput, calls=%fused_computation.41.clone.1 | convolution fusion | flops 1611005440 | bytes 6818304 | tf_op jit(solution)/shard_map/while/body/eval_jaxpr/dot_general | solution.py:32
  142.9 0.7 multiply_reduce_fusion.2
  143.6 0.1 dynamic_update_slice.24
  143.7 0.1 dynamic_update_slice.22
  143.8 3.5 %fusion.19 = (f32[512]{0:T(512)S(1)}, f32[512,768]{1,0:T(8,128)S(1)}) fusion(bf16[2048,768]{1,0:T(8,128)(2,1)S(1)} %get-tuple-element.519, bf16[4,512,2048]{2,1,0:T(8,128)(2,1)} %get-tuple-element.518, s32[]{:T(128)} %get-tuple-element.502), kind=kOutput, calls=%fused_computation.41.clone.1 | convolution fusion | flops 1611005440 | bytes 6818304 | tf_op jit(solution)/shard_map/while/body/eval_jaxpr/dot_general | solution.py:32
  147.4 0.7 multiply_reduce_fusion.2
  148.3 3.5 %fusion.19 = (f32[512]{0:T(512)S(1)}, f32[512,768]{1,0:T(8,128)S(1)}) fusion(bf16[2048,768]{1,0:T(8,128)(2,1)S(1)} %get-tuple-element.519, bf16[4,512,2048]{2,1,0:T(8,128)(2,1)} %get-tuple-element.518, s32[]{:T(128)} %get-tuple-element.502), kind=kOutput, calls=%fused_computation.41.clone.1 | convolution fusion | flops 1611005440 | bytes 6818304 | tf_op jit(solution)/shard_map/while/body/eval_jaxpr/dot_general | solution.py:32
  151.9 0.7 multiply_reduce_fusion.2
  152.8 3.5 %fusion.19 = (f32[512]{0:T(512)S(1)}, f32[512,768]{1,0:T(8,128)S(1)}) fusion(bf16[2048,768]{1,0:T(8,128)(2,1)S(1)} %get-tuple-element.519, bf16[4,512,2048]{2,1,0:T(8,128)(2,1)} %get-tuple-element.518, s32[]{:T(128)} %get-tuple-element.502), kind=kOutput, calls=%fused_computation.41.clone.1 | convolution fusion | flops 1611005440 | bytes 6818304 | tf_op jit(solution)/shard_map/while/body/eval_jaxpr/dot_general | solution.py:32
  156.3 0.7 multiply_reduce_fusion.2
  157.3 0.6 all_to_all.30
  157.9 3.3 %all-to-all-start = ((f32[8,1,256]{2,1,0:T(1,128)}), f32[8,1,256]{2,1,0:T(1,128)S(1)}, u32[]{:S(2)}, u32[]{:S(2)}) async-start(f32[8,1,256]{2,1,0:T(1,128)} %all_to_all.30), calls=%async_computation | async-start | bytes 16384 | tf_op jit(solution)/shard_map/all_to_all | solution.py:70
  161.2 0.6 all_to_all.32
  161.8 5.8 %all-to-all-done = f32[8,1,256]{2,1,0:T(1,128)S(1)} async-done(((f32[8,1,256]{2,1,0:T(1,128)}), f32[8,1,256]{2,1,0:T(1,128)S(1)}, u32[]{:S(2)}, u32[]{:S(2)}) %all-to-all-start) | async-done | bytes 8224 | tf_op jit(solution)/shard_map/all_to_all | solution.py:70
  167.7 3.3 %all-to-all-start.1 = ((f32[8,1,256]{2,1,0:T(1,128)}), f32[8,1,256]{2,1,0:T(1,128)S(1)}, u32[]{:S(2)}, u32[]{:S(2)}) async-start(f32[8,1,256]{2,1,0:T(1,128)} %all_to_all.32), calls=%async_computation.1 | async-start | bytes 16384 | tf_op jit(solution)/shard_map/all_to_all | solution.py:71
  171.0 0.6 all_to_all.36
  171.6 5.8 %all-to-all-done.1 = f32[8,1,256]{2,1,0:T(1,128)S(1)} async-done(((f32[8,1,256]{2,1,0:T(1,128)}), f32[8,1,256]{2,1,0:T(1,128)S(1)}, u32[]{:S(2)}, u32[]{:S(2)}) %all-to-all-start.1) | async-done | bytes 8224 | tf_op jit(solution)/shard_map/all_to_all | solution.py:71
  177.5 3.3 %all-to-all-start.2 = ((f32[8,1,256]{2,1,0:T(1,128)}), f32[8,1,256]{2,1,0:T(1,128)S(1)}, u32[]{:S(2)}, u32[]{:S(2)}) async-start(f32[8,1,256]{2,1,0:T(1,128)} %all_to_all.36), calls=%async_computation.2 | async-start | bytes 16384 | tf_op jit(solution)/shard_map/all_to_all | solution.py:72
  181.4 0.6 all_to_all.39
  182.1 5.2 %all-to-all-done.2 = f32[8,1,256]{2,1,0:T(1,128)S(1)} async-done(((f32[8,1,256]{2,1,0:T(1,128)}), f32[8,1,256]{2,1,0:T(1,128)S(1)}, u32[]{:S(2)}, u32[]{:S(2)}) %all-to-all-start.2) | async-done | bytes 8224 | tf_op jit(solution)/shard_map/all_to_all | solution.py:72
  187.3 3.3 %all-to-all-start.3 = ((f32[8,1,256]{2,1,0:T(1,128)}), f32[8,1,256]{2,1,0:T(1,128)S(1)}, u32[]{:S(2)}, u32[]{:S(2)}) async-start(f32[8,1,256]{2,1,0:T(1,128)} %all_to_all.39), calls=%async_computation.3 | async-start | bytes 16384 | tf_op jit(solution)/shard_map/all_to_all | solution.py:73
  190.6 5.1 %all-gather.6 = f32[4,1,256]{2,1,0:T(1,128)S(1)} all-gather(f32[1,1,256]{2,1,0:T(1,128)S(1)} %bitcast.100), channel_id=3, replica_groups=mesh['req'=8,'tp'=4] {'tp'}, dimensions={0}, use_global_device_ids=true | all-gather | bytes 5120 | tf_op jit(solution)/shard_map/all_gather | solution.py:10
  195.7 5.1 %all-gather.7 = f32[4,1,256]{2,1,0:T(1,128)S(1)} all-gather(f32[1,1,256]{2,1,0:T(1,128)S(1)} %bitcast.99), channel_id=4, replica_groups=mesh['req'=8,'tp'=4] {'tp'}, dimensions={0}, use_global_device_ids=true | all-gather | bytes 5120 | tf_op jit(solution)/shard_map/all_gather | solution.py:10
  200.7 5.1 %all-gather.5 = f32[4,1,256]{2,1,0:T(1,128)S(1)} all-gather(f32[1,1,256]{2,1,0:T(1,128)S(1)} %bitcast.98), channel_id=2, replica_groups=mesh['req'=8,'tp'=4] {'tp'}, dimensions={0}, use_global_device_ids=true | all-gather | bytes 5120 | tf_op jit(solution)/shard_map/all_gather | solution.py:10
  205.8 5.1 %all-gather.8 = f32[4,1,256]{2,1,0:T(1,128)S(1)} all-gather(f32[1,1,256]{2,1,0:T(1,128)S(1)} %bitcast.101), channel_id=5, replica_groups=mesh['req'=8,'tp'=4] {'tp'}, dimensions={0}, use_global_device_ids=true | all-gather | bytes 5120 | tf_op jit(solution)/shard_map/all_gather | solution.py:10
  210.9 0.3 while.38
  211.2 1.2 fusion.13
  (65 shorter events, 1.2 us)
Async XLA Ops:
  7.2 4.4 %copy-start = (s32[256]{0:T(256)S(1)}, s32[256]{0:T(256)}, u32[]{:S(2)}) copy-start(s32[256]{0:T(256)} %param.12) | copy-start | bytes 3076
  7.2 132.2 %copy-start.1 = (bf16[2048,768]{1,0:T(8,128)(2,1)S(1)}, bf16[2048,768]{1,0:T(8,128)(2,1)}, u32[]{:S(2)}) copy-start(bf16[2048,768]{1,0:T(8,128)(2,1)} %param.11) | copy-start | bytes 9437188
  7.2 132.2 %all-gather.11.cloned.1.call-start = ((), (), s32[]{:S(2)}) async-start(), calls=%async_computation.4 | async-start | bytes 9437184 | tf_op jit(solution)/shard_map/all_gather | solution.py:64
  157.9 9.8 %all-to-all-start = ((f32[8,1,256]{2,1,0:T(1,128)}), f32[8,1,256]{2,1,0:T(1,128)S(1)}, u32[]{:S(2)}, u32[]{:S(2)}) async-start(f32[8,1,256]{2,1,0:T(1,128)} %all_to_all.30), calls=%async_computation | async-start | bytes 16384 | tf_op jit(solution)/shard_map/all_to_all | solution.py:70
  167.7 9.8 %all-to-all-start.1 = ((f32[8,1,256]{2,1,0:T(1,128)}), f32[8,1,256]{2,1,0:T(1,128)S(1)}, u32[]{:S(2)}, u32[]{:S(2)}) async-start(f32[8,1,256]{2,1,0:T(1,128)} %all_to_all.32), calls=%async_computation.1 | async-start | bytes 16384 | tf_op jit(solution)/shard_map/all_to_all | solution.py:71
  177.5 9.8 %all-to-all-start.2 = ((f32[8,1,256]{2,1,0:T(1,128)}), f32[8,1,256]{2,1,0:T(1,128)S(1)}, u32[]{:S(2)}, u32[]{:S(2)}) async-start(f32[8,1,256]{2,1,0:T(1,128)} %all_to_all.36), calls=%async_computation.2 | async-start | bytes 16384 | tf_op jit(solution)/shard_map/all_to_all | solution.py:72
  187.3 18.5 %all-to-all-start.3 = ((f32[8,1,256]{2,1,0:T(1,128)}), f32[8,1,256]{2,1,0:T(1,128)S(1)}, u32[]{:S(2)}, u32[]{:S(2)}) async-start(f32[8,1,256]{2,1,0:T(1,128)} %all_to_all.39), calls=%async_computation.3 | async-start | bytes 16384 | tf_op jit(solution)/shard_map/all_to_all | solution.py:73
Sparse Core Ops, SparseCore 0:
  11.7 127.6 all-gather.10
where the time goes:
time: 222 us; the launch traced here: 221 us
  waiting for transfers between devices  122 us (55%)
  blocking collectives  42.7 us (19%)
  between operations  16.6 us (7%)
  matrix products  14 us (6%)
  starting transfers between devices  13.3 us (6%)
  other arithmetic  8.65 us (4%)
  local copies, waits for them, and re-layouts  3.36 us (2%)
    all_gather x1, waiting for transfers between devices, per_device(): block = lax.all_gather(normed, 'req', axis=0, tiled=True)  105 us
    all_gather x1, blocking collectives, per_device(): target = lax.all_gather(target_ids, 'req', axis=0, tiled=True)  22.5 us
    all_gather x4, blocking collectives, combined_all(): everything = jax.tree.map(lambda part: lax.all_gather(part, axis), value)  20.2 us
    dot_general x4, matrix products, block_stats(): logits = jnp.dot(block, matrix, preferred_element_type=jnp.float32)  14 us
    all_to_all x1, waiting for transfers between devices, per_device(): lax.all_to_all(shaped[0], 'req', split_axis=0, concat_axis=0, tiled=True)  5.85 us
    all_to_all x1, waiting for transfers between devices, per_device(): lax.all_to_all(shaped[1], 'req', split_axis=0, concat_axis=0, tiled=True)  5.84 us
    all_to_all x1, waiting for transfers between devices, per_device(): lax.all_to_all(shaped[2], 'req', split_axis=0, concat_axis=0, tiled=True)  5.17 us
  transfers between devices with their start and end apart: 5, of which 4 were waited for; matrix products, arithmetic and copies ran while one was open for 0% of the time, Pallas kernels for 0%

commit v1 on v0

v1 whole, which is shorter than its diff:
```python
import functools

import jax
import jax.numpy as jnp
from jax import lax
from jax.experimental import pallas as pl
from jax.experimental.pallas import tpu as pltpu
from jax.sharding import PartitionSpec as P

AXES = ("req", "tp")
LANES = 128
STATS = 8
VMEM_BYTES = 48 * 1024 * 1024


def ring_place(req, n_req):
    half = n_req // 2
    return jnp.where(req % 2 == 0, req // 2, n_req - 1 - req // 2) if half else req


def ring_req(place, n_req):
    half = n_req // 2
    return jnp.where(place < half, 2 * place, 2 * (n_req - 1 - place) + 1)


def ring_req_py(place, n_req):
    place %= n_req
    return 2 * place if place < n_req // 2 else 2 * (n_req - 1 - place) + 1


def ring_pairs(n_req, n_tp, turn):
    pairs = []
    for place in range(n_req):
        here, there = ring_req_py(place, n_req), ring_req_py(place + turn, n_req)
        pairs += [(here * n_tp + t, there * n_tp + t) for t in range(n_tp)]
    return pairs


def tp_pairs(n_req, n_tp, bit):
    return [(r * n_tp + t, r * n_tp + (t ^ bit)) for r in range(n_req) for t in range(n_tp)]


def block_starts(rows, b_rows):
    g = rows // 2 - b_rows
    return (0, g, rows // 2, rows - g), (g, b_rows, b_rows, g)


def norm_kernel(b_rows, x_ref, gain_ref, xn_ref, acw_ref, bcw_ref, accw_ref, bccw_ref):
    rows = x_ref.shape[0]
    plane = lax.axis_index("tp") // 2
    feats = x_ref[...].astype(jnp.float32)
    scale = lax.rsqrt(jnp.mean(feats * feats, axis=-1, keepdims=True) + 1e-06)
    xn_ref[...] = (feats * scale * gain_ref[...]).astype(jnp.bfloat16)
    starts, sizes = block_starts(rows, b_rows)
    for refs, flip in (((acw_ref, bcw_ref), 0), ((accw_ref, bccw_ref), 1)):
        down = plane != flip
        dests = ((refs[0], 0), (refs[0], sizes[0]), (refs[1], 0))
        for j, (ref, at) in enumerate(dests):
            start = pl.multiple_of(jnp.where(down, starts[3 - j], starts[j]), 16)
            ref[pl.ds(at, sizes[j]), :] = xn_ref[pl.ds(start, sizes[j]), :]


def norm_rows(hidden_half, norm_gain, b_rows):
    rows, d = hidden_half.shape
    a = rows // 2
    shapes = [(rows, d), (a, d), (b_rows, d), (a, d), (b_rows, d)]
    return pl.pallas_call(
        functools.partial(norm_kernel, b_rows),
        out_shape=[jax.ShapeDtypeStruct(s, jnp.bfloat16) for s in shapes],
        compiler_params=pltpu.CompilerParams(vmem_limit_bytes=VMEM_BYTES),
        name="norm",
    )(hidden_half, norm_gain.reshape(1, d))


def piece_segments(part, rows, b_rows):
    return {"all": (0, 1, 2, 3), "a": (0, 1), "b": (2,), "y": (3,)}[part]


def stats_kernel(metas, n_req, b_rows, rows, *refs):
    n = len(metas)
    piece_refs, (w0_ref, w1_ref, tid_ref, out_ref, x_s, l_s, t_s, tc_s) = refs[:n], refs[n:]
    req, tp = lax.axis_index("req"), lax.axis_index("tp")
    n_tp = lax.axis_size("tp")
    plane = tp // 2
    place = ring_place(req, n_req)
    vdev = w0_ref.shape[1]
    total = x_s.shape[0]

    lane = lax.broadcasted_iota(jnp.int32, (1, LANES), 1)
    t_s[:, :] = jnp.zeros_like(t_s)
    t_s[:, : tid_ref.shape[0]] = tid_ref[...].T
    starts, sizes = block_starts(rows, b_rows)
    at = 0
    for (turn, hops, part), ref in zip(metas, piece_refs):
        x_s[pl.ds(at, ref.shape[0]), :] = ref[...]
        source = ring_req((place - turn * hops + n_req) % n_req, n_req)
        down = plane != (0 if turn >= 0 else 1)
        for j in piece_segments(part, rows, b_rows):
            start = starts[j] if part == "all" else jnp.where(down, starts[3 - j], starts[j])
            seg = t_s[pl.ds(pl.multiple_of(start, 16), sizes[j]), :]
            tc_s[pl.ds(at, sizes[j]), :] = jnp.sum(
                jnp.where(lane == source, seg, 0), axis=1, keepdims=True
            )
            at += sizes[j]

    x = x_s[...]
    l_s[:, :vdev] = jnp.dot(x, w0_ref[...], preferred_element_type=jnp.float32)
    l_s[:, vdev:] = jnp.dot(x, w1_ref[...], preferred_element_type=jnp.float32)

    column = lax.broadcasted_iota(jnp.int32, (1, vdev), 1)
    ids0 = column + (req * n_tp + tp) * vdev
    ids1 = column + (req * n_tp + (tp ^ 1)) * vdev
    step = 16

    def body(i, _):
        here = pl.ds(pl.multiple_of(i * step, step), step)
        logits = l_s[here, :]
        target = tc_s[here, :]
        top = jnp.max(logits, axis=1, keepdims=True)
        shifted = jnp.exp(logits - top)
        weight_sum = jnp.sum(shifted, axis=1, keepdims=True)
        weighted = jnp.sum(shifted * logits, axis=1, keepdims=True)
        hit0 = jnp.where(ids0 == target, logits[:, :vdev], 0.0)
        hit1 = jnp.where(ids1 == target, logits[:, vdev:], 0.0)
        picked = jnp.sum(hit0 + hit1, axis=1, keepdims=True)
        out_ref[here, :] = jnp.where(
            lane == 0, top, jnp.where(lane == 1, weight_sum, jnp.where(lane == 2, weighted, picked))
        )
        return 0

    lax.fori_loop(0, total // step, body, 0, unroll=2)


def stats_of(pieces, metas, w0, w1, tids, n_req, b_rows, rows):
    d, vdev = w0.shape
    total = sum(p.shape[0] for p in pieces)
    return pl.pallas_call(
        functools.partial(stats_kernel, metas, n_req, b_rows, rows),
        out_shape=jax.ShapeDtypeStruct((total, LANES), jnp.float32),
        scratch_shapes=[
            pltpu.VMEM((total, d), jnp.bfloat16),
            pltpu.VMEM((total, 2 * vdev), jnp.float32),
            pltpu.VMEM((rows, LANES), jnp.int32),
            pltpu.VMEM((total, 1), jnp.int32),
        ],
        compiler_params=pltpu.CompilerParams(vmem_limit_bytes=VMEM_BYTES),
        cost_estimate=pl.CostEstimate(
            flops=4 * total * d * vdev, bytes_accessed=4 * d * vdev, transcendentals=2 * total * vdev
        ),
        name="stats",
    )(*pieces, w0, w1, tids)


def pack_kernel(metas, n_req, n_tp, b_rows, rows, *refs):
    *stat_refs, out_ref = refs
    req, tp = lax.axis_index("req"), lax.axis_index("tp")
    plane = tp // 2
    place = ring_place(req, n_req)
    starts, sizes = block_starts(rows, b_rows)
    shards = {}
    for meta, ref in zip(metas, stat_refs):
        at = 0
        for turn, hops, part in meta:
            for j in piece_segments(part, rows, b_rows):
                shards.setdefault((turn, hops) if 2 * hops != n_req else (0, hops), []).append(
                    (turn, j, ref[pl.ds(at, sizes[j]), :])
                )
                at += sizes[j]
    for (turn, hops), found in shards.items():
        if turn == 0 and hops:
            up = {j: v for t, j, v in found if t > 0} | {3 - j: v for t, j, v in found if t < 0}
        else:
            up = {j: v for _, j, v in found}
        ordered = jnp.concatenate([up[j] for j in range(4)], axis=0)
        if hops:
            flipped = jnp.concatenate([up[3 - j] for j in range(4)], axis=0)
            down = plane != (0 if turn >= 0 else 1)
            ordered = jnp.where(down, flipped, ordered)
        source = ring_req((place - turn * hops + n_req) % n_req, n_req)
        if turn == 0 and hops:
            source = ring_req((place + hops) % n_req, n_req)
        packed = ordered.T[:STATS, :]
        for t in range(n_tp):
            out_ref[source * n_tp + t] = packed


def pack(stats, metas, n_req, n_tp, b_rows, rows):
    return pl.pallas_call(
        functools.partial(pack_kernel, metas, n_req, n_tp, b_rows, rows),
        out_shape=jax.ShapeDtypeStruct((n_req * n_tp, STATS, rows), jnp.float32),
        compiler_params=pltpu.CompilerParams(vmem_limit_bytes=VMEM_BYTES),
        name="pack",
    )(*stats)


def final_kernel(n_parts, r_ref, len_ref, lp_ref, ent_ref, mean_ref, top_ref):
    rows = r_ref.shape[2]
    length = len_ref[0]
    total = jnp.float32(0.0)
    best = jnp.float32(-1e30)
    for half in range(2):
        mine = [r_ref[2 * k + half] for k in range(n_parts // 2)]
        top = functools.reduce(jnp.maximum, [m[0:1] for m in mine])
        scaled = functools.reduce(jnp.add, [m * jnp.exp(m[0:1] - top) for m in mine])
        picked = functools.reduce(jnp.add, [m[3:4] for m in mine])
        weight_sum, weighted = scaled[1:2], scaled[2:3]
        log_norm = top + jnp.log(weight_sum)
        slot = lax.broadcasted_iota(jnp.int32, (1, rows), 1) + half * rows
        live = slot < length
        logprob = jnp.where(live, picked - log_norm, 0.0)
        lp_ref[half : half + 1, :] = logprob
        ent_ref[half : half + 1, :] = jnp.where(live, log_norm - weighted / weight_sum, 0.0)
        total += jnp.sum(logprob)
        best = jnp.maximum(best, jnp.max(jnp.where(live, top, -1e30)))
    mean_ref[...] = jnp.full((1, 1), total, jnp.float32) / length.astype(jnp.float32)
    top_ref[...] = jnp.full((1, 1), best, jnp.float32)


def finish(received, lengths):
    n_parts, _, rows = received.shape
    outs = pl.pallas_call(
        functools.partial(final_kernel, n_parts),
        out_shape=[jax.ShapeDtypeStruct((2, rows), jnp.float32)] * 2
        + [jax.ShapeDtypeStruct((1, 1), jnp.float32)] * 2,
        in_specs=[
            pl.BlockSpec(memory_space=pltpu.VMEM),
            pl.BlockSpec(memory_space=pltpu.SMEM),
        ],
        name="finish",
    )(received, lengths)
    return tuple(o.reshape(-1) for o in outs)


def per_device(n_req, n_tp, hidden_states, norm_gain, head, target_ids, lengths):
    rows = hidden_states.shape[0] // 2
    b_rows = rows // 4
    core = lax.axis_index("tp") % 2
    cw, ccw = ring_pairs(n_req, n_tp, 1), ring_pairs(n_req, n_tp, -1)
    other_core, other_y = tp_pairs(n_req, n_tp, 1), tp_pairs(n_req, n_tp, 2)

    def send(value, pairs):
        return lax.ppermute(value, AXES, pairs)

    other_head = send(head, other_core)
    hidden_half = lax.dynamic_slice_in_dim(hidden_states, core * rows, rows, 0)
    xn, a_cw, b_cw, a_ccw, b_ccw = norm_rows(hidden_half, norm_gain, b_rows)
    my_targets = lax.dynamic_slice_in_dim(target_ids, core * rows, rows, 0)
    tids = lax.all_to_all(
        jnp.broadcast_to(my_targets[None, :], (n_req, rows)), "req", 0, 0, tiled=True
    )
    metas, stats = [], []

    def work(pieces, meta):
        metas.append(tuple(meta))
        stats.append(
            stats_of(pieces, tuple(meta), head, other_head, tids, n_req, b_rows, rows)
        )

    pieces, meta = [xn], [(0, 0, "all")]
    g = rows // 2 - b_rows
    for hops in range(1, n_req // 2 + 1):
        last = 2 * hops == n_req
        a_cw, a_ccw = send(a_cw, cw), send(a_ccw, ccw)
        if not last:
            b_cw, b_ccw = send(b_cw, cw), send(b_ccw, ccw)
        work(pieces, meta)
        if last:
            pieces, meta = [a_cw, a_ccw], [(1, hops, "a"), (-1, hops, "a")]
        else:
            pieces = [a_cw, b_cw, a_ccw, b_ccw]
            meta = [(1, hops, "a"), (1, hops, "b"), (-1, hops, "a"), (-1, hops, "b")]
        if hops > 1:
            pieces += [y_piece[:g], y_piece[g:]]
            meta += [(1, hops - 1, "y"), (-1, hops - 1, "y")]
        if not last:
            y_piece = send(jnp.concatenate([a_cw[:g], a_ccw[:g]], axis=0), other_y)
    work(pieces, meta)
    packed = pack(stats, metas, n_req, n_tp, b_rows, rows)
    received = lax.all_to_all(packed, AXES, 0, 0, tiled=True)
    return finish(received, lengths)


def solution(mesh):
    n_req, n_tp = mesh.shape["req"], mesh.shape["tp"]
    in_specs = (P("req", None), P(), P(None, ("req", "tp")), P("req"), P("req"))
    out_specs = (P("req"), P("req"), P("req"), P("req"))
    return jax.shard_map(
        functools.partial(per_device, n_req, n_tp),
        mesh=mesh,
        in_specs=in_specs,
        out_specs=out_specs,
        check_vma=False,
    )
```

time: 222 us -> 93.6 us (0.42)
  waiting for transfers between devices: 122 us -> 25.9 us
  blocking collectives: 42.7 us -> 0 us
  Pallas kernels: 0 us -> 27.9 us
  starting transfers between devices: 13.3 us -> 30.5 us
  between operations: 16.6 us -> 1.57 us
  matrix products: 14 us -> 0 us
  other arithmetic: 8.65 us -> 0.06 us
  local copies, waits for them, and re-layouts: 3.36 us -> 7.18 us
    all_gather x1 -> x0, waiting for transfers between devices: 105 us -> none  [per_device(): block = lax.all_gather(normed, 'req', axis=0, tiled=True)]
    all_gather x5 -> x0, blocking collectives: 42.7 us -> none  [the longest x1 22.5 us: per_device(): target = lax.all_gather(target_ids, 'req', axis=0, tiled=True)]
    pallas_call x0 -> x8, Pallas kernels: none -> 27.9 us  [the longest x5 25.2 us: stats_of(): pl.pallas_call(functools.partial(stats_kernel, metas, n_req, b_rows, rows...]
    ppermute x0 -> x18, starting transfers between devices: none -> 22 us  [send(): return lax.ppermute(value, AXES, pairs)]
    ppermute x0 -> x18, waiting for transfers between devices: none -> 18.3 us  [send(): return lax.ppermute(value, AXES, pairs)]
    dot_general x4 -> x0, matrix products: 14 us -> none  [block_stats(): logits = jnp.dot(block, matrix, preferred_element_type=jnp.float32)]
    all_to_all x4 -> x2, waiting for transfers between devices: 16.9 us -> 7.58 us  [the longest x1 7.58 us: per_device(): received = lax.all_to_all(packed, AXES, 0, 0, tiled=True)]
    reduce_sum x8 -> x0, other arithmetic: 5.77 us -> none  [the longest x4 2.88 us: block_stats(): weighted = jnp.sum(shifted * logits, axis=-1)]
  transfers between devices with their start and end apart: 5 -> 20, of which waited for: 4 -> 7; matrix products, arithmetic and copies ran while one was open for 0% -> 3% of each run, Pallas kernels for 0% -> 22%
where the time goes in v1:
time: 93.6 us; the launch traced here: 93.2 us
  starting transfers between devices  30.5 us (33%)
  Pallas kernels  27.9 us (30%)
  waiting for transfers between devices  25.9 us (28%)
  local copies, waits for them, and re-layouts  7.18 us (8%)
  between operations  1.57 us (2%)
    pallas_call x5, Pallas kernels, stats_of(): pl.pallas_call(functools.partial(stats_kernel, metas, n_req, b_rows, rows...  25.2 us
    ppermute x18, starting transfers between devices, send(): return lax.ppermute(value, AXES, pairs)  22 us
    ppermute x18, waiting for transfers between devices, send(): return lax.ppermute(value, AXES, pairs)  18.3 us
    all_to_all x1, waiting for transfers between devices, per_device(): received = lax.all_to_all(packed, AXES, 0, 0, tiled=True)  7.58 us
    all_to_all x1, starting transfers between devices, per_device(): lax.all_to_all(jnp.broadcast_to(my_targets[None, :], (n_req, rows)), 'req...  4.88 us
    unnamed x18, local copies, waits for them, and re-layouts  4.72 us
    all_to_all x1, starting transfers between devices, per_device(): received = lax.all_to_all(packed, AXES, 0, 0, tiled=True)  3.64 us
  transfers between devices with their start and end apart: 20, of which 7 were waited for; matrix products, arithmetic and copies ran while one was open for 3% of the time, Pallas kernels for 22%

profile of v1, /device:TPU:0, one launch (start us, length us, event | category | flops | bytes accessed | tf_op | source)
XLA Modules:
  0.0 93.2 jit_solution(12707938357701684500)
XLA Ops:
  1.2 0.7 copy-done
  1.9 0.7 copy-done.7
  2.9 0.8 copy-done.3
  3.7 2.9 %collective-permute-start.3 = (bf16[64,2048]{1,0:T(8,128)(2,1)S(1)}, bf16[64,2048]{1,0:T(8,128)(2,1)S(1)}, u32[]{:S(2)}, u32[]{:S(2)}) collective-permute-start(bf16[64,2048]{1,0:T(8,128)(2,1)S(1)} %get-tuple-element.16), channel_id=1, source_target_pairs={{0,4},{1,5},{2,6},{3,7},{8,0},{9,1},{10,2},{11,3},{16,8},{17,9},{1... | collective-permute-start | bytes 786440 | tf_op jit(solution)/shard_map/ppermute | solution.py:242
  6.7 2.0 %collective-permute-start.2 = (bf16[32,2048]{1,0:T(8,128)(2,1)S(1)}, bf16[32,2048]{1,0:T(8,128)(2,1)S(1)}, u32[]{:S(2)}, u32[]{:S(2)}) collective-permute-start(bf16[32,2048]{1,0:T(8,128)(2,1)S(1)} %get-tuple-element.15), channel_id=1, source_target_pairs={{0,8},{1,9},{2,10},{3,11},{8,16},{9,17},{10,18},{11,19},{16,24},{1... | collective-permute-start | bytes 393224 | tf_op jit(solution)/shard_map/ppermute | solution.py:242
  8.7 4.3 %collective-permute-done.3.refs_2_ = bf16[64,2048]{1,0:T(8,128)(2,1)S(1)} collective-permute-done((bf16[64,2048]{1,0:T(8,128)(2,1)S(1)}, bf16[64,2048]{1,0:T(8,128)(2,1)S(1)}, u32[]{:S(2)}, u32[]{:S(2)}) %collective-permute-start.3) | collective-permute-done | bytes 262176 | tf_op jit(solution)/shard_map/ppermute | solution.py:242
  13.0 1.7 %collective-permute-start.7 = (bf16[64,2048]{1,0:T(8,128)(2,1)S(1)}, bf16[64,2048]{1,0:T(8,128)(2,1)S(1)}, u32[]{:S(2)}, u32[]{:S(2)}) collective-permute-start(bf16[64,2048]{1,0:T(8,128)(2,1)S(1)} %collective-permute-done.3.refs_2_), channel_id=1, source_target_pairs={{0,4},{1,5},{2,6},{3,7},{8,0},{9,1},{10,2},{11,3},{16,8},{17,9},{1... | collective-permute-start | bytes 786440 | tf_op jit(solution)/shard_map/ppermute | solution.py:242
  14.7 1.1 %collective-permute-done.1.refs_0_ = bf16[64,2048]{1,0:T(8,128)(2,1)S(1)} collective-permute-done((bf16[64,2048]{1,0:T(8,128)(2,1)S(1)}, bf16[64,2048]{1,0:T(8,128)(2,1)S(1)}, u32[]{:S(2)}, u32[]{:S(2)}) %collective-permute-start.1) | collective-permute-done | bytes 262176 | tf_op jit(solution)/shard_map/ppermute | solution.py:242
  15.9 1.9 %collective-permute-start.4 = (bf16[32,2048]{1,0:T(8,128)(2,1)S(1)}, bf16[32,2048]{1,0:T(8,128)(2,1)S(1)}, u32[]{:S(2)}, u32[]{:S(2)}) collective-permute-start(bf16[32,2048]{1,0:T(8,128)(2,1)S(1)} %get-tuple-element.17), channel_id=1, source_target_pairs={{0,4},{1,5},{2,6},{3,7},{8,0},{9,1},{10,2},{11,3},{16,8},{17,9},{1... | collective-permute-start | bytes 393224 | tf_op jit(solution)/shard_map/ppermute | solution.py:242
  18.4 1.5 %collective-permute-start.9 = (bf16[64,2048]{1,0:T(8,128)(2,1)S(1)}, bf16[64,2048]{1,0:T(8,128)(2,1)}, u32[]{:S(2)}, u32[]{:S(2)}) collective-permute-start(bf16[64,2048]{1,0:T(8,128)(2,1)S(1)} %pad_maximum_fusion), channel_id=1, source_target_pairs={{0,2},{1,3},{2,0},{3,1},{4,6},{5,7},{6,4},{7,5},{8,10},{9,11},{10,... | collective-permute-start | bytes 786440 | tf_op jit(solution)/shard_map/ppermute | solution.py:242
  19.9 0.8 dynamic_slice.7
  21.3 4.9 %all-to-all-start = ((s32[8,1,128]{2,1,0:T(1,128)}), s32[8,1,128]{2,1,0:T(1,128)S(1)}, u32[]{:S(2)}, u32[]{:S(2)}) async-start(s32[8,1,128]{2,1,0:T(1,128)} %broadcast_in_dim.2), calls=%async_computation | async-start | bytes 8192 | tf_op jit(solution)/shard_map/all_to_all | solution.py:248
  26.1 2.1 %collective-permute-start.6 = (bf16[32,2048]{1,0:T(8,128)(2,1)S(1)}, bf16[32,2048]{1,0:T(8,128)(2,1)}, u32[]{:S(2)}, u32[]{:S(2)}) collective-permute-start(bf16[32,2048]{1,0:T(8,128)(2,1)S(1)} %collective-permute-done.2.refs_1_), channel_id=1, source_target_pairs={{0,8},{1,9},{2,10},{3,11},{8,16},{9,17},{10,18},{11,19},{16,24},{1... | collective-permute-start | bytes 393224 | tf_op jit(solution)/shard_map/ppermute | solution.py:242
  28.9 3.8 %collective-permute-done.6.refs_1_ = bf16[32,2048]{1,0:T(8,128)(2,1)} collective-permute-done((bf16[32,2048]{1,0:T(8,128)(2,1)S(1)}, bf16[32,2048]{1,0:T(8,128)(2,1)}, u32[]{:S(2)}, u32[]{:S(2)}) %collective-permute-start.6) | collective-permute-done | bytes 131104 | tf_op jit(solution)/shard_map/ppermute | solution.py:242
  32.7 1.9 %collective-permute-start.10 = (bf16[64,2048]{1,0:T(8,128)(2,1)S(1)}, bf16[64,2048]{1,0:T(8,128)(2,1)S(1)}, u32[]{:S(2)}, u32[]{:S(2)}) collective-permute-start(bf16[64,2048]{1,0:T(8,128)(2,1)S(1)} %collective-permute-done.5.refs_0_), channel_id=1, source_target_pairs={{0,8},{1,9},{2,10},{3,11},{8,16},{9,17},{10,18},{11,19},{16,24},{1... | collective-permute-start | bytes 786440 | tf_op jit(solution)/shard_map/ppermute | solution.py:242
  34.7 1.0 %fusion.2 = (bf16[32,2048]{1,0:T(8,128)(2,1)S(1)}, bf16[32,2048]{1,0:T(8,128)(2,1)S(1)}) fusion(bf16[64,2048]{1,0:T(8,128)(2,1)} %collective-permute-done.9), kind=kLoop, calls=%fused_computation.6 | loop fusion | bytes 524288 | tf_op jit(solution)/shard_map/slice | solution.py:273
  35.7 2.0 %collective-permute-start.11 = (bf16[32,2048]{1,0:T(8,128)(2,1)}, bf16[32,2048]{1,0:T(8,128)(2,1)}, u32[]{:S(2)}, u32[]{:S(2)}) collective-permute-start(bf16[32,2048]{1,0:T(8,128)(2,1)} %collective-permute-done.6.refs_1_), channel_id=1, source_target_pairs={{0,8},{1,9},{2,10},{3,11},{8,16},{9,17},{10,18},{11,19},{16,24},{1... | collective-permute-start | bytes 393224 | tf_op jit(solution)/shard_map/ppermute | solution.py:242
  37.7 4.5 %collective-permute-done.12.refs_2_ = bf16[64,2048]{1,0:T(8,128)(2,1)S(1)} collective-permute-done((bf16[64,2048]{1,0:T(8,128)(2,1)S(1)}, bf16[64,2048]{1,0:T(8,128)(2,1)S(1)}, u32[]{:S(2)}, u32[]{:S(2)}) %collective-permute-start.12) | collective-permute-done | bytes 262176 | tf_op jit(solution)/shard_map/ppermute | solution.py:242
  43.1 1.7 %collective-permute-start.15 = (bf16[64,2048]{1,0:T(8,128)(2,1)S(1)}, bf16[64,2048]{1,0:T(8,128)(2,1)}, u32[]{:S(2)}, u32[]{:S(2)}) collective-permute-start(bf16[64,2048]{1,0:T(8,128)(2,1)S(1)} %collective-permute-done.10.refs_0_), channel_id=1, source_target_pairs={{0,8},{1,9},{2,10},{3,11},{8,16},{9,17},{10,18},{11,19},{16,24},{1... | collective-permute-start | bytes 786440 | tf_op jit(solution)/shard_map/ppermute | solution.py:242
  44.8 4.2 %collective-permute-done.17 = bf16[64,2048]{1,0:T(8,128)(2,1)S(1)} collective-permute-done((bf16[64,2048]{1,0:T(8,128)(2,1)S(1)}, bf16[64,2048]{1,0:T(8,128)(2,1)S(1)}, u32[]{:S(2)}, u32[]{:S(2)}) %collective-permute-start.17) | collective-permute-done | bytes 262176 | tf_op jit(solution)/shard_map/ppermute | solution.py:242
  49.0 1.9 %collective-permute-start.16 = (bf16[64,2048]{1,0:T(8,128)(2,1)S(1)}, bf16[64,2048]{1,0:T(8,128)(2,1)}, u32[]{:S(2)}, u32[]{:S(2)}) collective-permute-start(bf16[64,2048]{1,0:T(8,128)(2,1)S(1)} %collective-permute-done.12.refs_2_), channel_id=1, source_target_pairs={{0,4},{1,5},{2,6},{3,7},{8,0},{9,1},{10,2},{11,3},{16,8},{17,9},{1... | collective-permute-start | bytes 786440 | tf_op jit(solution)/shard_map/ppermute | solution.py:242
  51.0 1.9 %copy-done.1 = bf16[2048,768]{1,0:T(8,128)(2,1)S(1)} copy-done((bf16[2048,768]{1,0:T(8,128)(2,1)S(1)}, bf16[2048,768]{1,0:T(8,128)(2,1)}, u32[]{:S(2)}) %copy-start.1) | copy-done | bytes 3145752
  52.9 5.9 %stats.7.refs_2_ = f32[256,128]{1,0:T(8,128)S(1)} custom-call(bf16[64,2048]{1,0:T(8,128)(2,1)S(1)} %collective-permute-done.5.refs_0_, bf16[32,2048]{1,0:T(8,128)(2,1)} %collective-permute-done.6.refs_1_, bf16[64,2048]{1,0:T(8,128)(2,1)S(1)} %collective-permute-done.7.refs_2_, bf16[32,2048]{1,0:T(8,128)(2,1)} %collective-permute-done.8.refs_3_, ...), custom_call_target="tpu_custom_call" | custom-call | flops 1610612736 | bytes 6291456 | tf_op jit(solution)/shard_map/stats/pallas_call | solution.py:137
  58.8 3.9 %stats.5.refs_0_ = f32[128,128]{1,0:T(8,128)S(1)} custom-call(bf16[128,2048]{1,0:T(8,128)(2,1)S(1)} %copy-done.4, bf16[2048,768]{1,0:T(8,128)(2,1)S(1)} %copy-done.2, bf16[2048,768]{1,0:T(8,128)(2,1)} %collective-permute-done.refs_2_.refs_5_.refs_7_, s32[8,128]{1,0:T(8,128)S(1)} %bitcast.7), custom_call_target="tpu_custom_call" | custom-call | flops 805306368 | bytes 6291456 | tf_op jit(solution)/shard_map/stats/pallas_call | solution.py:137
  62.7 4.7 %stats.6.refs_1_ = f32[192,128]{1,0:T(8,128)S(1)} custom-call(bf16[64,2048]{1,0:T(8,128)(2,1)S(1)} %collective-permute-done.1.refs_0_, bf16[32,2048]{1,0:T(8,128)(2,1)S(1)} %collective-permute-done.2.refs_1_, bf16[64,2048]{1,0:T(8,128)(2,1)S(1)} %collective-permute-done.3.refs_2_, bf16[32,2048]{1,0:T(8,128)(2,1)S(1)} %copy-done.6, ...), custom_call_target="tpu_custom_call" | custom-call | flops 1207959552 | bytes 6291456 | tf_op jit(solution)/shard_map/stats/pallas_call | solution.py:137
  67.5 5.8 %stats.8.refs_3_ = f32[256,128]{1,0:T(8,128)S(1)} custom-call(bf16[64,2048]{1,0:T(8,128)(2,1)S(1)} %collective-permute-done.10.refs_0_, bf16[32,2048]{1,0:T(8,128)(2,1)} %collective-permute-done.11.refs_1_, bf16[64,2048]{1,0:T(8,128)(2,1)S(1)} %collective-permute-done.12.refs_2_, bf16[32,2048]{1,0:T(8,128)(2,1)} %collective-permute-done.13.refs_3_, ...), custom_call_target="tpu_custom_call" | custom-call | flops 1610612736 | bytes 6291456 | tf_op jit(solution)/shard_map/stats/pallas_call | solution.py:137
  73.3 4.9 %stats.9.refs_4_ = f32[192,128]{1,0:T(8,128)S(1)} custom-call(bf16[64,2048]{1,0:T(8,128)(2,1)} %collective-permute-done.15.refs_0_, bf16[64,2048]{1,0:T(8,128)(2,1)} %collective-permute-done.16.refs_1_, bf16[32,2048]{1,0:T(8,128)(2,1)S(1)} %get-tuple-element.23.refs_2_, bf16[32,2048]{1,0:T(8,128)(2,1)S(1)} %get-tuple-element.22.refs_3_, ...), custom_call_target="tpu_custom_call" | custom-call | flops 1207959552 | bytes 6291456 | tf_op jit(solution)/shard_map/stats/pallas_call | solution.py:137
  78.2 0.8 pack.1
  79.0 3.6 %all-to-all-start.1 = ((f32[32,8,128]{2,1,0:T(8,128)}), f32[32,8,128]{2,1,0:T(8,128)S(1)}, u32[]{:S(2)}, u32[]{:S(2)}) async-start(f32[32,8,128]{2,1,0:T(8,128)} %pack.1), calls=%async_computation.1 | async-start | bytes 262144 | tf_op jit(solution)/shard_map/all_to_all | solution.py:279
  83.3 7.6 %all-to-all-done.1.r_ref = f32[32,8,128]{2,1,0:T(8,128)S(1)} async-done(((f32[32,8,128]{2,1,0:T(8,128)}), f32[32,8,128]{2,1,0:T(8,128)S(1)}, u32[]{:S(2)}, u32[]{:S(2)}) %all-to-all-start.1) | async-done | bytes 131104 | tf_op jit(solution)/shard_map/all_to_all | solution.py:279
  90.9 0.6 copy-done.8
  91.6 1.6 %finish.1 = (f32[2,128]{1,0:T(2,128)}, f32[2,128]{1,0:T(2,128)}, f32[1,1]{1,0:T(1,128)}, f32[1,1]{1,0:T(1,128)}) custom-call(f32[32,8,128]{2,1,0:T(8,128)} %copy-done.8, s32[1]{0:T(128)S(6)} %copy.9.len_ref), custom_call_target="tpu_custom_call" | custom-call | tf_op jit(solution)/shard_map/finish/pallas_call | solution.py:221
  (49 shorter events, 4.0 us)
Async XLA Ops:
  0.6 1.2 %copy-start = (bf16[256,2048]{1,0:T(8,128)(2,1)S(1)}, bf16[256,2048]{1,0:T(8,128)(2,1)}, u32[]{:S(2)}) copy-start(bf16[256,2048]{1,0:T(8,128)(2,1)} %param.5) | copy-start | bytes 3145732
  0.6 50.3 %collective-permute-start = (bf16[2048,768]{1,0:T(8,128)(2,1)}, bf16[2048,768]{1,0:T(8,128)(2,1)}, u32[]{:S(2)}, u32[]{:S(2)}) collective-permute-start(bf16[2048,768]{1,0:T(8,128)(2,1)} %refs_4_.3), channel_id=1, source_target_pairs={{0,1},{1,0},{2,3},{3,2},{4,5},{5,4},{6,7},{7,6},{8,9},{9,8},{10,11... | collective-permute-start | bytes 9437192 | tf_op jit(solution)/shard_map/ppermute | solution.py:242
  1.9 0.7 copy-start.7
  2.9 0.8 copy-start.3
  3.7 9.3 %collective-permute-start.3 = (bf16[64,2048]{1,0:T(8,128)(2,1)S(1)}, bf16[64,2048]{1,0:T(8,128)(2,1)S(1)}, u32[]{:S(2)}, u32[]{:S(2)}) collective-permute-start(bf16[64,2048]{1,0:T(8,128)(2,1)S(1)} %get-tuple-element.16), channel_id=1, source_target_pairs={{0,4},{1,5},{2,6},{3,7},{8,0},{9,1},{10,2},{11,3},{16,8},{17,9},{1... | collective-permute-start | bytes 786440 | tf_op jit(solution)/shard_map/ppermute | solution.py:242
  6.6 9.2 %collective-permute-start.1 = (bf16[64,2048]{1,0:T(8,128)(2,1)S(1)}, bf16[64,2048]{1,0:T(8,128)(2,1)S(1)}, u32[]{:S(2)}, u32[]{:S(2)}) collective-permute-start(bf16[64,2048]{1,0:T(8,128)(2,1)S(1)} %get-tuple-element.14), channel_id=1, source_target_pairs={{0,8},{1,9},{2,10},{3,11},{8,16},{9,17},{10,18},{11,19},{16,24},{1... | collective-permute-start | bytes 786440 | tf_op jit(solution)/shard_map/ppermute | solution.py:242
  6.7 11.7 %collective-permute-start.2 = (bf16[32,2048]{1,0:T(8,128)(2,1)S(1)}, bf16[32,2048]{1,0:T(8,128)(2,1)S(1)}, u32[]{:S(2)}, u32[]{:S(2)}) collective-permute-start(bf16[32,2048]{1,0:T(8,128)(2,1)S(1)} %get-tuple-element.15), channel_id=1, source_target_pairs={{0,8},{1,9},{2,10},{3,11},{8,16},{9,17},{10,18},{11,19},{16,24},{1... | collective-permute-start | bytes 393224 | tf_op jit(solution)/shard_map/ppermute | solution.py:242
  13.0 15.2 %collective-permute-start.7 = (bf16[64,2048]{1,0:T(8,128)(2,1)S(1)}, bf16[64,2048]{1,0:T(8,128)(2,1)S(1)}, u32[]{:S(2)}, u32[]{:S(2)}) collective-permute-start(bf16[64,2048]{1,0:T(8,128)(2,1)S(1)} %collective-permute-done.3.refs_2_), channel_id=1, source_target_pairs={{0,4},{1,5},{2,6},{3,7},{8,0},{9,1},{10,2},{11,3},{16,8},{17,9},{1... | collective-permute-start | bytes 786440 | tf_op jit(solution)/shard_map/ppermute | solution.py:242
  15.8 12.5 %collective-permute-start.5 = (bf16[64,2048]{1,0:T(8,128)(2,1)S(1)}, bf16[64,2048]{1,0:T(8,128)(2,1)S(1)}, u32[]{:S(2)}, u32[]{:S(2)}) collective-permute-start(bf16[64,2048]{1,0:T(8,128)(2,1)S(1)} %collective-permute-done.1.refs_0_), channel_id=1, source_target_pairs={{0,8},{1,9},{2,10},{3,11},{8,16},{9,17},{10,18},{11,19},{16,24},{1... | collective-permute-start | bytes 786440 | tf_op jit(solution)/shard_map/ppermute | solution.py:242
  15.9 10.2 %collective-permute-start.4 = (bf16[32,2048]{1,0:T(8,128)(2,1)S(1)}, bf16[32,2048]{1,0:T(8,128)(2,1)S(1)}, u32[]{:S(2)}, u32[]{:S(2)}) collective-permute-start(bf16[32,2048]{1,0:T(8,128)(2,1)S(1)} %get-tuple-element.17), channel_id=1, source_target_pairs={{0,4},{1,5},{2,6},{3,7},{8,0},{9,1},{10,2},{11,3},{16,8},{17,9},{1... | collective-permute-start | bytes 393224 | tf_op jit(solution)/shard_map/ppermute | solution.py:242
  18.4 16.2 %collective-permute-start.9 = (bf16[64,2048]{1,0:T(8,128)(2,1)S(1)}, bf16[64,2048]{1,0:T(8,128)(2,1)}, u32[]{:S(2)}, u32[]{:S(2)}) collective-permute-start(bf16[64,2048]{1,0:T(8,128)(2,1)S(1)} %pad_maximum_fusion), channel_id=1, source_target_pairs={{0,2},{1,3},{2,0},{3,1},{4,6},{5,7},{6,4},{7,5},{8,10},{9,11},{10,... | collective-permute-start | bytes 786440 | tf_op jit(solution)/shard_map/ppermute | solution.py:242
  21.3 29.7 %all-to-all-start = ((s32[8,1,128]{2,1,0:T(1,128)}), s32[8,1,128]{2,1,0:T(1,128)S(1)}, u32[]{:S(2)}, u32[]{:S(2)}) async-start(s32[8,1,128]{2,1,0:T(1,128)} %broadcast_in_dim.2), calls=%async_computation | async-start | bytes 8192 | tf_op jit(solution)/shard_map/all_to_all | solution.py:248
  26.1 22.9 %copy-start.5 = (bf16[32,2048]{1,0:T(8,128)(2,1)}, bf16[32,2048]{1,0:T(8,128)(2,1)S(1)}, u32[]{:S(2)}) copy-start(bf16[32,2048]{1,0:T(8,128)(2,1)S(1)} %collective-permute-done.4.refs_3_) | copy-start | bytes 393220
  26.1 6.5 %collective-permute-start.6 = (bf16[32,2048]{1,0:T(8,128)(2,1)S(1)}, bf16[32,2048]{1,0:T(8,128)(2,1)}, u32[]{:S(2)}, u32[]{:S(2)}) collective-permute-start(bf16[32,2048]{1,0:T(8,128)(2,1)S(1)} %collective-permute-done.2.refs_1_), channel_id=1, source_target_pairs={{0,8},{1,9},{2,10},{3,11},{8,16},{9,17},{10,18},{11,19},{16,24},{1... | collective-permute-start | bytes 393224 | tf_op jit(solution)/shard_map/ppermute | solution.py:242
  28.2 7.5 %collective-permute-start.8 = (bf16[32,2048]{1,0:T(8,128)(2,1)S(1)}, bf16[32,2048]{1,0:T(8,128)(2,1)}, u32[]{:S(2)}, u32[]{:S(2)}) collective-permute-start(bf16[32,2048]{1,0:T(8,128)(2,1)S(1)} %collective-permute-done.4.refs_3_), channel_id=1, source_target_pairs={{0,4},{1,5},{2,6},{3,7},{8,0},{9,1},{10,2},{11,3},{16,8},{17,9},{1... | collective-permute-start | bytes 393224 | tf_op jit(solution)/shard_map/ppermute | solution.py:242
  28.4 14.8 %collective-permute-start.14 = (bf16[64,2048]{1,0:T(8,128)(2,1)S(1)}, bf16[64,2048]{1,0:T(8,128)(2,1)S(1)}, u32[]{:S(2)}, u32[]{:S(2)}) collective-permute-start(bf16[64,2048]{1,0:T(8,128)(2,1)S(1)} %pad_maximum_fusion.1), channel_id=1, source_target_pairs={{0,2},{1,3},{2,0},{3,1},{4,6},{5,7},{6,4},{7,5},{8,10},{9,11},{10,... | collective-permute-start | bytes 786440 | tf_op jit(solution)/shard_map/ppermute | solution.py:242
  32.7 9.8 %collective-permute-start.10 = (bf16[64,2048]{1,0:T(8,128)(2,1)S(1)}, bf16[64,2048]{1,0:T(8,128)(2,1)S(1)}, u32[]{:S(2)}, u32[]{:S(2)}) collective-permute-start(bf16[64,2048]{1,0:T(8,128)(2,1)S(1)} %collective-permute-done.5.refs_0_), channel_id=1, source_target_pairs={{0,8},{1,9},{2,10},{3,11},{8,16},{9,17},{10,18},{11,19},{16,24},{1... | collective-permute-start | bytes 786440 | tf_op jit(solution)/shard_map/ppermute | solution.py:242
  34.6 7.5 %collective-permute-start.12 = (bf16[64,2048]{1,0:T(8,128)(2,1)S(1)}, bf16[64,2048]{1,0:T(8,128)(2,1)S(1)}, u32[]{:S(2)}, u32[]{:S(2)}) collective-permute-start(bf16[64,2048]{1,0:T(8,128)(2,1)S(1)} %collective-permute-done.7.refs_2_), channel_id=1, source_target_pairs={{0,4},{1,5},{2,6},{3,7},{8,0},{9,1},{10,2},{11,3},{16,8},{17,9},{1... | collective-permute-start | bytes 786440 | tf_op jit(solution)/shard_map/ppermute | solution.py:242
  35.7 31.7 %collective-permute-start.11 = (bf16[32,2048]{1,0:T(8,128)(2,1)}, bf16[32,2048]{1,0:T(8,128)(2,1)}, u32[]{:S(2)}, u32[]{:S(2)}) collective-permute-start(bf16[32,2048]{1,0:T(8,128)(2,1)} %collective-permute-done.6.refs_1_), channel_id=1, source_target_pairs={{0,8},{1,9},{2,10},{3,11},{8,16},{9,17},{10,18},{11,19},{16,24},{1... | collective-permute-start | bytes 393224 | tf_op jit(solution)/shard_map/ppermute | solution.py:242
  42.1 25.3 %collective-permute-start.13 = (bf16[32,2048]{1,0:T(8,128)(2,1)}, bf16[32,2048]{1,0:T(8,128)(2,1)}, u32[]{:S(2)}, u32[]{:S(2)}) collective-permute-start(bf16[32,2048]{1,0:T(8,128)(2,1)} %collective-permute-done.8.refs_3_), channel_id=1, source_target_pairs={{0,4},{1,5},{2,6},{3,7},{8,0},{9,1},{10,2},{11,3},{16,8},{17,9},{1... | collective-permute-start | bytes 393224 | tf_op jit(solution)/shard_map/ppermute | solution.py:242
  42.6 6.4 %collective-permute-start.17 = (bf16[64,2048]{1,0:T(8,128)(2,1)S(1)}, bf16[64,2048]{1,0:T(8,128)(2,1)S(1)}, u32[]{:S(2)}, u32[]{:S(2)}) collective-permute-start(bf16[64,2048]{1,0:T(8,128)(2,1)S(1)} %pad_maximum_fusion.2), channel_id=1, source_target_pairs={{0,2},{1,3},{2,0},{3,1},{4,6},{5,7},{6,4},{7,5},{8,10},{9,11},{10,... | collective-permute-start | bytes 786440 | tf_op jit(solution)/shard_map/ppermute | solution.py:242
  43.1 30.1 %collective-permute-start.15 = (bf16[64,2048]{1,0:T(8,128)(2,1)S(1)}, bf16[64,2048]{1,0:T(8,128)(2,1)}, u32[]{:S(2)}, u32[]{:S(2)}) collective-permute-start(bf16[64,2048]{1,0:T(8,128)(2,1)S(1)} %collective-permute-done.10.refs_0_), channel_id=1, source_target_pairs={{0,8},{1,9},{2,10},{3,11},{8,16},{9,17},{10,18},{11,19},{16,24},{1... | collective-permute-start | bytes 786440 | tf_op jit(solution)/shard_map/ppermute | solution.py:242
  49.0 24.3 %collective-permute-start.16 = (bf16[64,2048]{1,0:T(8,128)(2,1)S(1)}, bf16[64,2048]{1,0:T(8,128)(2,1)}, u32[]{:S(2)}, u32[]{:S(2)}) collective-permute-start(bf16[64,2048]{1,0:T(8,128)(2,1)S(1)} %collective-permute-done.12.refs_2_), channel_id=1, source_target_pairs={{0,4},{1,5},{2,6},{3,7},{8,0},{9,1},{10,2},{11,3},{16,8},{17,9},{1... | collective-permute-start | bytes 786440 | tf_op jit(solution)/shard_map/ppermute | solution.py:242
  51.0 1.9 %copy-start.1 = (bf16[2048,768]{1,0:T(8,128)(2,1)S(1)}, bf16[2048,768]{1,0:T(8,128)(2,1)}, u32[]{:S(2)}) copy-start(bf16[2048,768]{1,0:T(8,128)(2,1)} %refs_4_.3) | copy-start | bytes 9437188
  52.9 5.9 %copy-start.2 = (bf16[2048,768]{1,0:T(8,128)(2,1)S(1)}, bf16[2048,768]{1,0:T(8,128)(2,1)}, u32[]{:S(2)}) copy-start(bf16[2048,768]{1,0:T(8,128)(2,1)} %refs_4_.3) | copy-start | bytes 9437188
  52.9 5.9 %copy-start.4 = (bf16[128,2048]{1,0:T(8,128)(2,1)S(1)}, bf16[128,2048]{1,0:T(8,128)(2,1)}, u32[]{:S(2)}) copy-start(bf16[128,2048]{1,0:T(8,128)(2,1)} %copy-done.3) | copy-start | bytes 1572868
  58.8 3.9 %copy-start.6 = (bf16[32,2048]{1,0:T(8,128)(2,1)S(1)}, bf16[32,2048]{1,0:T(8,128)(2,1)}, u32[]{:S(2)}) copy-start(bf16[32,2048]{1,0:T(8,128)(2,1)} %copy-done.5) | copy-start | bytes 393220
  79.0 11.9 %all-to-all-start.1 = ((f32[32,8,128]{2,1,0:T(8,128)}), f32[32,8,128]{2,1,0:T(8,128)S(1)}, u32[]{:S(2)}, u32[]{:S(2)}) async-start(f32[32,8,128]{2,1,0:T(8,128)} %pack.1), calls=%async_computation.1 | async-start | bytes 262144 | tf_op jit(solution)/shard_map/all_to_all | solution.py:279
  90.9 0.6 copy-start.8

commit v2 on v1

v2 whole, which is shorter than its diff:
```python
import functools

import jax
import jax.numpy as jnp
from jax import lax
from jax.experimental import pallas as pl
from jax.experimental.pallas import tpu as pltpu
from jax.sharding import PartitionSpec as P

AXES = ("req", "tp")
LANES = 128
STATS = 8
DIGIT_BITS = 7
VMEM_BYTES = 10 * 1024 * 1024


def ring_place(req, n_req):
    half = n_req // 2
    return jnp.where(req % 2 == 0, req // 2, n_req - 1 - req // 2) if half else req


def ring_req(place, n_req):
    half = n_req // 2
    return jnp.where(place < half, 2 * place, 2 * (n_req - 1 - place) + 1)


def ring_req_py(place, n_req):
    place %= n_req
    return 2 * place if place < n_req // 2 else 2 * (n_req - 1 - place) + 1


def ring_pairs(n_req, n_tp, turn):
    pairs = []
    for place in range(n_req):
        here, there = ring_req_py(place, n_req), ring_req_py(place + turn, n_req)
        pairs += [(here * n_tp + t, there * n_tp + t) for t in range(n_tp)]
    return pairs


def tp_pairs(n_req, n_tp, bit):
    return [(r * n_tp + t, r * n_tp + (t ^ bit)) for r in range(n_req) for t in range(n_tp)]


def block_starts(rows, b_rows):
    g = rows // 2 - b_rows
    return (0, g, rows // 2, rows - g), (g, b_rows, b_rows, g)


def digits(target, first):
    lane = lax.broadcasted_iota(jnp.int32, (1, LANES), 1) - first
    shift = jnp.where(lane == 0, 2 * DIGIT_BITS, jnp.where(lane == 1, DIGIT_BITS, 0))
    digit = (target >> shift) & ((1 << DIGIT_BITS) - 1)
    return jnp.where((lane >= 0) & (lane < 3), digit, 0)


def undigits(ext, first):
    lane = lax.broadcasted_iota(jnp.int32, (1, LANES), 1) - first
    base = float(1 << DIGIT_BITS)
    weight = jnp.where(
        lane == 0, base * base, jnp.where(lane == 1, base, jnp.where(lane == 2, 1.0, 0.0))
    )
    return jnp.sum(ext.astype(jnp.float32) * weight, axis=1, keepdims=True)


def norm_kernel(
    b_rows, x_hbm, gain_hbm, tid_ref, xn_ref, acw_ref, bcw_ref, accw_ref, bccw_ref,
    x_ref, gain_ref, ext_ref, sems,
):
    rows, d = x_ref.shape
    tp = lax.axis_index("tp")
    core, plane = tp % 2, tp // 2
    mine = pl.ds(pl.multiple_of(core * rows, rows), rows)
    get_x = pltpu.make_async_copy(x_hbm.at[mine, :], x_ref, sems.at[0])
    get_gain = pltpu.make_async_copy(gain_hbm, gain_ref, sems.at[1])
    get_x.start()
    get_gain.start()
    target = jnp.where(core == 0, tid_ref[0:1, :], tid_ref[1:2, :])
    target = jnp.broadcast_to(target, (8, rows)).T[:, :1]
    ext = digits(target, 0)
    ext_ref[0] = ext
    ext_ref[1] = digits(target, 3)
    xn_ref[:, d:] = ext.astype(jnp.float32).astype(jnp.bfloat16)
    get_x.wait()
    get_gain.wait()
    feats = x_ref[...].astype(jnp.float32)
    scale = lax.rsqrt(jnp.mean(feats * feats, axis=-1, keepdims=True) + 1e-06)
    xn_ref[:, :d] = (feats * scale * gain_ref[...]).astype(jnp.bfloat16)
    starts, sizes = block_starts(rows, b_rows)
    for a_ref, b_ref, flip in ((acw_ref, bcw_ref, 0), (accw_ref, bccw_ref, 1)):
        down = plane != flip
        place = [
            pl.ds(pl.multiple_of(jnp.where(down, starts[3 - j], starts[j]), 16), sizes[j])
            for j in range(3)
        ]
        at = 0
        for j in range(2):
            here = pl.ds(at, sizes[j])
            a_ref[here, :d] = xn_ref[place[j], :d]
            own = ext_ref[0, place[j], :]
            if at < b_rows:
                part = min(b_rows - at, sizes[j])
                beside = pl.ds(pl.multiple_of(place[2].start + at, 16), part)
                a_ref[pl.ds(at, part), d:] = (
                    (own[:part] + ext_ref[1, beside, :]).astype(jnp.float32).astype(jnp.bfloat16)
                )
                if part < sizes[j]:
                    a_ref[pl.ds(at + part, sizes[j] - part), d:] = (
                        own[part:].astype(jnp.float32).astype(jnp.bfloat16)
                    )
            else:
                a_ref[here, d:] = own.astype(jnp.float32).astype(jnp.bfloat16)
            at += sizes[j]
        b_ref[...] = xn_ref[place[2], :d]


def norm_rows(hidden, norm_gain, target_ids, rows, b_rows):
    d = hidden.shape[1]
    a, wide = rows // 2, d + LANES
    shapes = [(rows, wide), (a, wide), (b_rows, d), (a, wide), (b_rows, d)]
    return pl.pallas_call(
        functools.partial(norm_kernel, b_rows),
        out_shape=[jax.ShapeDtypeStruct(s, jnp.bfloat16) for s in shapes],
        in_specs=[pl.BlockSpec(memory_space=pl.ANY)] * 2 + [pl.BlockSpec(memory_space=pltpu.VMEM)],
        scratch_shapes=[
            pltpu.VMEM((rows, d), jnp.bfloat16),
            pltpu.VMEM((1, d), jnp.float32),
            pltpu.VMEM((2, rows, LANES), jnp.int32),
            pltpu.SemaphoreType.DMA((2,)),
        ],
        compiler_params=pltpu.CompilerParams(vmem_limit_bytes=VMEM_BYTES),
        name="norm",
    )(
        pltpu.with_memory_space_constraint(hidden, pltpu.HBM),
        pltpu.with_memory_space_constraint(norm_gain.reshape(1, d), pltpu.HBM),
        target_ids.reshape(2, rows),
    )


def join_kernel(first_ref, second_ref, out_ref):
    half = out_ref.shape[0] // 2
    out_ref[:half, :] = first_ref[:half, :]
    out_ref[half:, :] = second_ref[:half, :]


def join_heads(first, second, count):
    return pl.pallas_call(
        join_kernel,
        out_shape=jax.ShapeDtypeStruct((2 * count, first.shape[1]), first.dtype),
        compiler_params=pltpu.CompilerParams(vmem_limit_bytes=VMEM_BYTES),
        name="join",
    )(first, second)


def piece_segments(part):
    return {"all": (0, 1, 2, 3), "a": (0, 1), "b": (2,), "y": (3,)}[part]


def stats_kernel(metas, n_req, n_tp, b_rows, rows, earlier, tail, *refs):
    n = len(metas)
    piece_refs, (w0_ref, w1_ref), refs = refs[:n], refs[n : n + 2], refs[n + 2 :]
    if tail:
        stat_refs, (packed_ref, x_s, l_s, t_s, out_ref) = refs[: len(earlier)], refs[len(earlier) :]
    else:
        out_ref, x_s, l_s, t_s = refs
    req, tp = lax.axis_index("req"), lax.axis_index("tp")
    d, vdev = w0_ref.shape
    total = x_s.shape[0]

    lane = lax.broadcasted_iota(jnp.int32, (1, LANES), 1)
    at = 0
    for parts, ref in zip(metas, piece_refs):
        here = pl.ds(at, ref.shape[0])
        x_s[here, :] = ref[:, :d]
        if parts[0][2] == "b":
            t_s[here, :] = undigits(before[: ref.shape[0], d:], 3)
        else:
            t_s[here, :] = undigits(ref[:, d:], 0)
        before = ref
        at += ref.shape[0]

    x = x_s[...]
    l_s[:, :vdev] = jnp.dot(x, w0_ref[...], preferred_element_type=jnp.float32)
    l_s[:, vdev:] = jnp.dot(x, w1_ref[...], preferred_element_type=jnp.float32)

    column = lax.broadcasted_iota(jnp.int32, (1, vdev), 1)
    ids0 = (column + (req * n_tp + tp) * vdev).astype(jnp.float32)
    ids1 = (column + (req * n_tp + (tp ^ 1)) * vdev).astype(jnp.float32)
    step = 16

    def body(i, _):
        here = pl.ds(pl.multiple_of(i * step, step), step)
        logits = l_s[here, :]
        target = t_s[here, :]
        top = jnp.max(logits, axis=1, keepdims=True)
        shifted = jnp.exp(logits - top)
        weight_sum = jnp.sum(shifted, axis=1, keepdims=True)
        weighted = jnp.sum(shifted * logits, axis=1, keepdims=True)
        hit0 = jnp.where(ids0 == target, logits[:, :vdev], 0.0)
        hit1 = jnp.where(ids1 == target, logits[:, vdev:], 0.0)
        picked = jnp.sum(hit0 + hit1, axis=1, keepdims=True)
        out_ref[here, :] = jnp.where(
            lane == 0, top, jnp.where(lane == 1, weight_sum, jnp.where(lane == 2, weighted, picked))
        )
        return 0

    lax.fori_loop(0, total // step, body, 0, unroll=4)
    if tail:
        pack_stats(earlier + (metas,), (*stat_refs, out_ref), packed_ref, n_req, n_tp, b_rows, rows)


def pack_stats(metas, stat_refs, packed_ref, n_req, n_tp, b_rows, rows):
    plane = lax.axis_index("tp") // 2
    place = ring_place(lax.axis_index("req"), n_req)
    starts, sizes = block_starts(rows, b_rows)
    shards = {}
    for pieces, ref in zip(metas, stat_refs):
        at = 0
        for turn, hops, part in (p for parts in pieces for p in parts):
            for j in piece_segments(part):
                shards.setdefault((turn, hops) if 2 * hops != n_req else (0, hops), []).append(
                    (turn, j, ref[pl.ds(at, sizes[j]), :])
                )
                at += sizes[j]
    for (turn, hops), found in shards.items():
        if turn == 0 and hops:
            up = {j: v for t, j, v in found if t > 0} | {3 - j: v for t, j, v in found if t < 0}
        else:
            up = {j: v for _, j, v in found}
        ordered = jnp.concatenate([up[j] for j in range(4)], axis=0)
        if hops:
            flipped = jnp.concatenate([up[3 - j] for j in range(4)], axis=0)
            down = plane != (0 if turn >= 0 else 1)
            ordered = jnp.where(down, flipped, ordered)
        source = ring_req((place - (turn or 1) * hops + n_req) % n_req, n_req)
        packed = ordered.T[:STATS, :]
        for t in range(n_tp):
            packed_ref[source * n_tp + t] = packed


def stats_of(pieces, metas, w0, w1, n_req, n_tp, b_rows, rows, earlier=(), stats=(), tail=False):
    d, vdev = w0.shape
    total = sum(p.shape[0] for p in pieces)
    row_stats = (total, LANES)
    return pl.pallas_call(
        functools.partial(stats_kernel, metas, n_req, n_tp, b_rows, rows, earlier, tail),
        out_shape=jax.ShapeDtypeStruct(
            (n_req * n_tp, STATS, rows) if tail else row_stats, jnp.float32
        ),
        scratch_shapes=[
            pltpu.VMEM((total, d), jnp.bfloat16),
            pltpu.VMEM((total, 2 * vdev), jnp.float32),
            pltpu.VMEM((total, 1), jnp.float32),
        ]
        + [pltpu.VMEM(row_stats, jnp.float32)] * tail,
        compiler_params=pltpu.CompilerParams(vmem_limit_bytes=VMEM_BYTES),
        cost_estimate=pl.CostEstimate(
            flops=4 * total * d * vdev, bytes_accessed=4 * d * vdev, transcendentals=2 * total * vdev
        ),
        name="stats_last" if tail else "stats",
    )(*pieces, w0, w1, *stats)


def final_kernel(n_parts, r_ref, len_ref, lp_ref, ent_ref, mean_ref, top_ref):
    rows = r_ref.shape[2]
    length = len_ref[0]
    total = jnp.float32(0.0)
    best = jnp.float32(-1e30)
    for half in range(2):
        mine = [r_ref[2 * k + half] for k in range(n_parts // 2)]
        top = functools.reduce(jnp.maximum, [m[0:1] for m in mine])
        scaled = functools.reduce(jnp.add, [m * jnp.exp(m[0:1] - top) for m in mine])
        picked = functools.reduce(jnp.add, [m[3:4] for m in mine])
        weight_sum, weighted = scaled[1:2], scaled[2:3]
        log_norm = top + jnp.log(weight_sum)
        slot = lax.broadcasted_iota(jnp.int32, (1, rows), 1) + half * rows
        live = slot < length
        logprob = jnp.where(live, picked - log_norm, 0.0)
        lp_ref[half : half + 1, :] = logprob
        ent_ref[half : half + 1, :] = jnp.where(live, log_norm - weighted / weight_sum, 0.0)
        total += jnp.sum(logprob)
        best = jnp.maximum(best, jnp.max(jnp.where(live, top, -1e30)))
    mean_ref[...] = jnp.full((1, 1), total, jnp.float32) / length.astype(jnp.float32)
    top_ref[...] = jnp.full((1, 1), best, jnp.float32)


def finish(received, lengths):
    n_parts, _, rows = received.shape
    outs = pl.pallas_call(
        functools.partial(final_kernel, n_parts),
        out_shape=[jax.ShapeDtypeStruct((2, rows), jnp.float32)] * 2
        + [jax.ShapeDtypeStruct((1, 1), jnp.float32)] * 2,
        in_specs=[
            pl.BlockSpec(memory_space=pltpu.VMEM),
            pl.BlockSpec(memory_space=pltpu.SMEM),
        ],
        compiler_params=pltpu.CompilerParams(vmem_limit_bytes=VMEM_BYTES),
        name="finish",
    )(received, lengths)
    return tuple(o.reshape(-1) for o in outs)


def per_device(n_req, n_tp, hidden_states, norm_gain, head, target_ids, lengths):
    rows = hidden_states.shape[0] // 2
    b_rows = rows // 4
    cw, ccw = ring_pairs(n_req, n_tp, 1), ring_pairs(n_req, n_tp, -1)
    other_core, other_y = tp_pairs(n_req, n_tp, 1), tp_pairs(n_req, n_tp, 2)

    def send(value, pairs):
        return lax.ppermute(value, AXES, pairs)

    other_head = send(head, other_core)
    xn, a_cw, b_cw, a_ccw, b_ccw = norm_rows(hidden_states, norm_gain, target_ids, rows, b_rows)
    sizes = (n_req, n_tp, b_rows, rows)
    g = rows // 2 - b_rows
    meta = (((0, 0, "all"),),)
    metas = [meta]
    stats = [stats_of([xn], meta, head, other_head, *sizes)]
    y_piece = None
    for hops in range(1, n_req // 2 + 1):
        last = 2 * hops == n_req
        a_cw, a_ccw = send(a_cw, cw), send(a_ccw, ccw)
        if not last:
            b_cw, b_ccw = send(b_cw, cw), send(b_ccw, ccw)
        if hops > 1:
            y_next = send(y_message, other_y)
            stats.append(stats_of(pieces, meta, head, other_head, *sizes))
            metas.append(meta)
        a_cw, a_ccw, stats[-1] = lax.optimization_barrier((a_cw, a_ccw, stats[-1]))
        if last:
            pieces, meta = [a_cw, a_ccw], [((1, hops, "a"),), ((-1, hops, "a"),)]
        else:
            y_message = join_heads(a_cw, a_ccw, g)
            pieces = [a_cw, b_cw, a_ccw, b_ccw]
            meta = [((1, hops, "a"),), ((1, hops, "b"),), ((-1, hops, "a"),), ((-1, hops, "b"),)]
        if hops > 1:
            pieces.append(y_next)
            meta.append(((1, hops - 1, "y"), (-1, hops - 1, "y")))
        meta = tuple(meta)
    packed = stats_of(
        pieces, meta, head, other_head, *sizes, earlier=tuple(metas), stats=stats, tail=True
    )
    received = lax.all_to_all(packed, AXES, 0, 0, tiled=True)
    return finish(received, lengths)


def solution(mesh):
    n_req, n_tp = mesh.shape["req"], mesh.shape["tp"]
    in_specs = (P("req", None), P(), P(None, ("req", "tp")), P("req"), P("req"))
    out_specs = (P("req"), P("req"), P("req"), P("req"))
    return jax.shard_map(
        functools.partial(per_device, n_req, n_tp),
        mesh=mesh,
        in_specs=in_specs,
        out_specs=out_specs,
        check_vma=False,
    )
```

time: 93.6 us -> 65.4 us (0.70)
  Pallas kernels: 27.9 us -> 15 us
  starting transfers between devices: 30.5 us -> 24.9 us
  local copies, waits for them, and re-layouts: 7.18 us -> 2.57 us
  waiting for transfers between devices: 25.9 us -> 21.3 us
    pallas_call x6 -> x8, Pallas kernels: 26 us -> 12.9 us  [the longest x5 12.9 us: stats_of(): pl.pallas_call(functools.partial(stats_kernel, metas, n_req, n_tp, b_rows...]
    all_to_all x1 -> x0, starting transfers between devices: 4.88 us -> none  [per_device(): lax.all_to_all(jnp.broadcast_to(my_targets[None, :], (n_req, rows)), 'req...]
    ppermute x18, waiting for transfers between devices: 18.3 us -> 13.7 us  [send(): return lax.ppermute(value, AXES, pairs)]
    unnamed x18 -> x6, local copies, waits for them, and re-layouts: 4.72 us -> 2.57 us
    ppermute x18, starting transfers between devices: 22 us -> 20.1 us  [send(): return lax.ppermute(value, AXES, pairs)]
    all_to_all x1, starting transfers between devices: 3.64 us -> 4.8 us  [per_device(): received = lax.all_to_all(packed, AXES, 0, 0, tiled=True)]
    slice x9 -> x0, local copies, waits for them, and re-layouts: 1.08 us -> none  [the longest x3 1.02 us: per_device(): pieces += [y_piece[:g], y_piece[g:]]]
    pallas_call x1, Pallas kernels: 0.3 us -> 1.37 us  [norm_rows(): pl.pallas_call(functools.partial(norm_kernel, b_rows), out_shape=[jax.Sha...]
  transfers between devices with their start and end apart: 20 -> 19, of which waited for: 7 -> 8; matrix products, arithmetic and copies ran while one was open for 3% -> 0% of each run, Pallas kernels for 22% -> 17%
where the time goes in v2:
time: 65.4 us; the launch traced here: 65.1 us
  starting transfers between devices  24.9 us (38%)
  waiting for transfers between devices  21.3 us (33%)
  Pallas kernels  15 us (23%)
  local copies, waits for them, and re-layouts  2.57 us (4%)
  between operations  1.36 us (2%)
    ppermute x18, starting transfers between devices, send(): return lax.ppermute(value, AXES, pairs)  20.1 us
    ppermute x18, waiting for transfers between devices, send(): return lax.ppermute(value, AXES, pairs)  13.7 us
    pallas_call x5, Pallas kernels, stats_of(): pl.pallas_call(functools.partial(stats_kernel, metas, n_req, n_tp, b_rows...  12.9 us
    all_to_all x1, waiting for transfers between devices, per_device(): received = lax.all_to_all(packed, AXES, 0, 0, tiled=True)  7.58 us
    all_to_all x1, starting transfers between devices, per_device(): received = lax.all_to_all(packed, AXES, 0, 0, tiled=True)  4.8 us
    unnamed x6, local copies, waits for them, and re-layouts  2.57 us
    pallas_call x1, Pallas kernels, norm_rows(): pl.pallas_call(functools.partial(norm_kernel, b_rows), out_shape=[jax.Sha...  1.37 us
  transfers between devices with their start and end apart: 19, of which 8 were waited for; matrix products, arithmetic and copies ran while one was open for 0% of the time, Pallas kernels for 17%

profile of v2, /device:TPU:0, one launch (start us, length us, event | category | flops | bytes accessed | tf_op | source)
XLA Modules:
  0.0 65.1 jit_solution(2362147690565232446)
XLA Ops:
  0.6 0.5 collective-permute-start.2
  1.2 0.7 %copy-done.2 = s32[256]{0:T(256)S(1)} copy-done((s32[256]{0:T(256)S(1)}, s32[256]{0:T(256)}, u32[]{:S(2)}) %copy-start.2) | copy-done | bytes 1048
  1.8 1.4 %norm.1 = (bf16[128,2176]{1,0:T(8,128)(2,1)S(1)}, bf16[64,2176]{1,0:T(8,128)(2,1)S(1)}, bf16[32,2048]{1,0:T(8,128)(2,1)S(1)}, bf16[64,2176]{1,0:T(8,128)(2,1)S(1)}, bf16[32,2048]{1,0:T(8,128)(2,1)S(1)}) custom-call(bf16[256,2048]{1,0:T(8,128)(2,1)} %x_hbm.1, f32[1,2048]{1,0:T(1,128)} %bitcast.7, s32[2,128]{1,0:T(2,128)S(1)} %bitcast.6), custom_call_target="tpu_custom_call" | custom-call | tf_op jit(solution)/shard_map/norm/pallas_call | solution.py:120
  3.2 2.6 %collective-permute-start = (bf16[64,2176]{1,0:T(8,128)(2,1)S(1)}, bf16[64,2176]{1,0:T(8,128)(2,1)S(1)}, u32[]{:S(2)}, u32[]{:S(2)}) collective-permute-start(bf16[64,2176]{1,0:T(8,128)(2,1)S(1)} %get-tuple-element.25), channel_id=1, source_target_pairs={{0,8},{1,9},{2,10},{3,11},{8,16},{9,17},{10,18},{11,19},{16,24},{1... | collective-permute-start | bytes 835592 | tf_op jit(solution)/shard_map/ppermute | solution.py:309
  5.9 0.8 %collective-permute-done.2.refs_2_.refs_5_.refs_6_.refs_4_ = bf16[2048,768]{1,0:T(8,128)(2,1)S(1)} collective-permute-done((bf16[2048,768]{1,0:T(8,128)(2,1)}, bf16[2048,768]{1,0:T(8,128)(2,1)S(1)}, u32[]{:S(2)}, u32[]{:S(2)}) %collective-permute-start.2) | collective-permute-done | bytes 3145760 | tf_op jit(solution)/shard_map/ppermute | solution.py:309
  6.6 1.9 %copy-done = bf16[2048,768]{1,0:T(8,128)(2,1)S(1)} copy-done((bf16[2048,768]{1,0:T(8,128)(2,1)S(1)}, bf16[2048,768]{1,0:T(8,128)(2,1)}, u32[]{:S(2)}) %copy-start) | copy-done | bytes 3145752
  8.5 1.6 %stats.4.refs_5_ = f32[128,128]{1,0:T(8,128)S(1)} custom-call(bf16[128,2176]{1,0:T(8,128)(2,1)S(1)} %get-tuple-element.27.refs_0_, bf16[2048,768]{1,0:T(8,128)(2,1)S(1)} %copy-done, bf16[2048,768]{1,0:T(8,128)(2,1)S(1)} %collective-permute-done.2.refs_2_.refs_5_.refs_6_.refs_4_), custom_call_target="tpu_custom_call" | custom-call | flops 805306368 | bytes 6291456 | tf_op jit(solution)/shard_map/stats/pallas_call | solution.py:244
  10.1 3.0 %collective-permute-done.refs_0_.first_ref = bf16[64,2176]{1,0:T(8,128)(2,1)S(1)} collective-permute-done((bf16[64,2176]{1,0:T(8,128)(2,1)S(1)}, bf16[64,2176]{1,0:T(8,128)(2,1)S(1)}, u32[]{:S(2)}, u32[]{:S(2)}) %collective-permute-start) | collective-permute-done | bytes 278560 | tf_op jit(solution)/shard_map/ppermute | solution.py:309
  13.1 1.5 %collective-permute-done.1.refs_2_.second_ref = bf16[64,2176]{1,0:T(8,128)(2,1)S(1)} collective-permute-done((bf16[64,2176]{1,0:T(8,128)(2,1)S(1)}, bf16[64,2176]{1,0:T(8,128)(2,1)S(1)}, u32[]{:S(2)}, u32[]{:S(2)}) %collective-permute-start.1) | collective-permute-done | bytes 278560 | tf_op jit(solution)/shard_map/ppermute | solution.py:309
  14.6 1.6 %collective-permute-start.3 = (bf16[64,2176]{1,0:T(8,128)(2,1)S(1)}, bf16[64,2176]{1,0:T(8,128)(2,1)S(1)}, u32[]{:S(2)}, u32[]{:S(2)}) collective-permute-start(bf16[64,2176]{1,0:T(8,128)(2,1)S(1)} %collective-permute-done.refs_0_.first_ref), channel_id=1, source_target_pairs={{0,8},{1,9},{2,10},{3,11},{8,16},{9,17},{10,18},{11,19},{16,24},{1... | collective-permute-start | bytes 835592 | tf_op jit(solution)/shard_map/ppermute | solution.py:309
  16.7 1.6 %collective-permute-start.5 = (bf16[32,2048]{1,0:T(8,128)(2,1)S(1)}, bf16[32,2048]{1,0:T(8,128)(2,1)S(1)}, u32[]{:S(2)}, u32[]{:S(2)}) collective-permute-start(bf16[32,2048]{1,0:T(8,128)(2,1)S(1)} %get-tuple-element.30), channel_id=1, source_target_pairs={{0,8},{1,9},{2,10},{3,11},{8,16},{9,17},{10,18},{11,19},{16,24},{1... | collective-permute-start | bytes 393224 | tf_op jit(solution)/shard_map/ppermute | solution.py:309
  18.7 1.6 %collective-permute-start.11 = (bf16[64,2176]{1,0:T(8,128)(2,1)S(1)}, bf16[64,2176]{1,0:T(8,128)(2,1)S(1)}, u32[]{:S(2)}, u32[]{:S(2)}) collective-permute-start(bf16[64,2176]{1,0:T(8,128)(2,1)S(1)} %join.3), channel_id=1, source_target_pairs={{0,2},{1,3},{2,0},{3,1},{4,6},{5,7},{6,4},{7,5},{8,10},{9,11},{10,... | collective-permute-start | bytes 835592 | tf_op jit(solution)/shard_map/ppermute | solution.py:309
  20.3 5.1 %collective-permute-done.5.refs_1_ = bf16[32,2048]{1,0:T(8,128)(2,1)S(1)} collective-permute-done((bf16[32,2048]{1,0:T(8,128)(2,1)S(1)}, bf16[32,2048]{1,0:T(8,128)(2,1)S(1)}, u32[]{:S(2)}, u32[]{:S(2)}) %collective-permute-start.5) | collective-permute-done | bytes 131104 | tf_op jit(solution)/shard_map/ppermute | solution.py:309
  25.4 1.6 %collective-permute-start.9 = (bf16[32,2048]{1,0:T(8,128)(2,1)S(1)}, bf16[32,2048]{1,0:T(8,128)(2,1)S(1)}, u32[]{:S(2)}, u32[]{:S(2)}) collective-permute-start(bf16[32,2048]{1,0:T(8,128)(2,1)S(1)} %collective-permute-done.5.refs_1_), channel_id=1, source_target_pairs={{0,8},{1,9},{2,10},{3,11},{8,16},{9,17},{10,18},{11,19},{16,24},{1... | collective-permute-start | bytes 393224 | tf_op jit(solution)/shard_map/ppermute | solution.py:309
  27.0 0.4 collective-permute-start.10
  27.4 2.3 %stats.5.refs_6_ = f32[192,128]{1,0:T(8,128)S(1)} custom-call(bf16[64,2176]{1,0:T(8,128)(2,1)S(1)} %collective-permute-done.refs_0_.first_ref, bf16[32,2048]{1,0:T(8,128)(2,1)S(1)} %collective-permute-done.5.refs_1_, bf16[64,2176]{1,0:T(8,128)(2,1)S(1)} %collective-permute-done.1.refs_2_.second_ref, bf16[32,2048]{1,0:T(8,128)(2,1)S(1)} %collective-permute-done.6.refs_3_, ...), custom_call_target="tpu_custom_call" | custom-call | flops 1207959552 | bytes 6291456 | tf_op jit(solution)/shard_map/stats/pallas_call | solution.py:244
  29.7 1.6 %collective-permute-start.7 = (bf16[64,2176]{1,0:T(8,128)(2,1)S(1)}, bf16[64,2176]{1,0:T(8,128)(2,1)S(1)}, u32[]{:S(2)}, u32[]{:S(2)}) collective-permute-start(bf16[64,2176]{1,0:T(8,128)(2,1)S(1)} %collective-permute-done.3.refs_0_.first_ref), channel_id=1, source_target_pairs={{0,8},{1,9},{2,10},{3,11},{8,16},{9,17},{10,18},{11,19},{16,24},{1... | collective-permute-start | bytes 835592 | tf_op jit(solution)/shard_map/ppermute | solution.py:309
  31.3 0.5 collective-permute-start.8
  31.8 1.6 %collective-permute-start.14 = (bf16[32,2048]{1,0:T(8,128)(2,1)S(1)}, bf16[32,2048]{1,0:T(8,128)(2,1)S(1)}, u32[]{:S(2)}, u32[]{:S(2)}) collective-permute-start(bf16[32,2048]{1,0:T(8,128)(2,1)S(1)} %collective-permute-done.9.refs_1_), channel_id=1, source_target_pairs={{0,8},{1,9},{2,10},{3,11},{8,16},{9,17},{10,18},{11,19},{16,24},{1... | collective-permute-start | bytes 393224 | tf_op jit(solution)/shard_map/ppermute | solution.py:309
  33.4 0.5 collective-permute-start.15
  33.9 1.6 %collective-permute-start.16 = (bf16[64,2176]{1,0:T(8,128)(2,1)S(1)}, bf16[64,2176]{1,0:T(8,128)(2,1)S(1)}, u32[]{:S(2)}, u32[]{:S(2)}) collective-permute-start(bf16[64,2176]{1,0:T(8,128)(2,1)S(1)} %join.4), channel_id=1, source_target_pairs={{0,2},{1,3},{2,0},{3,1},{4,6},{5,7},{6,4},{7,5},{8,10},{9,11},{10,... | collective-permute-start | bytes 835592 | tf_op jit(solution)/shard_map/ppermute | solution.py:309
  35.5 3.0 %stats.6.refs_7_ = f32[256,128]{1,0:T(8,128)S(1)} custom-call(bf16[64,2176]{1,0:T(8,128)(2,1)S(1)} %collective-permute-done.3.refs_0_.first_ref, bf16[32,2048]{1,0:T(8,128)(2,1)S(1)} %collective-permute-done.9.refs_1_, bf16[64,2176]{1,0:T(8,128)(2,1)S(1)} %collective-permute-done.4.refs_2_.second_ref, bf16[32,2048]{1,0:T(8,128)(2,1)S(1)} %collective-permute-done.10.refs_3_, ...), custom_call_target="tpu_custom_call" | custom-call | flops 1610612736 | bytes 6291456 | tf_op jit(solution)/shard_map/stats/pallas_call | solution.py:244
  38.4 1.2 %collective-permute-done.8.refs_2_.second_ref = bf16[64,2176]{1,0:T(8,128)(2,1)S(1)} collective-permute-done((bf16[64,2176]{1,0:T(8,128)(2,1)S(1)}, bf16[64,2176]{1,0:T(8,128)(2,1)S(1)}, u32[]{:S(2)}, u32[]{:S(2)}) %collective-permute-start.8) | collective-permute-done | bytes 278560 | tf_op jit(solution)/shard_map/ppermute | solution.py:309
  39.6 1.6 %collective-permute-start.12 = (bf16[64,2176]{1,0:T(8,128)(2,1)S(1)}, bf16[64,2176]{1,0:T(8,128)(2,1)S(1)}, u32[]{:S(2)}, u32[]{:S(2)}) collective-permute-start(bf16[64,2176]{1,0:T(8,128)(2,1)S(1)} %collective-permute-done.7.refs_0_.first_ref), channel_id=1, source_target_pairs={{0,8},{1,9},{2,10},{3,11},{8,16},{9,17},{10,18},{11,19},{16,24},{1... | collective-permute-start | bytes 835592 | tf_op jit(solution)/shard_map/ppermute | solution.py:309
  41.7 1.6 %collective-permute-start.17 = (bf16[64,2176]{1,0:T(8,128)(2,1)S(1)}, bf16[64,2176]{1,0:T(8,128)(2,1)S(1)}, u32[]{:S(2)}, u32[]{:S(2)}) collective-permute-start(bf16[64,2176]{1,0:T(8,128)(2,1)S(1)} %join.5), channel_id=1, source_target_pairs={{0,2},{1,3},{2,0},{3,1},{4,6},{5,7},{6,4},{7,5},{8,10},{9,11},{10,... | collective-permute-start | bytes 835592 | tf_op jit(solution)/shard_map/ppermute | solution.py:309
  43.3 3.0 %stats.7.refs_8_ = f32[256,128]{1,0:T(8,128)S(1)} custom-call(bf16[64,2176]{1,0:T(8,128)(2,1)S(1)} %collective-permute-done.7.refs_0_.first_ref, bf16[32,2048]{1,0:T(8,128)(2,1)S(1)} %collective-permute-done.14.refs_1_, bf16[64,2176]{1,0:T(8,128)(2,1)S(1)} %collective-permute-done.8.refs_2_.second_ref, bf16[32,2048]{1,0:T(8,128)(2,1)S(1)} %collective-permute-done.15.refs_3_, ...), custom_call_target="tpu_custom_call" | custom-call | flops 1610612736 | bytes 6291456 | tf_op jit(solution)/shard_map/stats/pallas_call | solution.py:244
  46.3 1.5 %collective-permute-done.13.refs_1_ = bf16[64,2176]{1,0:T(8,128)(2,1)S(1)} collective-permute-done((bf16[64,2176]{1,0:T(8,128)(2,1)S(1)}, bf16[64,2176]{1,0:T(8,128)(2,1)S(1)}, u32[]{:S(2)}, u32[]{:S(2)}) %collective-permute-start.13) | collective-permute-done | bytes 278560 | tf_op jit(solution)/shard_map/ppermute | solution.py:309
  47.8 0.5 collective-permute-done.17.refs_2_
  48.3 3.1 %stats_last.1 = f32[32,8,128]{2,1,0:T(8,128)} custom-call(bf16[64,2176]{1,0:T(8,128)(2,1)S(1)} %collective-permute-done.12.refs_0_, bf16[64,2176]{1,0:T(8,128)(2,1)S(1)} %collective-permute-done.13.refs_1_, bf16[64,2176]{1,0:T(8,128)(2,1)S(1)} %collective-permute-done.17.refs_2_, bf16[2048,768]{1,0:T(8,128)(2,1)S(1)} %copy-done.1, ...), custom_call_target="tpu_custom_call" | custom-call | flops 1207959552 | bytes 6291456 | tf_op jit(solution)/shard_map/stats_last/pallas_call | solution.py:244
  51.4 4.8 %all-to-all-start = ((f32[32,8,128]{2,1,0:T(8,128)}), f32[32,8,128]{2,1,0:T(8,128)S(1)}, u32[]{:S(2)}, u32[]{:S(2)}) async-start(f32[32,8,128]{2,1,0:T(8,128)} %stats_last.1), calls=%async_computation | async-start | bytes 262144 | tf_op jit(solution)/shard_map/all_to_all | solution.py:342
  56.9 7.6 %all-to-all-done.r_ref = f32[32,8,128]{2,1,0:T(8,128)S(1)} async-done(((f32[32,8,128]{2,1,0:T(8,128)}), f32[32,8,128]{2,1,0:T(8,128)S(1)}, u32[]{:S(2)}, u32[]{:S(2)}) %all-to-all-start) | async-done | bytes 131104 | tf_op jit(solution)/shard_map/all_to_all | solution.py:342
  64.4 0.7 %finish.1 = (f32[2,128]{1,0:T(2,128)}, f32[2,128]{1,0:T(2,128)}, f32[1,1]{1,0:T(1,128)}, f32[1,1]{1,0:T(1,128)}) custom-call(f32[32,8,128]{2,1,0:T(8,128)S(1)} %all-to-all-done.r_ref, s32[1]{0:T(128)S(6)} %copy.9.len_ref), custom_call_target="tpu_custom_call" | custom-call | tf_op jit(solution)/shard_map/finish/pallas_call | solution.py:288
  (22 shorter events, 1.4 us)
Async XLA Ops:
  0.6 6.0 %collective-permute-start.2 = (bf16[2048,768]{1,0:T(8,128)(2,1)}, bf16[2048,768]{1,0:T(8,128)(2,1)S(1)}, u32[]{:S(2)}, u32[]{:S(2)}) collective-permute-start(bf16[2048,768]{1,0:T(8,128)(2,1)} %refs_3_.1), channel_id=1, source_target_pairs={{0,1},{1,0},{2,3},{3,2},{4,5},{5,4},{6,7},{7,6},{8,9},{9,8},{10,11... | collective-permute-start | bytes 9437192 | tf_op jit(solution)/shard_map/ppermute | solution.py:309
  1.1 0.7 %copy-start.2 = (s32[256]{0:T(256)S(1)}, s32[256]{0:T(256)}, u32[]{:S(2)}) copy-start(s32[256]{0:T(256)} %param.8) | copy-start | bytes 3076
  3.2 9.9 %collective-permute-start = (bf16[64,2176]{1,0:T(8,128)(2,1)S(1)}, bf16[64,2176]{1,0:T(8,128)(2,1)S(1)}, u32[]{:S(2)}, u32[]{:S(2)}) collective-permute-start(bf16[64,2176]{1,0:T(8,128)(2,1)S(1)} %get-tuple-element.25), channel_id=1, source_target_pairs={{0,8},{1,9},{2,10},{3,11},{8,16},{9,17},{10,18},{11,19},{16,24},{1... | collective-permute-start | bytes 835592 | tf_op jit(solution)/shard_map/ppermute | solution.py:309
  5.8 8.8 %collective-permute-start.1 = (bf16[64,2176]{1,0:T(8,128)(2,1)S(1)}, bf16[64,2176]{1,0:T(8,128)(2,1)S(1)}, u32[]{:S(2)}, u32[]{:S(2)}) collective-permute-start(bf16[64,2176]{1,0:T(8,128)(2,1)S(1)} %get-tuple-element.26), channel_id=1, source_target_pairs={{0,4},{1,5},{2,6},{3,7},{8,0},{9,1},{10,2},{11,3},{16,8},{17,9},{1... | collective-permute-start | bytes 835592 | tf_op jit(solution)/shard_map/ppermute | solution.py:309
  6.6 1.9 %copy-start = (bf16[2048,768]{1,0:T(8,128)(2,1)S(1)}, bf16[2048,768]{1,0:T(8,128)(2,1)}, u32[]{:S(2)}) copy-start(bf16[2048,768]{1,0:T(8,128)(2,1)} %refs_3_.1) | copy-start | bytes 9437188
  8.5 18.9 %copy-start.1 = (bf16[2048,768]{1,0:T(8,128)(2,1)S(1)}, bf16[2048,768]{1,0:T(8,128)(2,1)}, u32[]{:S(2)}) copy-start(bf16[2048,768]{1,0:T(8,128)(2,1)} %refs_3_.1) | copy-start | bytes 9437188
  14.6 15.1 %collective-permute-start.3 = (bf16[64,2176]{1,0:T(8,128)(2,1)S(1)}, bf16[64,2176]{1,0:T(8,128)(2,1)S(1)}, u32[]{:S(2)}, u32[]{:S(2)}) collective-permute-start(bf16[64,2176]{1,0:T(8,128)(2,1)S(1)} %collective-permute-done.refs_0_.first_ref), channel_id=1, source_target_pairs={{0,8},{1,9},{2,10},{3,11},{8,16},{9,17},{10,18},{11,19},{16,24},{1... | collective-permute-start | bytes 835592 | tf_op jit(solution)/shard_map/ppermute | solution.py:309
  16.2 13.5 %collective-permute-start.4 = (bf16[64,2176]{1,0:T(8,128)(2,1)S(1)}, bf16[64,2176]{1,0:T(8,128)(2,1)S(1)}, u32[]{:S(2)}, u32[]{:S(2)}) collective-permute-start(bf16[64,2176]{1,0:T(8,128)(2,1)S(1)} %collective-permute-done.1.refs_2_.second_ref), channel_id=1, source_target_pairs={{0,4},{1,5},{2,6},{3,7},{8,0},{9,1},{10,2},{11,3},{16,8},{17,9},{1... | collective-permute-start | bytes 835592 | tf_op jit(solution)/shard_map/ppermute | solution.py:309
  16.7 8.7 %collective-permute-start.5 = (bf16[32,2048]{1,0:T(8,128)(2,1)S(1)}, bf16[32,2048]{1,0:T(8,128)(2,1)S(1)}, u32[]{:S(2)}, u32[]{:S(2)}) collective-permute-start(bf16[32,2048]{1,0:T(8,128)(2,1)S(1)} %get-tuple-element.30), channel_id=1, source_target_pairs={{0,8},{1,9},{2,10},{3,11},{8,16},{9,17},{10,18},{11,19},{16,24},{1... | collective-permute-start | bytes 393224 | tf_op jit(solution)/shard_map/ppermute | solution.py:309
  18.2 8.7 %collective-permute-start.6 = (bf16[32,2048]{1,0:T(8,128)(2,1)S(1)}, bf16[32,2048]{1,0:T(8,128)(2,1)S(1)}, u32[]{:S(2)}, u32[]{:S(2)}) collective-permute-start(bf16[32,2048]{1,0:T(8,128)(2,1)S(1)} %get-tuple-element.31), channel_id=1, source_target_pairs={{0,4},{1,5},{2,6},{3,7},{8,0},{9,1},{10,2},{11,3},{16,8},{17,9},{1... | collective-permute-start | bytes 393224 | tf_op jit(solution)/shard_map/ppermute | solution.py:309
  18.7 15.2 %collective-permute-start.11 = (bf16[64,2176]{1,0:T(8,128)(2,1)S(1)}, bf16[64,2176]{1,0:T(8,128)(2,1)S(1)}, u32[]{:S(2)}, u32[]{:S(2)}) collective-permute-start(bf16[64,2176]{1,0:T(8,128)(2,1)S(1)} %join.3), channel_id=1, source_target_pairs={{0,2},{1,3},{2,0},{3,1},{4,6},{5,7},{6,4},{7,5},{8,10},{9,11},{10,... | collective-permute-start | bytes 835592 | tf_op jit(solution)/shard_map/ppermute | solution.py:309
  25.4 6.4 %collective-permute-start.9 = (bf16[32,2048]{1,0:T(8,128)(2,1)S(1)}, bf16[32,2048]{1,0:T(8,128)(2,1)S(1)}, u32[]{:S(2)}, u32[]{:S(2)}) collective-permute-start(bf16[32,2048]{1,0:T(8,128)(2,1)S(1)} %collective-permute-done.5.refs_1_), channel_id=1, source_target_pairs={{0,8},{1,9},{2,10},{3,11},{8,16},{9,17},{10,18},{11,19},{16,24},{1... | collective-permute-start | bytes 393224 | tf_op jit(solution)/shard_map/ppermute | solution.py:309
  27.0 6.4 %collective-permute-start.10 = (bf16[32,2048]{1,0:T(8,128)(2,1)S(1)}, bf16[32,2048]{1,0:T(8,128)(2,1)S(1)}, u32[]{:S(2)}, u32[]{:S(2)}) collective-permute-start(bf16[32,2048]{1,0:T(8,128)(2,1)S(1)} %collective-permute-done.6.refs_3_), channel_id=1, source_target_pairs={{0,4},{1,5},{2,6},{3,7},{8,0},{9,1},{10,2},{11,3},{16,8},{17,9},{1... | collective-permute-start | bytes 393224 | tf_op jit(solution)/shard_map/ppermute | solution.py:309
  29.7 8.7 %collective-permute-start.7 = (bf16[64,2176]{1,0:T(8,128)(2,1)S(1)}, bf16[64,2176]{1,0:T(8,128)(2,1)S(1)}, u32[]{:S(2)}, u32[]{:S(2)}) collective-permute-start(bf16[64,2176]{1,0:T(8,128)(2,1)S(1)} %collective-permute-done.3.refs_0_.first_ref), channel_id=1, source_target_pairs={{0,8},{1,9},{2,10},{3,11},{8,16},{9,17},{10,18},{11,19},{16,24},{1... | collective-permute-start | bytes 835592 | tf_op jit(solution)/shard_map/ppermute | solution.py:309
  31.3 8.3 %collective-permute-start.8 = (bf16[64,2176]{1,0:T(8,128)(2,1)S(1)}, bf16[64,2176]{1,0:T(8,128)(2,1)S(1)}, u32[]{:S(2)}, u32[]{:S(2)}) collective-permute-start(bf16[64,2176]{1,0:T(8,128)(2,1)S(1)} %collective-permute-done.4.refs_2_.second_ref), channel_id=1, source_target_pairs={{0,4},{1,5},{2,6},{3,7},{8,0},{9,1},{10,2},{11,3},{16,8},{17,9},{1... | collective-permute-start | bytes 835592 | tf_op jit(solution)/shard_map/ppermute | solution.py:309
  31.8 9.9 %collective-permute-start.14 = (bf16[32,2048]{1,0:T(8,128)(2,1)S(1)}, bf16[32,2048]{1,0:T(8,128)(2,1)S(1)}, u32[]{:S(2)}, u32[]{:S(2)}) collective-permute-start(bf16[32,2048]{1,0:T(8,128)(2,1)S(1)} %collective-permute-done.9.refs_1_), channel_id=1, source_target_pairs={{0,8},{1,9},{2,10},{3,11},{8,16},{9,17},{10,18},{11,19},{16,24},{1... | collective-permute-start | bytes 393224 | tf_op jit(solution)/shard_map/ppermute | solution.py:309
  33.4 9.9 %collective-permute-start.15 = (bf16[32,2048]{1,0:T(8,128)(2,1)S(1)}, bf16[32,2048]{1,0:T(8,128)(2,1)S(1)}, u32[]{:S(2)}, u32[]{:S(2)}) collective-permute-start(bf16[32,2048]{1,0:T(8,128)(2,1)S(1)} %collective-permute-done.10.refs_3_), channel_id=1, source_target_pairs={{0,4},{1,5},{2,6},{3,7},{8,0},{9,1},{10,2},{11,3},{16,8},{17,9},{1... | collective-permute-start | bytes 393224 | tf_op jit(solution)/shard_map/ppermute | solution.py:309
  33.9 9.4 %collective-permute-start.16 = (bf16[64,2176]{1,0:T(8,128)(2,1)S(1)}, bf16[64,2176]{1,0:T(8,128)(2,1)S(1)}, u32[]{:S(2)}, u32[]{:S(2)}) collective-permute-start(bf16[64,2176]{1,0:T(8,128)(2,1)S(1)} %join.4), channel_id=1, source_target_pairs={{0,2},{1,3},{2,0},{3,1},{4,6},{5,7},{6,4},{7,5},{8,10},{9,11},{10,... | collective-permute-start | bytes 835592 | tf_op jit(solution)/shard_map/ppermute | solution.py:309
  39.6 6.6 %collective-permute-start.12 = (bf16[64,2176]{1,0:T(8,128)(2,1)S(1)}, bf16[64,2176]{1,0:T(8,128)(2,1)S(1)}, u32[]{:S(2)}, u32[]{:S(2)}) collective-permute-start(bf16[64,2176]{1,0:T(8,128)(2,1)S(1)} %collective-permute-done.7.refs_0_.first_ref), channel_id=1, source_target_pairs={{0,8},{1,9},{2,10},{3,11},{8,16},{9,17},{10,18},{11,19},{16,24},{1... | collective-permute-start | bytes 835592 | tf_op jit(solution)/shard_map/ppermute | solution.py:309
  41.3 6.5 %collective-permute-start.13 = (bf16[64,2176]{1,0:T(8,128)(2,1)S(1)}, bf16[64,2176]{1,0:T(8,128)(2,1)S(1)}, u32[]{:S(2)}, u32[]{:S(2)}) collective-permute-start(bf16[64,2176]{1,0:T(8,128)(2,1)S(1)} %collective-permute-done.8.refs_2_.second_ref), channel_id=1, source_target_pairs={{0,4},{1,5},{2,6},{3,7},{8,0},{9,1},{10,2},{11,3},{16,8},{17,9},{1... | collective-permute-start | bytes 835592 | tf_op jit(solution)/shard_map/ppermute | solution.py:309
  41.7 6.6 %collective-permute-start.17 = (bf16[64,2176]{1,0:T(8,128)(2,1)S(1)}, bf16[64,2176]{1,0:T(8,128)(2,1)S(1)}, u32[]{:S(2)}, u32[]{:S(2)}) collective-permute-start(bf16[64,2176]{1,0:T(8,128)(2,1)S(1)} %join.5), channel_id=1, source_target_pairs={{0,2},{1,3},{2,0},{3,1},{4,6},{5,7},{6,4},{7,5},{8,10},{9,11},{10,... | collective-permute-start | bytes 835592 | tf_op jit(solution)/shard_map/ppermute | solution.py:309
  51.4 13.0 %all-to-all-start = ((f32[32,8,128]{2,1,0:T(8,128)}), f32[32,8,128]{2,1,0:T(8,128)S(1)}, u32[]{:S(2)}, u32[]{:S(2)}) async-start(f32[32,8,128]{2,1,0:T(8,128)} %stats_last.1), calls=%async_computation | async-start | bytes 262144 | tf_op jit(solution)/shard_map/all_to_all | solution.py:342

commit v3 on v2

--- a/solution.py
+++ b/solution.py
@@ -46,15 +46,15 @@
     return (0, g, rows // 2, rows - g), (g, b_rows, b_rows, g)
 
 
-def digits(target, first):
-    lane = lax.broadcasted_iota(jnp.int32, (1, LANES), 1) - first
+def digits(target):
+    lane = lax.broadcasted_iota(jnp.int32, (1, LANES), 1)
     shift = jnp.where(lane == 0, 2 * DIGIT_BITS, jnp.where(lane == 1, DIGIT_BITS, 0))
     digit = (target >> shift) & ((1 << DIGIT_BITS) - 1)
-    return jnp.where((lane >= 0) & (lane < 3), digit, 0)
-
-
-def undigits(ext, first):
-    lane = lax.broadcasted_iota(jnp.int32, (1, LANES), 1) - first
+    return jnp.where(lane < 3, digit, 0).astype(jnp.float32).astype(jnp.bfloat16)
+
+
+def undigits(ext):
+    lane = lax.broadcasted_iota(jnp.int32, (1, LANES), 1)
     base = float(1 << DIGIT_BITS)
     weight = jnp.where(
         lane == 0, base * base, jnp.where(lane == 1, base, jnp.where(lane == 2, 1.0, 0.0))
@@ -63,8 +63,7 @@
 
 
 def norm_kernel(
-    b_rows, x_hbm, gain_hbm, tid_ref, xn_ref, acw_ref, bcw_ref, accw_ref, bccw_ref,
-    x_ref, gain_ref, ext_ref, sems,
+    b_rows, x_hbm, gain_hbm, tid_hbm, xn_ref, cw_ref, ccw_ref, x_ref, gain_ref, tid_ref, sems
 ):
     rows, d = x_ref.shape
     tp = lax.axis_index("tp")
@@ -72,87 +71,69 @@
     mine = pl.ds(pl.multiple_of(core * rows, rows), rows)
     get_x = pltpu.make_async_copy(x_hbm.at[mine, :], x_ref, sems.at[0])
     get_gain = pltpu.make_async_copy(gain_hbm, gain_ref, sems.at[1])
+    get_tid = pltpu.make_async_copy(tid_hbm, tid_ref, sems.at[2])
     get_x.start()
     get_gain.start()
+    get_tid.start()
+    get_tid.wait()
     target = jnp.where(core == 0, tid_ref[0:1, :], tid_ref[1:2, :])
-    target = jnp.broadcast_to(target, (8, rows)).T[:, :1]
-    ext = digits(target, 0)
-    ext_ref[0] = ext
-    ext_ref[1] = digits(target, 3)
-    xn_ref[:, d:] = ext.astype(jnp.float32).astype(jnp.bfloat16)
+    xn_ref[:, d:] = digits(jnp.broadcast_to(target, (8, rows)).T[:, :1])
+    get_gain.wait()
     get_x.wait()
-    get_gain.wait()
     feats = x_ref[...].astype(jnp.float32)
     scale = lax.rsqrt(jnp.mean(feats * feats, axis=-1, keepdims=True) + 1e-06)
     xn_ref[:, :d] = (feats * scale * gain_ref[...]).astype(jnp.bfloat16)
     starts, sizes = block_starts(rows, b_rows)
-    for a_ref, b_ref, flip in ((acw_ref, bcw_ref, 0), (accw_ref, bccw_ref, 1)):
+    for ref, flip in ((cw_ref, 0), (ccw_ref, 1)):
         down = plane != flip
-        place = [
-            pl.ds(pl.multiple_of(jnp.where(down, starts[3 - j], starts[j]), 16), sizes[j])
-            for j in range(3)
-        ]
         at = 0
-        for j in range(2):
-            here = pl.ds(at, sizes[j])
-            a_ref[here, :d] = xn_ref[place[j], :d]
-            own = ext_ref[0, place[j], :]
-            if at < b_rows:
-                part = min(b_rows - at, sizes[j])
-                beside = pl.ds(pl.multiple_of(place[2].start + at, 16), part)
-                a_ref[pl.ds(at, part), d:] = (
-                    (own[:part] + ext_ref[1, beside, :]).astype(jnp.float32).astype(jnp.bfloat16)
-                )
-                if part < sizes[j]:
-                    a_ref[pl.ds(at + part, sizes[j] - part), d:] = (
-                        own[part:].astype(jnp.float32).astype(jnp.bfloat16)
-                    )
-            else:
-                a_ref[here, d:] = own.astype(jnp.float32).astype(jnp.bfloat16)
+        for j in range(3):
+            start = pl.multiple_of(jnp.where(down, starts[3 - j], starts[j]), 16)
+            ref[pl.ds(at, sizes[j]), :] = xn_ref[pl.ds(start, sizes[j]), :]
             at += sizes[j]
-        b_ref[...] = xn_ref[place[2], :d]
 
 
 def norm_rows(hidden, norm_gain, target_ids, rows, b_rows):
     d = hidden.shape[1]
-    a, wide = rows // 2, d + LANES
-    shapes = [(rows, wide), (a, wide), (b_rows, d), (a, wide), (b_rows, d)]
+    wide = d + LANES
+    shapes = [(rows, wide), (rows // 2 + b_rows, wide), (rows // 2 + b_rows, wide)]
+    hbm_operands = (hidden, norm_gain.reshape(1, d), target_ids.reshape(2, rows))
     return pl.pallas_call(
         functools.partial(norm_kernel, b_rows),
         out_shape=[jax.ShapeDtypeStruct(s, jnp.bfloat16) for s in shapes],
-        in_specs=[pl.BlockSpec(memory_space=pl.ANY)] * 2 + [pl.BlockSpec(memory_space=pltpu.VMEM)],
+        in_specs=[pl.BlockSpec(memory_space=pl.ANY)] * 3,
         scratch_shapes=[
             pltpu.VMEM((rows, d), jnp.bfloat16),
             pltpu.VMEM((1, d), jnp.float32),
-            pltpu.VMEM((2, rows, LANES), jnp.int32),
-            pltpu.SemaphoreType.DMA((2,)),
+            pltpu.VMEM((2, rows), jnp.int32),
+            pltpu.SemaphoreType.DMA((3,)),
         ],
         compiler_params=pltpu.CompilerParams(vmem_limit_bytes=VMEM_BYTES),
         name="norm",
-    )(
-        pltpu.with_memory_space_constraint(hidden, pltpu.HBM),
-        pltpu.with_memory_space_constraint(norm_gain.reshape(1, d), pltpu.HBM),
-        target_ids.reshape(2, rows),
-    )
-
-
-def join_kernel(first_ref, second_ref, out_ref):
-    half = out_ref.shape[0] // 2
-    out_ref[:half, :] = first_ref[:half, :]
-    out_ref[half:, :] = second_ref[:half, :]
-
-
-def join_heads(first, second, count):
+    )(*(pltpu.with_memory_space_constraint(v, pltpu.HBM) for v in hbm_operands))
+
+
+def join_kernel(first_ref, second_ref, joined_ref, *head_refs):
+    half = joined_ref.shape[0] // 2
+    joined_ref[:half, :] = first_ref[:half, :]
+    joined_ref[half:, :] = second_ref[:half, :]
+    for ref, head_ref in zip((first_ref, second_ref), head_refs):
+        head_ref[...] = ref[: head_ref.shape[0], :]
+
+
+def join_heads(first, second, count, head_count=0):
+    wide = first.shape[1]
+    shapes = [(2 * count, wide)] + [(head_count, wide)] * (2 if head_count else 0)
     return pl.pallas_call(
         join_kernel,
-        out_shape=jax.ShapeDtypeStruct((2 * count, first.shape[1]), first.dtype),
+        out_shape=[jax.ShapeDtypeStruct(s, first.dtype) for s in shapes],
         compiler_params=pltpu.CompilerParams(vmem_limit_bytes=VMEM_BYTES),
         name="join",
     )(first, second)
 
 
 def piece_segments(part):
-    return {"all": (0, 1, 2, 3), "a": (0, 1), "b": (2,), "y": (3,)}[part]
+    return {"all": (0, 1, 2, 3), "most": (0, 1, 2), "half": (0, 1), "y": (3,)}[part]
 
 
 def stats_kernel(metas, n_req, n_tp, b_rows, rows, earlier, tail, *refs):
@@ -171,11 +152,7 @@
     for parts, ref in zip(metas, piece_refs):
         here = pl.ds(at, ref.shape[0])
         x_s[here, :] = ref[:, :d]
-        if parts[0][2] == "b":
-            t_s[here, :] = undigits(before[: ref.shape[0], d:], 3)
-        else:
-            t_s[here, :] = undigits(ref[:, d:], 0)
-        before = ref
+        t_s[here, :] = undigits(ref[:, d:])
         at += ref.shape[0]
 
     x = x_s[...]
@@ -302,36 +279,32 @@
 def per_device(n_req, n_tp, hidden_states, norm_gain, head, target_ids, lengths):
     rows = hidden_states.shape[0] // 2
     b_rows = rows // 4
-    cw, ccw = ring_pairs(n_req, n_tp, 1), ring_pairs(n_req, n_tp, -1)
+    cw_pairs, ccw_pairs = ring_pairs(n_req, n_tp, 1), ring_pairs(n_req, n_tp, -1)
     other_core, other_y = tp_pairs(n_req, n_tp, 1), tp_pairs(n_req, n_tp, 2)
 
     def send(value, pairs):
         return lax.ppermute(value, AXES, pairs)
 
     other_head = send(head, other_core)
-    xn, a_cw, b_cw, a_ccw, b_ccw = norm_rows(hidden_states, norm_gain, target_ids, rows, b_rows)
+    xn, to_cw, to_ccw = norm_rows(hidden_states, norm_gain, target_ids, rows, b_rows)
     sizes = (n_req, n_tp, b_rows, rows)
     g = rows // 2 - b_rows
     meta = (((0, 0, "all"),),)
     metas = [meta]
     stats = [stats_of([xn], meta, head, other_head, *sizes)]
-    y_piece = None
     for hops in range(1, n_req // 2 + 1):
         last = 2 * hops == n_req
-        a_cw, a_ccw = send(a_cw, cw), send(a_ccw, ccw)
-        if not last:
-            b_cw, b_ccw = send(b_cw, cw), send(b_ccw, ccw)
+        cw, ccw = send(to_cw, cw_pairs), send(to_ccw, ccw_pairs)
         if hops > 1:
             y_next = send(y_message, other_y)
             stats.append(stats_of(pieces, meta, head, other_head, *sizes))
             metas.append(meta)
-        a_cw, a_ccw, stats[-1] = lax.optimization_barrier((a_cw, a_ccw, stats[-1]))
-        if last:
-            pieces, meta = [a_cw, a_ccw], [((1, hops, "a"),), ((-1, hops, "a"),)]
-        else:
-            y_message = join_heads(a_cw, a_ccw, g)
-            pieces = [a_cw, b_cw, a_ccw, b_ccw]
-            meta = [((1, hops, "a"),), ((1, hops, "b"),), ((-1, hops, "a"),), ((-1, hops, "b"),)]
+        cw, ccw, stats[-1] = lax.optimization_barrier((cw, ccw, stats[-1]))
+        part = "half" if last else "most"
+        pieces, meta = [cw, ccw], [((1, hops, part),), ((-1, hops, part),)]
+        if not last:
+            y_message, *heads = join_heads(cw, ccw, g, rows // 2 if 2 * hops + 2 == n_req else 0)
+            to_cw, to_ccw = heads or (cw, ccw)
         if hops > 1:
             pieces.append(y_next)
             meta.append(((1, hops - 1, "y"), (-1, hops - 1, "y")))

time: 65.4 us -> 64.1 us (0.980)
  starting transfers between devices: 24.9 us -> 17 us
  waiting for transfers between devices: 21.3 us -> 28.5 us
  local copies, waits for them, and re-layouts: 2.57 us -> 1.89 us
    ppermute x18 -> x12, waiting for transfers between devices: 13.7 us -> 20.9 us  [send(): return lax.ppermute(value, AXES, pairs)]
    ppermute x18 -> x12, starting transfers between devices: 20.1 us -> 14 us  [send(): return lax.ppermute(value, AXES, pairs)]
    all_to_all x1, starting transfers between devices: 4.8 us -> 3.01 us  [per_device(): received = lax.all_to_all(packed, AXES, 0, 0, tiled=True)]
    unnamed x6 -> x4, local copies, waits for them, and re-layouts: 2.57 us -> 1.89 us
  transfers between devices with their start and end apart: 19 -> 13, of which waited for: 8 -> 10; matrix products, arithmetic and copies ran while one was open for 0% -> 0% of each run, Pallas kernels for 17% -> 18%
where the time goes in v3:
time: 64.1 us; the launch traced here: 63.9 us
  waiting for transfers between devices  28.5 us (44%)
  starting transfers between devices  17 us (27%)
  Pallas kernels  15.1 us (24%)
  local copies, waits for them, and re-layouts  1.89 us (3%)
  between operations  1.32 us (2%)
    ppermute x12, waiting for transfers between devices, send(): return lax.ppermute(value, AXES, pairs)  20.9 us
    ppermute x12, starting transfers between devices, send(): return lax.ppermute(value, AXES, pairs)  14 us
    pallas_call x5, Pallas kernels, stats_of(): pl.pallas_call(functools.partial(stats_kernel, metas, n_req, n_tp, b_rows...  12.9 us
    all_to_all x1, waiting for transfers between devices, per_device(): received = lax.all_to_all(packed, AXES, 0, 0, tiled=True)  7.58 us
    all_to_all x1, starting transfers between devices, per_device(): received = lax.all_to_all(packed, AXES, 0, 0, tiled=True)  3.01 us
    unnamed x4, local copies, waits for them, and re-layouts  1.89 us
    pallas_call x1, Pallas kernels, norm_rows(): pl.pallas_call(functools.partial(norm_kernel, b_rows), out_shape=[jax.Sha...  1.41 us
  transfers between devices with their start and end apart: 13, of which 10 were waited for; matrix products, arithmetic and copies ran while one was open for 0% of the time, Pallas kernels for 18%

profile of v3, /device:TPU:0, one launch (start us, length us, event | category | flops | bytes accessed | tf_op | source)
XLA Modules:
  0.0 63.9 jit_solution(3648161444463213276)
XLA Ops:
  0.6 0.5 collective-permute-start.2
  1.1 1.4 %norm.1 = (bf16[128,2176]{1,0:T(8,128)(2,1)S(1)}, bf16[96,2176]{1,0:T(8,128)(2,1)S(1)}, bf16[96,2176]{1,0:T(8,128)(2,1)S(1)}) custom-call(bf16[256,2048]{1,0:T(8,128)(2,1)} %x_hbm.1, f32[1,2048]{1,0:T(1,128)} %bitcast.6, s32[2,128]{1,0:T(2,128)} %bitcast.7), custom_call_target="tpu_custom_call" | custom-call | tf_op jit(solution)/shard_map/norm/pallas_call | solution.py:101
  2.6 2.7 %collective-permute-start = (bf16[96,2176]{1,0:T(8,128)(2,1)S(1)}, bf16[96,2176]{1,0:T(8,128)(2,1)S(1)}, u32[]{:S(2)}, u32[]{:S(2)}) collective-permute-start(bf16[96,2176]{1,0:T(8,128)(2,1)S(1)} %get-tuple-element.26), channel_id=1, source_target_pairs={{0,8},{1,9},{2,10},{3,11},{8,16},{9,17},{10,18},{11,19},{16,24},{1... | collective-permute-start | bytes 1253384 | tf_op jit(solution)/shard_map/ppermute | solution.py:286
  5.2 1.4 %collective-permute-done.2.refs_2_.refs_3_.refs_4_ = bf16[2048,768]{1,0:T(8,128)(2,1)S(1)} collective-permute-done((bf16[2048,768]{1,0:T(8,128)(2,1)}, bf16[2048,768]{1,0:T(8,128)(2,1)S(1)}, u32[]{:S(2)}, u32[]{:S(2)}) %collective-permute-start.2) | collective-permute-done | bytes 3145760 | tf_op jit(solution)/shard_map/ppermute | solution.py:286
  6.6 1.9 %copy-done = bf16[2048,768]{1,0:T(8,128)(2,1)S(1)} copy-done((bf16[2048,768]{1,0:T(8,128)(2,1)S(1)}, bf16[2048,768]{1,0:T(8,128)(2,1)}, u32[]{:S(2)}) %copy-start) | copy-done | bytes 3145752
  8.5 1.6 %stats.4.refs_5_ = f32[128,128]{1,0:T(8,128)S(1)} custom-call(bf16[128,2176]{1,0:T(8,128)(2,1)S(1)} %get-tuple-element.28.refs_0_, bf16[2048,768]{1,0:T(8,128)(2,1)S(1)} %copy-done, bf16[2048,768]{1,0:T(8,128)(2,1)S(1)} %collective-permute-done.2.refs_2_.refs_3_.refs_4_), custom_call_target="tpu_custom_call" | custom-call | flops 805306368 | bytes 6291456 | tf_op jit(solution)/shard_map/stats/pallas_call | solution.py:221
  10.1 5.3 %collective-permute-done.refs_0_.first_ref = bf16[96,2176]{1,0:T(8,128)(2,1)S(1)} collective-permute-done((bf16[96,2176]{1,0:T(8,128)(2,1)S(1)}, bf16[96,2176]{1,0:T(8,128)(2,1)S(1)}, u32[]{:S(2)}, u32[]{:S(2)}) %collective-permute-start) | collective-permute-done | bytes 417824 | tf_op jit(solution)/shard_map/ppermute | solution.py:286
  15.4 1.5 %collective-permute-done.1.refs_1_.second_ref = bf16[96,2176]{1,0:T(8,128)(2,1)S(1)} collective-permute-done((bf16[96,2176]{1,0:T(8,128)(2,1)S(1)}, bf16[96,2176]{1,0:T(8,128)(2,1)S(1)}, u32[]{:S(2)}, u32[]{:S(2)}) %collective-permute-start.1) | collective-permute-done | bytes 417824 | tf_op jit(solution)/shard_map/ppermute | solution.py:286
  16.9 1.6 %collective-permute-start.3 = (bf16[96,2176]{1,0:T(8,128)(2,1)S(1)}, bf16[96,2176]{1,0:T(8,128)(2,1)S(1)}, u32[]{:S(2)}, u32[]{:S(2)}) collective-permute-start(bf16[96,2176]{1,0:T(8,128)(2,1)S(1)} %collective-permute-done.refs_0_.first_ref), channel_id=1, source_target_pairs={{0,8},{1,9},{2,10},{3,11},{8,16},{9,17},{10,18},{11,19},{16,24},{1... | collective-permute-start | bytes 1253384 | tf_op jit(solution)/shard_map/ppermute | solution.py:286
  18.5 0.4 collective-permute-start.4
  19.0 1.6 %collective-permute-start.7 = (bf16[64,2176]{1,0:T(8,128)(2,1)S(1)}, bf16[64,2176]{1,0:T(8,128)(2,1)S(1)}, u32[]{:S(2)}, u32[]{:S(2)}) collective-permute-start(bf16[64,2176]{1,0:T(8,128)(2,1)S(1)} %join.3), channel_id=1, source_target_pairs={{0,2},{1,3},{2,0},{3,1},{4,6},{5,7},{6,4},{7,5},{8,10},{9,11},{10,... | collective-permute-start | bytes 835592 | tf_op jit(solution)/shard_map/ppermute | solution.py:286
  20.6 2.3 %stats.5.refs_6_ = f32[192,128]{1,0:T(8,128)S(1)} custom-call(bf16[96,2176]{1,0:T(8,128)(2,1)S(1)} %collective-permute-done.refs_0_.first_ref, bf16[96,2176]{1,0:T(8,128)(2,1)S(1)} %collective-permute-done.1.refs_1_.second_ref, bf16[2048,768]{1,0:T(8,128)(2,1)S(1)} %copy-done.1, bf16[2048,768]{1,0:T(8,128)(2,1)S(1)} %collective-permute-done.2.refs_2_.refs_3_.refs_4_), custom_call_target="tpu_custom_call" | custom-call | flops 1207959552 | bytes 6291456 | tf_op jit(solution)/shard_map/stats/pallas_call | solution.py:221
  22.8 5.0 %collective-permute-done.3.refs_0_.first_ref = bf16[96,2176]{1,0:T(8,128)(2,1)S(1)} collective-permute-done((bf16[96,2176]{1,0:T(8,128)(2,1)S(1)}, bf16[96,2176]{1,0:T(8,128)(2,1)S(1)}, u32[]{:S(2)}, u32[]{:S(2)}) %collective-permute-start.3) | collective-permute-done | bytes 417824 | tf_op jit(solution)/shard_map/ppermute | solution.py:286
  27.8 1.3 %collective-permute-done.4.refs_1_.second_ref = bf16[96,2176]{1,0:T(8,128)(2,1)S(1)} collective-permute-done((bf16[96,2176]{1,0:T(8,128)(2,1)S(1)}, bf16[96,2176]{1,0:T(8,128)(2,1)S(1)}, u32[]{:S(2)}, u32[]{:S(2)}) %collective-permute-start.4) | collective-permute-done | bytes 417824 | tf_op jit(solution)/shard_map/ppermute | solution.py:286
  29.1 1.6 %collective-permute-start.5 = (bf16[96,2176]{1,0:T(8,128)(2,1)S(1)}, bf16[96,2176]{1,0:T(8,128)(2,1)S(1)}, u32[]{:S(2)}, u32[]{:S(2)}) collective-permute-start(bf16[96,2176]{1,0:T(8,128)(2,1)S(1)} %collective-permute-done.3.refs_0_.first_ref), channel_id=1, source_target_pairs={{0,8},{1,9},{2,10},{3,11},{8,16},{9,17},{10,18},{11,19},{16,24},{1... | collective-permute-start | bytes 1253384 | tf_op jit(solution)/shard_map/ppermute | solution.py:286
  30.7 0.4 collective-permute-start.6
  31.2 1.6 %collective-permute-start.10 = (bf16[64,2176]{1,0:T(8,128)(2,1)S(1)}, bf16[64,2176]{1,0:T(8,128)(2,1)S(1)}, u32[]{:S(2)}, u32[]{:S(2)}) collective-permute-start(bf16[64,2176]{1,0:T(8,128)(2,1)S(1)} %join.5), channel_id=1, source_target_pairs={{0,2},{1,3},{2,0},{3,1},{4,6},{5,7},{6,4},{7,5},{8,10},{9,11},{10,... | collective-permute-start | bytes 835592 | tf_op jit(solution)/shard_map/ppermute | solution.py:286
  32.8 3.0 %stats.6.refs_7_ = f32[256,128]{1,0:T(8,128)S(1)} custom-call(bf16[96,2176]{1,0:T(8,128)(2,1)S(1)} %collective-permute-done.3.refs_0_.first_ref, bf16[96,2176]{1,0:T(8,128)(2,1)S(1)} %collective-permute-done.4.refs_1_.second_ref, bf16[64,2176]{1,0:T(8,128)(2,1)S(1)} %collective-permute-done.7.refs_2_, bf16[2048,768]{1,0:T(8,128)(2,1)S(1)} %copy-done.1, ...), custom_call_target="tpu_custom_call" | custom-call | flops 1610612736 | bytes 6291456 | tf_op jit(solution)/shard_map/stats/pallas_call | solution.py:221
  35.7 3.1 %collective-permute-done.5.first_ref.refs_0_ = bf16[96,2176]{1,0:T(8,128)(2,1)S(1)} collective-permute-done((bf16[96,2176]{1,0:T(8,128)(2,1)S(1)}, bf16[96,2176]{1,0:T(8,128)(2,1)S(1)}, u32[]{:S(2)}, u32[]{:S(2)}) %collective-permute-start.5) | collective-permute-done | bytes 417824 | tf_op jit(solution)/shard_map/ppermute | solution.py:286
  38.8 1.3 %collective-permute-done.6.second_ref.refs_1_ = bf16[96,2176]{1,0:T(8,128)(2,1)S(1)} collective-permute-done((bf16[96,2176]{1,0:T(8,128)(2,1)S(1)}, bf16[96,2176]{1,0:T(8,128)(2,1)S(1)}, u32[]{:S(2)}, u32[]{:S(2)}) %collective-permute-start.6) | collective-permute-done | bytes 417824 | tf_op jit(solution)/shard_map/ppermute | solution.py:286
  40.1 0.1 join.4
  40.2 1.5 %collective-permute-start.8 = (bf16[64,2176]{1,0:T(8,128)(2,1)S(1)}, bf16[64,2176]{1,0:T(8,128)(2,1)S(1)}, u32[]{:S(2)}, u32[]{:S(2)}) collective-permute-start(bf16[64,2176]{1,0:T(8,128)(2,1)S(1)} %get-tuple-element.35), channel_id=1, source_target_pairs={{0,8},{1,9},{2,10},{3,11},{8,16},{9,17},{10,18},{11,19},{16,24},{1... | collective-permute-start | bytes 835592 | tf_op jit(solution)/shard_map/ppermute | solution.py:286
  41.7 0.5 collective-permute-start.9
  42.2 1.5 %collective-permute-start.11 = (bf16[64,2176]{1,0:T(8,128)(2,1)S(1)}, bf16[64,2176]{1,0:T(8,128)(2,1)S(1)}, u32[]{:S(2)}, u32[]{:S(2)}) collective-permute-start(bf16[64,2176]{1,0:T(8,128)(2,1)S(1)} %get-tuple-element.39), channel_id=1, source_target_pairs={{0,2},{1,3},{2,0},{3,1},{4,6},{5,7},{6,4},{7,5},{8,10},{9,11},{10,... | collective-permute-start | bytes 835592 | tf_op jit(solution)/shard_map/ppermute | solution.py:286
  43.8 3.0 %stats.7.refs_8_ = f32[256,128]{1,0:T(8,128)S(1)} custom-call(bf16[96,2176]{1,0:T(8,128)(2,1)S(1)} %collective-permute-done.5.first_ref.refs_0_, bf16[96,2176]{1,0:T(8,128)(2,1)S(1)} %collective-permute-done.6.second_ref.refs_1_, bf16[64,2176]{1,0:T(8,128)(2,1)S(1)} %collective-permute-done.10.refs_2_, bf16[2048,768]{1,0:T(8,128)(2,1)S(1)} %copy-done.1, ...), custom_call_target="tpu_custom_call" | custom-call | flops 1610612736 | bytes 6291456 | tf_op jit(solution)/shard_map/stats/pallas_call | solution.py:221
  46.7 0.0 collective-permute-done.8.refs_0_
  46.8 1.5 %collective-permute-done.9.refs_1_ = bf16[64,2176]{1,0:T(8,128)(2,1)S(1)} collective-permute-done((bf16[64,2176]{1,0:T(8,128)(2,1)S(1)}, bf16[64,2176]{1,0:T(8,128)(2,1)S(1)}, u32[]{:S(2)}, u32[]{:S(2)}) %collective-permute-start.9) | collective-permute-done | bytes 278560 | tf_op jit(solution)/shard_map/ppermute | solution.py:286
  48.2 0.5 collective-permute-done.11.refs_2_
  48.8 3.1 %stats_last.1 = f32[32,8,128]{2,1,0:T(8,128)} custom-call(bf16[64,2176]{1,0:T(8,128)(2,1)S(1)} %collective-permute-done.8.refs_0_, bf16[64,2176]{1,0:T(8,128)(2,1)S(1)} %collective-permute-done.9.refs_1_, bf16[64,2176]{1,0:T(8,128)(2,1)S(1)} %collective-permute-done.11.refs_2_, bf16[2048,768]{1,0:T(8,128)(2,1)S(1)} %copy-done.1, ...), custom_call_target="tpu_custom_call" | custom-call | flops 1207959552 | bytes 6291456 | tf_op jit(solution)/shard_map/stats_last/pallas_call | solution.py:221
  51.9 3.0 %all-to-all-start = ((f32[32,8,128]{2,1,0:T(8,128)}), f32[32,8,128]{2,1,0:T(8,128)S(1)}, u32[]{:S(2)}, u32[]{:S(2)}) async-start(f32[32,8,128]{2,1,0:T(8,128)} %stats_last.1), calls=%async_computation | async-start | bytes 262144 | tf_op jit(solution)/shard_map/all_to_all | solution.py:315
  55.6 7.6 %all-to-all-done.r_ref = f32[32,8,128]{2,1,0:T(8,128)S(1)} async-done(((f32[32,8,128]{2,1,0:T(8,128)}), f32[32,8,128]{2,1,0:T(8,128)S(1)}, u32[]{:S(2)}, u32[]{:S(2)}) %all-to-all-start) | async-done | bytes 131104 | tf_op jit(solution)/shard_map/all_to_all | solution.py:315
  63.2 0.7 %finish.1 = (f32[2,128]{1,0:T(2,128)}, f32[2,128]{1,0:T(2,128)}, f32[1,1]{1,0:T(1,128)}, f32[1,1]{1,0:T(1,128)}) custom-call(f32[32,8,128]{2,1,0:T(8,128)S(1)} %all-to-all-done.r_ref, s32[1]{0:T(128)S(6)} %copy.9.len_ref), custom_call_target="tpu_custom_call" | custom-call | tf_op jit(solution)/shard_map/finish/pallas_call | solution.py:265
  (8 shorter events, 0.1 us)
Async XLA Ops:
  0.6 6.0 %collective-permute-start.2 = (bf16[2048,768]{1,0:T(8,128)(2,1)}, bf16[2048,768]{1,0:T(8,128)(2,1)S(1)}, u32[]{:S(2)}, u32[]{:S(2)}) collective-permute-start(bf16[2048,768]{1,0:T(8,128)(2,1)} %refs_3_.5), channel_id=1, source_target_pairs={{0,1},{1,0},{2,3},{3,2},{4,5},{5,4},{6,7},{7,6},{8,9},{9,8},{10,11... | collective-permute-start | bytes 9437192 | tf_op jit(solution)/shard_map/ppermute | solution.py:286
  2.6 12.8 %collective-permute-start = (bf16[96,2176]{1,0:T(8,128)(2,1)S(1)}, bf16[96,2176]{1,0:T(8,128)(2,1)S(1)}, u32[]{:S(2)}, u32[]{:S(2)}) collective-permute-start(bf16[96,2176]{1,0:T(8,128)(2,1)S(1)} %get-tuple-element.26), channel_id=1, source_target_pairs={{0,8},{1,9},{2,10},{3,11},{8,16},{9,17},{10,18},{11,19},{16,24},{1... | collective-permute-start | bytes 1253384 | tf_op jit(solution)/shard_map/ppermute | solution.py:286
  5.2 11.7 %collective-permute-start.1 = (bf16[96,2176]{1,0:T(8,128)(2,1)S(1)}, bf16[96,2176]{1,0:T(8,128)(2,1)S(1)}, u32[]{:S(2)}, u32[]{:S(2)}) collective-permute-start(bf16[96,2176]{1,0:T(8,128)(2,1)S(1)} %get-tuple-element.27), channel_id=1, source_target_pairs={{0,4},{1,5},{2,6},{3,7},{8,0},{9,1},{10,2},{11,3},{16,8},{17,9},{1... | collective-permute-start | bytes 1253384 | tf_op jit(solution)/shard_map/ppermute | solution.py:286
  6.6 1.9 %copy-start = (bf16[2048,768]{1,0:T(8,128)(2,1)S(1)}, bf16[2048,768]{1,0:T(8,128)(2,1)}, u32[]{:S(2)}) copy-start(bf16[2048,768]{1,0:T(8,128)(2,1)} %refs_3_.5) | copy-start | bytes 9437188
  8.5 12.0 %copy-start.1 = (bf16[2048,768]{1,0:T(8,128)(2,1)S(1)}, bf16[2048,768]{1,0:T(8,128)(2,1)}, u32[]{:S(2)}) copy-start(bf16[2048,768]{1,0:T(8,128)(2,1)} %refs_3_.5) | copy-start | bytes 9437188
  16.9 10.9 %collective-permute-start.3 = (bf16[96,2176]{1,0:T(8,128)(2,1)S(1)}, bf16[96,2176]{1,0:T(8,128)(2,1)S(1)}, u32[]{:S(2)}, u32[]{:S(2)}) collective-permute-start(bf16[96,2176]{1,0:T(8,128)(2,1)S(1)} %collective-permute-done.refs_0_.first_ref), channel_id=1, source_target_pairs={{0,8},{1,9},{2,10},{3,11},{8,16},{9,17},{10,18},{11,19},{16,24},{1... | collective-permute-start | bytes 1253384 | tf_op jit(solution)/shard_map/ppermute | solution.py:286
  18.5 10.6 %collective-permute-start.4 = (bf16[96,2176]{1,0:T(8,128)(2,1)S(1)}, bf16[96,2176]{1,0:T(8,128)(2,1)S(1)}, u32[]{:S(2)}, u32[]{:S(2)}) collective-permute-start(bf16[96,2176]{1,0:T(8,128)(2,1)S(1)} %collective-permute-done.1.refs_1_.second_ref), channel_id=1, source_target_pairs={{0,4},{1,5},{2,6},{3,7},{8,0},{9,1},{10,2},{11,3},{16,8},{17,9},{1... | collective-permute-start | bytes 1253384 | tf_op jit(solution)/shard_map/ppermute | solution.py:286
  19.0 13.8 %collective-permute-start.7 = (bf16[64,2176]{1,0:T(8,128)(2,1)S(1)}, bf16[64,2176]{1,0:T(8,128)(2,1)S(1)}, u32[]{:S(2)}, u32[]{:S(2)}) collective-permute-start(bf16[64,2176]{1,0:T(8,128)(2,1)S(1)} %join.3), channel_id=1, source_target_pairs={{0,2},{1,3},{2,0},{3,1},{4,6},{5,7},{6,4},{7,5},{8,10},{9,11},{10,... | collective-permute-start | bytes 835592 | tf_op jit(solution)/shard_map/ppermute | solution.py:286
  29.1 9.7 %collective-permute-start.5 = (bf16[96,2176]{1,0:T(8,128)(2,1)S(1)}, bf16[96,2176]{1,0:T(8,128)(2,1)S(1)}, u32[]{:S(2)}, u32[]{:S(2)}) collective-permute-start(bf16[96,2176]{1,0:T(8,128)(2,1)S(1)} %collective-permute-done.3.refs_0_.first_ref), channel_id=1, source_target_pairs={{0,8},{1,9},{2,10},{3,11},{8,16},{9,17},{10,18},{11,19},{16,24},{1... | collective-permute-start | bytes 1253384 | tf_op jit(solution)/shard_map/ppermute | solution.py:286
  30.7 9.4 %collective-permute-start.6 = (bf16[96,2176]{1,0:T(8,128)(2,1)S(1)}, bf16[96,2176]{1,0:T(8,128)(2,1)S(1)}, u32[]{:S(2)}, u32[]{:S(2)}) collective-permute-start(bf16[96,2176]{1,0:T(8,128)(2,1)S(1)} %collective-permute-done.4.refs_1_.second_ref), channel_id=1, source_target_pairs={{0,4},{1,5},{2,6},{3,7},{8,0},{9,1},{10,2},{11,3},{16,8},{17,9},{1... | collective-permute-start | bytes 1253384 | tf_op jit(solution)/shard_map/ppermute | solution.py:286
  31.2 12.6 %collective-permute-start.10 = (bf16[64,2176]{1,0:T(8,128)(2,1)S(1)}, bf16[64,2176]{1,0:T(8,128)(2,1)S(1)}, u32[]{:S(2)}, u32[]{:S(2)}) collective-permute-start(bf16[64,2176]{1,0:T(8,128)(2,1)S(1)} %join.5), channel_id=1, source_target_pairs={{0,2},{1,3},{2,0},{3,1},{4,6},{5,7},{6,4},{7,5},{8,10},{9,11},{10,... | collective-permute-start | bytes 835592 | tf_op jit(solution)/shard_map/ppermute | solution.py:286
  40.2 6.6 %collective-permute-start.8 = (bf16[64,2176]{1,0:T(8,128)(2,1)S(1)}, bf16[64,2176]{1,0:T(8,128)(2,1)S(1)}, u32[]{:S(2)}, u32[]{:S(2)}) collective-permute-start(bf16[64,2176]{1,0:T(8,128)(2,1)S(1)} %get-tuple-element.35), channel_id=1, source_target_pairs={{0,8},{1,9},{2,10},{3,11},{8,16},{9,17},{10,18},{11,19},{16,24},{1... | collective-permute-start | bytes 835592 | tf_op jit(solution)/shard_map/ppermute | solution.py:286
  41.7 6.5 %collective-permute-start.9 = (bf16[64,2176]{1,0:T(8,128)(2,1)S(1)}, bf16[64,2176]{1,0:T(8,128)(2,1)S(1)}, u32[]{:S(2)}, u32[]{:S(2)}) collective-permute-start(bf16[64,2176]{1,0:T(8,128)(2,1)S(1)} %get-tuple-element.36), channel_id=1, source_target_pairs={{0,4},{1,5},{2,6},{3,7},{8,0},{9,1},{10,2},{11,3},{16,8},{17,9},{1... | collective-permute-start | bytes 835592 | tf_op jit(solution)/shard_map/ppermute | solution.py:286
  42.2 6.5 %collective-permute-start.11 = (bf16[64,2176]{1,0:T(8,128)(2,1)S(1)}, bf16[64,2176]{1,0:T(8,128)(2,1)S(1)}, u32[]{:S(2)}, u32[]{:S(2)}) collective-permute-start(bf16[64,2176]{1,0:T(8,128)(2,1)S(1)} %get-tuple-element.39), channel_id=1, source_target_pairs={{0,2},{1,3},{2,0},{3,1},{4,6},{5,7},{6,4},{7,5},{8,10},{9,11},{10,... | collective-permute-start | bytes 835592 | tf_op jit(solution)/shard_map/ppermute | solution.py:286
  51.9 11.2 %all-to-all-start = ((f32[32,8,128]{2,1,0:T(8,128)}), f32[32,8,128]{2,1,0:T(8,128)S(1)}, u32[]{:S(2)}, u32[]{:S(2)}) async-start(f32[32,8,128]{2,1,0:T(8,128)} %stats_last.1), calls=%async_computation | async-start | bytes 262144 | tf_op jit(solution)/shard_map/all_to_all | solution.py:315

commit v4 on v3

--- a/solution.py
+++ b/solution.py
@@ -41,9 +41,23 @@
     return [(r * n_tp + t, r * n_tp + (t ^ bit)) for r in range(n_req) for t in range(n_tp)]
 
 
-def block_starts(rows, b_rows):
-    g = rows // 2 - b_rows
-    return (0, g, rows // 2, rows - g), (g, b_rows, b_rows, g)
+def segments(rows):
+    e = rows // 8
+    return (0, 2 * e, 3 * e, 4 * e, 5 * e, 6 * e), (2 * e, e, e, e, e, 2 * e)
+
+
+PARTS = {
+    "all": (0, 1, 2, 3, 4, 5),
+    "most": (0, 1, 2, 3),
+    "half": (0, 1, 2),
+    "y": (5, 4),
+    "y_last": (5,),
+    "c": (4,),
+}
+
+
+def part_rows(part, rows):
+    return sum(segments(rows)[1][j] for j in PARTS[part])
 
 
 def digits(target):
@@ -62,9 +76,7 @@
     return jnp.sum(ext.astype(jnp.float32) * weight, axis=1, keepdims=True)
 
 
-def norm_kernel(
-    b_rows, x_hbm, gain_hbm, tid_hbm, xn_ref, cw_ref, ccw_ref, x_ref, gain_ref, tid_ref, sems
-):
+def norm_kernel(x_hbm, gain_hbm, tid_hbm, xn_ref, cw_ref, ccw_ref, x_ref, gain_ref, tid_ref, sems):
     rows, d = x_ref.shape
     tp = lax.axis_index("tp")
     core, plane = tp % 2, tp // 2
@@ -83,23 +95,24 @@
     feats = x_ref[...].astype(jnp.float32)
     scale = lax.rsqrt(jnp.mean(feats * feats, axis=-1, keepdims=True) + 1e-06)
     xn_ref[:, :d] = (feats * scale * gain_ref[...]).astype(jnp.bfloat16)
-    starts, sizes = block_starts(rows, b_rows)
+    starts, sizes = segments(rows)
     for ref, flip in ((cw_ref, 0), (ccw_ref, 1)):
         down = plane != flip
         at = 0
-        for j in range(3):
-            start = pl.multiple_of(jnp.where(down, starts[3 - j], starts[j]), 16)
+        for j in PARTS["most"]:
+            start = pl.multiple_of(jnp.where(down, starts[5 - j], starts[j]), 16)
             ref[pl.ds(at, sizes[j]), :] = xn_ref[pl.ds(start, sizes[j]), :]
             at += sizes[j]
 
 
-def norm_rows(hidden, norm_gain, target_ids, rows, b_rows):
+def norm_rows(hidden, norm_gain, target_ids, rows):
     d = hidden.shape[1]
     wide = d + LANES
-    shapes = [(rows, wide), (rows // 2 + b_rows, wide), (rows // 2 + b_rows, wide)]
+    message = (part_rows("most", rows), wide)
+    shapes = [(rows, wide), message, message]
     hbm_operands = (hidden, norm_gain.reshape(1, d), target_ids.reshape(2, rows))
     return pl.pallas_call(
-        functools.partial(norm_kernel, b_rows),
+        norm_kernel,
         out_shape=[jax.ShapeDtypeStruct(s, jnp.bfloat16) for s in shapes],
         in_specs=[pl.BlockSpec(memory_space=pl.ANY)] * 3,
         scratch_shapes=[
@@ -113,30 +126,28 @@
     )(*(pltpu.with_memory_space_constraint(v, pltpu.HBM) for v in hbm_operands))
 
 
-def join_kernel(first_ref, second_ref, joined_ref, *head_refs):
-    half = joined_ref.shape[0] // 2
-    joined_ref[:half, :] = first_ref[:half, :]
-    joined_ref[half:, :] = second_ref[:half, :]
-    for ref, head_ref in zip((first_ref, second_ref), head_refs):
-        head_ref[...] = ref[: head_ref.shape[0], :]
-
-
-def join_heads(first, second, count, head_count=0):
-    wide = first.shape[1]
-    shapes = [(2 * count, wide)] + [(head_count, wide)] * (2 if head_count else 0)
+def cut_kernel(plan, n_in, *refs):
+    for out_ref, pieces in zip(refs[n_in:], plan):
+        to = 0
+        for k, at, count in pieces:
+            out_ref[pl.ds(to, count), :] = refs[k][pl.ds(at, count), :]
+            to += count
+
+
+def cut(arrays, plan):
+    wide = arrays[0].shape[1]
     return pl.pallas_call(
-        join_kernel,
-        out_shape=[jax.ShapeDtypeStruct(s, first.dtype) for s in shapes],
+        functools.partial(cut_kernel, plan, len(arrays)),
+        out_shape=[
+            jax.ShapeDtypeStruct((sum(count for _, _, count in pieces), wide), arrays[0].dtype)
+            for pieces in plan
+        ],
         compiler_params=pltpu.CompilerParams(vmem_limit_bytes=VMEM_BYTES),
-        name="join",
-    )(first, second)
-
-
-def piece_segments(part):
-    return {"all": (0, 1, 2, 3), "most": (0, 1, 2), "half": (0, 1), "y": (3,)}[part]
-
-
-def stats_kernel(metas, n_req, n_tp, b_rows, rows, earlier, tail, *refs):
+        name="cut",
+    )(*arrays)
+
+
+def stats_kernel(metas, n_req, n_tp, rows, earlier, tail, *refs):
     n = len(metas)
     piece_refs, (w0_ref, w1_ref), refs = refs[:n], refs[n : n + 2], refs[n + 2 :]
     if tail:
@@ -182,30 +193,30 @@
 
     lax.fori_loop(0, total // step, body, 0, unroll=4)
     if tail:
-        pack_stats(earlier + (metas,), (*stat_refs, out_ref), packed_ref, n_req, n_tp, b_rows, rows)
-
-
-def pack_stats(metas, stat_refs, packed_ref, n_req, n_tp, b_rows, rows):
+        pack_stats(earlier + (metas,), (*stat_refs, out_ref), packed_ref, n_req, n_tp, rows)
+
+
+def pack_stats(metas, stat_refs, packed_ref, n_req, n_tp, rows):
     plane = lax.axis_index("tp") // 2
     place = ring_place(lax.axis_index("req"), n_req)
-    starts, sizes = block_starts(rows, b_rows)
+    _, sizes = segments(rows)
     shards = {}
     for pieces, ref in zip(metas, stat_refs):
         at = 0
         for turn, hops, part in (p for parts in pieces for p in parts):
-            for j in piece_segments(part):
+            for j in PARTS[part]:
                 shards.setdefault((turn, hops) if 2 * hops != n_req else (0, hops), []).append(
                     (turn, j, ref[pl.ds(at, sizes[j]), :])
                 )
                 at += sizes[j]
     for (turn, hops), found in shards.items():
         if turn == 0 and hops:
-            up = {j: v for t, j, v in found if t > 0} | {3 - j: v for t, j, v in found if t < 0}
+            up = {j if t > 0 else 5 - j: v for t, j, v in found}
         else:
             up = {j: v for _, j, v in found}
-        ordered = jnp.concatenate([up[j] for j in range(4)], axis=0)
+        ordered = jnp.concatenate([up[j] for j in range(6)], axis=0)
         if hops:
-            flipped = jnp.concatenate([up[3 - j] for j in range(4)], axis=0)
+            flipped = jnp.concatenate([up[5 - j] for j in range(6)], axis=0)
             down = plane != (0 if turn >= 0 else 1)
             ordered = jnp.where(down, flipped, ordered)
         source = ring_req((place - (turn or 1) * hops + n_req) % n_req, n_req)
@@ -214,12 +225,12 @@
             packed_ref[source * n_tp + t] = packed
 
 
-def stats_of(pieces, metas, w0, w1, n_req, n_tp, b_rows, rows, earlier=(), stats=(), tail=False):
+def stats_of(pieces, metas, w0, w1, n_req, n_tp, rows, earlier=(), stats=(), tail=False):
     d, vdev = w0.shape
     total = sum(p.shape[0] for p in pieces)
     row_stats = (total, LANES)
     return pl.pallas_call(
-        functools.partial(stats_kernel, metas, n_req, n_tp, b_rows, rows, earlier, tail),
+        functools.partial(stats_kernel, metas, n_req, n_tp, rows, earlier, tail),
         out_shape=jax.ShapeDtypeStruct(
             (n_req * n_tp, STATS, rows) if tail else row_stats, jnp.float32
         ),
@@ -278,37 +289,59 @@
 
 def per_device(n_req, n_tp, hidden_states, norm_gain, head, target_ids, lengths):
     rows = hidden_states.shape[0] // 2
-    b_rows = rows // 4
     cw_pairs, ccw_pairs = ring_pairs(n_req, n_tp, 1), ring_pairs(n_req, n_tp, -1)
     other_core, other_y = tp_pairs(n_req, n_tp, 1), tp_pairs(n_req, n_tp, 2)
+    sizes = (n_req, n_tp, rows)
+    y_rows, c_rows, half = (part_rows(part, rows) for part in ("y", "c", "half"))
+    y_last_rows = part_rows("y_last", rows)
+    metas, stats = [], []
 
     def send(value, pairs):
         return lax.ppermute(value, AXES, pairs)
 
-    other_head = send(head, other_core)
-    xn, to_cw, to_ccw = norm_rows(hidden_states, norm_gain, target_ids, rows, b_rows)
-    sizes = (n_req, n_tp, b_rows, rows)
-    g = rows // 2 - b_rows
-    meta = (((0, 0, "all"),),)
-    metas = [meta]
-    stats = [stats_of([xn], meta, head, other_head, *sizes)]
-    for hops in range(1, n_req // 2 + 1):
-        last = 2 * hops == n_req
+    def work(items):
+        pieces, meta = zip(*items)
+        stats.append(stats_of(pieces, meta, head, other_head, *sizes))
+        metas.append(meta)
+
+    def after(value):
+        value, stats[-1] = lax.optimization_barrier((value, stats[-1]))
+        return value
+
+    xn, to_cw, to_ccw = norm_rows(hidden_states, norm_gain, target_ids, rows)
+    swapped, xn = lax.optimization_barrier((head, xn))
+    other_head = send(swapped, other_core)
+    items = [(xn, ((0, 0, "all"),))]
+    for hops in range(1, n_req // 2):
+        next_to_last = 2 * hops + 2 == n_req
         cw, ccw = send(to_cw, cw_pairs), send(to_ccw, ccw_pairs)
         if hops > 1:
             y_next = send(y_message, other_y)
-            stats.append(stats_of(pieces, meta, head, other_head, *sizes))
-            metas.append(meta)
-        cw, ccw, stats[-1] = lax.optimization_barrier((cw, ccw, stats[-1]))
-        part = "half" if last else "most"
-        pieces, meta = [cw, ccw], [((1, hops, part),), ((-1, hops, part),)]
-        if not last:
-            y_message, *heads = join_heads(cw, ccw, g, rows // 2 if 2 * hops + 2 == n_req else 0)
-            to_cw, to_ccw = heads or (cw, ccw)
+        work(items)
+        cw, ccw = after(cw), after(ccw)
+        items = [(cw, ((1, hops, "most"),)), (ccw, ((-1, hops, "most"),))]
         if hops > 1:
-            pieces.append(y_next)
-            meta.append(((1, hops - 1, "y"), (-1, hops - 1, "y")))
-        meta = tuple(meta)
+            items.append((y_next, ((1, hops - 1, "y"), (-1, hops - 1, "y"))))
+        if next_to_last:
+            (to_cw,), (to_ccw,) = cut((cw,), [[(0, 0, half)]]), cut((ccw,), [[(0, 0, half)]])
+        else:
+            to_cw, to_ccw = cw, ccw
+        count = y_last_rows if next_to_last else y_rows
+        (y_message,) = cut((cw, ccw), [[(0, 0, count), (1, 0, count)]])
+    hops = n_req // 2
+    c_cw, c_ccw = cut((y_next,), [[(0, y_rows - c_rows, c_rows)], [(0, 2 * y_rows - c_rows, c_rows)]])
+    cw, ccw = send(to_cw, cw_pairs), send(to_ccw, ccw_pairs)
+    y_next = send(y_message, other_y)
+    c_cw, c_ccw = send(c_cw, cw_pairs), send(c_ccw, ccw_pairs)
+    work(items)
+    cw, ccw = after(cw), after(ccw)
+    work([(cw, ((1, hops, "half"),)), (ccw, ((-1, hops, "half"),))])
+    items = [
+        (c_cw, ((1, hops - 1, "c"),)),
+        (c_ccw, ((-1, hops - 1, "c"),)),
+        (y_next, ((1, hops - 1, "y_last"), (-1, hops - 1, "y_last"))),
+    ]
+    pieces, meta = zip(*items)
     packed = stats_of(
         pieces, meta, head, other_head, *sizes, earlier=tuple(metas), stats=stats, tail=True
     )

time: 64.1 us -> 61.1 us (0.953)
  waiting for transfers between devices: 28.5 us -> 20.1 us
  starting transfers between devices: 17 us -> 21.4 us
  Pallas kernels: 15.1 us -> 16.1 us
    ppermute x12 -> x14, waiting for transfers between devices: 20.9 us -> 12.5 us  [send(): return lax.ppermute(value, AXES, pairs)]
    ppermute x12 -> x14, starting transfers between devices: 14 us -> 16.5 us  [send(): return lax.ppermute(value, AXES, pairs)]
    all_to_all x1, starting transfers between devices: 3.01 us -> 4.98 us  [per_device(): received = lax.all_to_all(packed, AXES, 0, 0, tiled=True)]
    pallas_call x9 -> x13, Pallas kernels: 14.4 us -> 15.4 us  [the longest x6 13.9 us: stats_of(): pl.pallas_call(functools.partial(stats_kernel, metas, n_req, n_tp, rows,...]
  transfers between devices with their start and end apart: 13 -> 15, of which waited for: 10 -> 6; matrix products, arithmetic and copies ran while one was open for 0% -> 0% of each run, Pallas kernels for 18% -> 19%
where the time goes in v4:
time: 61.1 us; the launch traced here: 60.9 us
  starting transfers between devices  21.4 us (35%)
  waiting for transfers between devices  20.1 us (33%)
  Pallas kernels  16.1 us (26%)
  local copies, waits for them, and re-layouts  1.89 us (3%)
  between operations  1.37 us (2%)
    ppermute x14, starting transfers between devices, send(): return lax.ppermute(value, AXES, pairs)  16.5 us
    pallas_call x6, Pallas kernels, stats_of(): pl.pallas_call(functools.partial(stats_kernel, metas, n_req, n_tp, rows,...  13.9 us
    ppermute x14, waiting for transfers between devices, send(): return lax.ppermute(value, AXES, pairs)  12.5 us
    all_to_all x1, waiting for transfers between devices, per_device(): received = lax.all_to_all(packed, AXES, 0, 0, tiled=True)  7.58 us
    all_to_all x1, starting transfers between devices, per_device(): received = lax.all_to_all(packed, AXES, 0, 0, tiled=True)  4.98 us
    unnamed x4, local copies, waits for them, and re-layouts  1.89 us
    pallas_call x1, Pallas kernels, norm_rows(): pl.pallas_call(norm_kernel, out_shape=[jax.ShapeDtypeStruct(s, jnp.bfloat...  1.41 us
  transfers between devices with their start and end apart: 15, of which 6 were waited for; matrix products, arithmetic and copies ran while one was open for 0% of the time, Pallas kernels for 19%

profile of v4, /device:TPU:0, one launch (start us, length us, event | category | flops | bytes accessed | tf_op | source)
XLA Modules:
  0.0 60.9 jit_solution(2181850100761645531)
XLA Ops:
  0.6 1.4 %norm.1 = (bf16[128,2176]{1,0:T(8,128)(2,1)S(1)}, bf16[80,2176]{1,0:T(8,128)(2,1)S(1)}, bf16[80,2176]{1,0:T(8,128)(2,1)S(1)}) custom-call(bf16[256,2048]{1,0:T(8,128)(2,1)} %x_hbm.1, f32[1,2048]{1,0:T(1,128)} %bitcast.6, s32[2,128]{1,0:T(2,128)} %bitcast.7), custom_call_target="tpu_custom_call" | custom-call | tf_op jit(solution)/shard_map/norm/pallas_call | solution.py:114
  2.1 0.5 collective-permute-start.1
  2.5 2.7 %collective-permute-start = (bf16[80,2176]{1,0:T(8,128)(2,1)S(1)}, bf16[80,2176]{1,0:T(8,128)(2,1)S(1)}, u32[]{:S(2)}, u32[]{:S(2)}) collective-permute-start(bf16[80,2176]{1,0:T(8,128)(2,1)S(1)} %get-tuple-element.31), channel_id=1, source_target_pairs={{0,8},{1,9},{2,10},{3,11},{8,16},{9,17},{10,18},{11,19},{16,24},{1... | collective-permute-start | bytes 1044488 | tf_op jit(solution)/shard_map/ppermute | solution.py:300
  5.2 2.8 %collective-permute-done.1.refs_2_.refs_3_.refs_4_ = bf16[2048,768]{1,0:T(8,128)(2,1)S(1)} collective-permute-done((bf16[2048,768]{1,0:T(8,128)(2,1)}, bf16[2048,768]{1,0:T(8,128)(2,1)S(1)}, u32[]{:S(2)}, u32[]{:S(2)}) %collective-permute-start.1) | collective-permute-done | bytes 3145760 | tf_op jit(solution)/shard_map/ppermute | solution.py:300
  8.0 1.9 %copy-done = bf16[2048,768]{1,0:T(8,128)(2,1)S(1)} copy-done((bf16[2048,768]{1,0:T(8,128)(2,1)S(1)}, bf16[2048,768]{1,0:T(8,128)(2,1)}, u32[]{:S(2)}) %copy-start) | copy-done | bytes 3145752
  9.9 1.6 %stats.5.refs_5_ = f32[128,128]{1,0:T(8,128)S(1)} custom-call(bf16[128,2176]{1,0:T(8,128)(2,1)S(1)} %get-tuple-element.33.refs_0_, bf16[2048,768]{1,0:T(8,128)(2,1)S(1)} %copy-done, bf16[2048,768]{1,0:T(8,128)(2,1)S(1)} %collective-permute-done.1.refs_2_.refs_3_.refs_4_), custom_call_target="tpu_custom_call" | custom-call | flops 805306368 | bytes 6291456 | tf_op jit(solution)/shard_map/stats/pallas_call | solution.py:232
  11.5 2.4 %collective-permute-done.refs_0_ = bf16[80,2176]{1,0:T(8,128)(2,1)S(1)} collective-permute-done((bf16[80,2176]{1,0:T(8,128)(2,1)S(1)}, bf16[80,2176]{1,0:T(8,128)(2,1)S(1)}, u32[]{:S(2)}, u32[]{:S(2)}) %collective-permute-start) | collective-permute-done | bytes 348192 | tf_op jit(solution)/shard_map/ppermute | solution.py:300
  13.9 1.8 %collective-permute-start.2 = (bf16[80,2176]{1,0:T(8,128)(2,1)S(1)}, bf16[80,2176]{1,0:T(8,128)(2,1)S(1)}, u32[]{:S(2)}, u32[]{:S(2)}) collective-permute-start(bf16[80,2176]{1,0:T(8,128)(2,1)S(1)} %collective-permute-done.refs_0_), channel_id=1, source_target_pairs={{0,8},{1,9},{2,10},{3,11},{8,16},{9,17},{10,18},{11,19},{16,24},{1... | collective-permute-start | bytes 1044488 | tf_op jit(solution)/shard_map/ppermute | solution.py:300
  15.7 0.0 collective-permute-done.3.refs_1_
  15.7 0.2 collective-permute-start.4
  15.9 1.8 %collective-permute-start.9 = (bf16[96,2176]{1,0:T(8,128)(2,1)S(1)}, bf16[96,2176]{1,0:T(8,128)(2,1)S(1)}, u32[]{:S(2)}, u32[]{:S(2)}) collective-permute-start(bf16[96,2176]{1,0:T(8,128)(2,1)S(1)} %cut.8), channel_id=1, source_target_pairs={{0,2},{1,3},{2,0},{3,1},{4,6},{5,7},{6,4},{7,5},{8,10},{9,11},{10,... | collective-permute-start | bytes 1253384 | tf_op jit(solution)/shard_map/ppermute | solution.py:300
  17.8 2.2 %stats.6.refs_6_ = f32[160,128]{1,0:T(8,128)S(1)} custom-call(bf16[80,2176]{1,0:T(8,128)(2,1)S(1)} %collective-permute-done.refs_0_, bf16[80,2176]{1,0:T(8,128)(2,1)S(1)} %collective-permute-done.3.refs_1_, bf16[2048,768]{1,0:T(8,128)(2,1)S(1)} %copy-done.1, bf16[2048,768]{1,0:T(8,128)(2,1)S(1)} %collective-permute-done.1.refs_2_.refs_3_.refs_4_), custom_call_target="tpu_custom_call" | custom-call | flops 1006632960 | bytes 6291456 | tf_op jit(solution)/shard_map/stats/pallas_call | solution.py:232
  20.0 3.8 %collective-permute-done.2.refs_0_ = bf16[80,2176]{1,0:T(8,128)(2,1)S(1)} collective-permute-done((bf16[80,2176]{1,0:T(8,128)(2,1)S(1)}, bf16[80,2176]{1,0:T(8,128)(2,1)S(1)}, u32[]{:S(2)}, u32[]{:S(2)}) %collective-permute-start.2) | collective-permute-done | bytes 348192 | tf_op jit(solution)/shard_map/ppermute | solution.py:300
  23.8 1.6 %collective-permute-start.8 = (bf16[80,2176]{1,0:T(8,128)(2,1)S(1)}, bf16[80,2176]{1,0:T(8,128)(2,1)S(1)}, u32[]{:S(2)}, u32[]{:S(2)}) collective-permute-start(bf16[80,2176]{1,0:T(8,128)(2,1)S(1)} %collective-permute-done.2.refs_0_), channel_id=1, source_target_pairs={{0,8},{1,9},{2,10},{3,11},{8,16},{9,17},{10,18},{11,19},{16,24},{1... | collective-permute-start | bytes 1044488 | tf_op jit(solution)/shard_map/ppermute | solution.py:300
  25.4 0.0 collective-permute-done.4.refs_1_
  25.4 0.4 collective-permute-start.10
  25.9 1.6 %collective-permute-start.5 = (bf16[96,2176]{1,0:T(8,128)(2,1)S(1)}, bf16[96,2176]{1,0:T(8,128)(2,1)S(1)}, u32[]{:S(2)}, u32[]{:S(2)}) collective-permute-start(bf16[96,2176]{1,0:T(8,128)(2,1)S(1)} %cut.6), channel_id=1, source_target_pairs={{0,2},{1,3},{2,0},{3,1},{4,6},{5,7},{6,4},{7,5},{8,10},{9,11},{10,... | collective-permute-start | bytes 1253384 | tf_op jit(solution)/shard_map/ppermute | solution.py:300
  27.5 0.0 collective-permute-done.9.refs_2_
  27.5 3.0 %stats.7.refs_7_ = f32[256,128]{1,0:T(8,128)S(1)} custom-call(bf16[80,2176]{1,0:T(8,128)(2,1)S(1)} %collective-permute-done.2.refs_0_, bf16[80,2176]{1,0:T(8,128)(2,1)S(1)} %collective-permute-done.4.refs_1_, bf16[96,2176]{1,0:T(8,128)(2,1)S(1)} %collective-permute-done.9.refs_2_, bf16[2048,768]{1,0:T(8,128)(2,1)S(1)} %copy-done.1, ...), custom_call_target="tpu_custom_call" | custom-call | flops 1610612736 | bytes 6291456 | tf_op jit(solution)/shard_map/stats/pallas_call | solution.py:232
  30.5 2.4 %collective-permute-done.8.refs_0_ = bf16[80,2176]{1,0:T(8,128)(2,1)S(1)} collective-permute-done((bf16[80,2176]{1,0:T(8,128)(2,1)S(1)}, bf16[80,2176]{1,0:T(8,128)(2,1)S(1)}, u32[]{:S(2)}, u32[]{:S(2)}) %collective-permute-start.8) | collective-permute-done | bytes 348192 | tf_op jit(solution)/shard_map/ppermute | solution.py:300
  32.8 1.1 %collective-permute-done.10.refs_1_.refs_0_ = bf16[80,2176]{1,0:T(8,128)(2,1)S(1)} collective-permute-done((bf16[80,2176]{1,0:T(8,128)(2,1)S(1)}, bf16[80,2176]{1,0:T(8,128)(2,1)S(1)}, u32[]{:S(2)}, u32[]{:S(2)}) %collective-permute-start.10) | collective-permute-done | bytes 348192 | tf_op jit(solution)/shard_map/ppermute | solution.py:300
  34.0 1.6 %collective-permute-start.13 = (bf16[64,2176]{1,0:T(8,128)(2,1)S(1)}, bf16[64,2176]{1,0:T(8,128)(2,1)S(1)}, u32[]{:S(2)}, u32[]{:S(2)}) collective-permute-start(bf16[64,2176]{1,0:T(8,128)(2,1)S(1)} %cut.11), channel_id=1, source_target_pairs={{0,8},{1,9},{2,10},{3,11},{8,16},{9,17},{10,18},{11,19},{16,24},{1... | collective-permute-start | bytes 835592 | tf_op jit(solution)/shard_map/ppermute | solution.py:300
  35.6 0.5 collective-permute-start.12
  36.1 1.6 %collective-permute-start.11 = (bf16[64,2176]{1,0:T(8,128)(2,1)S(1)}, bf16[64,2176]{1,0:T(8,128)(2,1)S(1)}, u32[]{:S(2)}, u32[]{:S(2)}) collective-permute-start(bf16[64,2176]{1,0:T(8,128)(2,1)S(1)} %cut.9), channel_id=1, source_target_pairs={{0,2},{1,3},{2,0},{3,1},{4,6},{5,7},{6,4},{7,5},{8,10},{9,11},{10,... | collective-permute-start | bytes 835592 | tf_op jit(solution)/shard_map/ppermute | solution.py:300
  37.7 1.6 %collective-permute-start.6 = (bf16[16,2176]{1,0:T(8,128)(2,1)S(1)}, bf16[16,2176]{1,0:T(8,128)(2,1)S(1)}, u32[]{:S(2)}, u32[]{:S(2)}) collective-permute-start(bf16[16,2176]{1,0:T(8,128)(2,1)S(1)} %get-tuple-element.42), channel_id=1, source_target_pairs={{0,8},{1,9},{2,10},{3,11},{8,16},{9,17},{10,18},{11,19},{16,24},{1... | collective-permute-start | bytes 208904 | tf_op jit(solution)/shard_map/ppermute | solution.py:300
  39.4 0.4 collective-permute-start.7
  39.8 3.0 %stats.8.refs_8_ = f32[256,128]{1,0:T(8,128)S(1)} custom-call(bf16[80,2176]{1,0:T(8,128)(2,1)S(1)} %collective-permute-done.8.refs_0_, bf16[80,2176]{1,0:T(8,128)(2,1)S(1)} %collective-permute-done.10.refs_1_.refs_0_, bf16[96,2176]{1,0:T(8,128)(2,1)S(1)} %collective-permute-done.5.refs_0_.refs_2_, bf16[2048,768]{1,0:T(8,128)(2,1)S(1)} %copy-done.1, ...), custom_call_target="tpu_custom_call" | custom-call | flops 1610612736 | bytes 6291456 | tf_op jit(solution)/shard_map/stats/pallas_call | solution.py:232
  42.8 1.6 %stats.9.refs_9_ = f32[128,128]{1,0:T(8,128)S(1)} custom-call(bf16[64,2176]{1,0:T(8,128)(2,1)S(1)} %collective-permute-done.13.refs_0_, bf16[64,2176]{1,0:T(8,128)(2,1)S(1)} %collective-permute-done.12.refs_1_, bf16[2048,768]{1,0:T(8,128)(2,1)S(1)} %copy-done.1, bf16[2048,768]{1,0:T(8,128)(2,1)S(1)} %collective-permute-done.1.refs_2_.refs_3_.refs_4_), custom_call_target="tpu_custom_call" | custom-call | flops 805306368 | bytes 6291456 | tf_op jit(solution)/shard_map/stats/pallas_call | solution.py:232
  44.4 2.6 %stats_last.1 = f32[32,8,128]{2,1,0:T(8,128)} custom-call(bf16[16,2176]{1,0:T(8,128)(2,1)S(1)} %collective-permute-done.6.refs_0_, bf16[16,2176]{1,0:T(8,128)(2,1)S(1)} %collective-permute-done.7.refs_1_, bf16[64,2176]{1,0:T(8,128)(2,1)S(1)} %collective-permute-done.11.refs_2_, bf16[2048,768]{1,0:T(8,128)(2,1)S(1)} %copy-done.1, ...), custom_call_target="tpu_custom_call" | custom-call | flops 603979776 | bytes 6291456 | tf_op jit(solution)/shard_map/stats_last/pallas_call | solution.py:232
  47.0 5.0 %all-to-all-start = ((f32[32,8,128]{2,1,0:T(8,128)}), f32[32,8,128]{2,1,0:T(8,128)S(1)}, u32[]{:S(2)}, u32[]{:S(2)}) async-start(f32[32,8,128]{2,1,0:T(8,128)} %stats_last.1), calls=%async_computation | async-start | bytes 262144 | tf_op jit(solution)/shard_map/all_to_all | solution.py:348
  52.6 7.6 %all-to-all-done.r_ref = f32[32,8,128]{2,1,0:T(8,128)S(1)} async-done(((f32[32,8,128]{2,1,0:T(8,128)}), f32[32,8,128]{2,1,0:T(8,128)S(1)}, u32[]{:S(2)}, u32[]{:S(2)}) %all-to-all-start) | async-done | bytes 131104 | tf_op jit(solution)/shard_map/all_to_all | solution.py:348
  60.2 0.7 %finish.1 = (f32[2,128]{1,0:T(2,128)}, f32[2,128]{1,0:T(2,128)}, f32[1,1]{1,0:T(1,128)}, f32[1,1]{1,0:T(1,128)}) custom-call(f32[32,8,128]{2,1,0:T(8,128)S(1)} %all-to-all-done.r_ref, s32[1]{0:T(128)S(6)} %copy.9.len_ref), custom_call_target="tpu_custom_call" | custom-call | tf_op jit(solution)/shard_map/finish/pallas_call | solution.py:276
  (16 shorter events, 0.2 us)
Async XLA Ops:
  2.1 6.0 %collective-permute-start.1 = (bf16[2048,768]{1,0:T(8,128)(2,1)}, bf16[2048,768]{1,0:T(8,128)(2,1)S(1)}, u32[]{:S(2)}, u32[]{:S(2)}) collective-permute-start(bf16[2048,768]{1,0:T(8,128)(2,1)} %refs_3_.5), channel_id=1, source_target_pairs={{0,1},{1,0},{2,3},{3,2},{4,5},{5,4},{6,7},{7,6},{8,9},{9,8},{10,11... | collective-permute-start | bytes 9437192 | tf_op jit(solution)/shard_map/ppermute | solution.py:300
  2.5 11.3 %collective-permute-start = (bf16[80,2176]{1,0:T(8,128)(2,1)S(1)}, bf16[80,2176]{1,0:T(8,128)(2,1)S(1)}, u32[]{:S(2)}, u32[]{:S(2)}) collective-permute-start(bf16[80,2176]{1,0:T(8,128)(2,1)S(1)} %get-tuple-element.31), channel_id=1, source_target_pairs={{0,8},{1,9},{2,10},{3,11},{8,16},{9,17},{10,18},{11,19},{16,24},{1... | collective-permute-start | bytes 1044488 | tf_op jit(solution)/shard_map/ppermute | solution.py:300
  5.2 10.5 %collective-permute-start.3 = (bf16[80,2176]{1,0:T(8,128)(2,1)S(1)}, bf16[80,2176]{1,0:T(8,128)(2,1)S(1)}, u32[]{:S(2)}, u32[]{:S(2)}) collective-permute-start(bf16[80,2176]{1,0:T(8,128)(2,1)S(1)} %get-tuple-element.36), channel_id=1, source_target_pairs={{0,4},{1,5},{2,6},{3,7},{8,0},{9,1},{10,2},{11,3},{16,8},{17,9},{1... | collective-permute-start | bytes 1044488 | tf_op jit(solution)/shard_map/ppermute | solution.py:300
  8.0 1.9 %copy-start = (bf16[2048,768]{1,0:T(8,128)(2,1)S(1)}, bf16[2048,768]{1,0:T(8,128)(2,1)}, u32[]{:S(2)}) copy-start(bf16[2048,768]{1,0:T(8,128)(2,1)} %refs_3_.5) | copy-start | bytes 9437188
  9.9 7.9 %copy-start.1 = (bf16[2048,768]{1,0:T(8,128)(2,1)S(1)}, bf16[2048,768]{1,0:T(8,128)(2,1)}, u32[]{:S(2)}) copy-start(bf16[2048,768]{1,0:T(8,128)(2,1)} %refs_3_.5) | copy-start | bytes 9437188
  13.9 9.9 %collective-permute-start.2 = (bf16[80,2176]{1,0:T(8,128)(2,1)S(1)}, bf16[80,2176]{1,0:T(8,128)(2,1)S(1)}, u32[]{:S(2)}, u32[]{:S(2)}) collective-permute-start(bf16[80,2176]{1,0:T(8,128)(2,1)S(1)} %collective-permute-done.refs_0_), channel_id=1, source_target_pairs={{0,8},{1,9},{2,10},{3,11},{8,16},{9,17},{10,18},{11,19},{16,24},{1... | collective-permute-start | bytes 1044488 | tf_op jit(solution)/shard_map/ppermute | solution.py:300
  15.7 9.7 %collective-permute-start.4 = (bf16[80,2176]{1,0:T(8,128)(2,1)S(1)}, bf16[80,2176]{1,0:T(8,128)(2,1)S(1)}, u32[]{:S(2)}, u32[]{:S(2)}) collective-permute-start(bf16[80,2176]{1,0:T(8,128)(2,1)S(1)} %collective-permute-done.3.refs_1_), channel_id=1, source_target_pairs={{0,4},{1,5},{2,6},{3,7},{8,0},{9,1},{10,2},{11,3},{16,8},{17,9},{1... | collective-permute-start | bytes 1044488 | tf_op jit(solution)/shard_map/ppermute | solution.py:300
  15.9 11.5 %collective-permute-start.9 = (bf16[96,2176]{1,0:T(8,128)(2,1)S(1)}, bf16[96,2176]{1,0:T(8,128)(2,1)S(1)}, u32[]{:S(2)}, u32[]{:S(2)}) collective-permute-start(bf16[96,2176]{1,0:T(8,128)(2,1)S(1)} %cut.8), channel_id=1, source_target_pairs={{0,2},{1,3},{2,0},{3,1},{4,6},{5,7},{6,4},{7,5},{8,10},{9,11},{10,... | collective-permute-start | bytes 1253384 | tf_op jit(solution)/shard_map/ppermute | solution.py:300
  23.8 9.1 %collective-permute-start.8 = (bf16[80,2176]{1,0:T(8,128)(2,1)S(1)}, bf16[80,2176]{1,0:T(8,128)(2,1)S(1)}, u32[]{:S(2)}, u32[]{:S(2)}) collective-permute-start(bf16[80,2176]{1,0:T(8,128)(2,1)S(1)} %collective-permute-done.2.refs_0_), channel_id=1, source_target_pairs={{0,8},{1,9},{2,10},{3,11},{8,16},{9,17},{10,18},{11,19},{16,24},{1... | collective-permute-start | bytes 1044488 | tf_op jit(solution)/shard_map/ppermute | solution.py:300
  25.4 8.5 %collective-permute-start.10 = (bf16[80,2176]{1,0:T(8,128)(2,1)S(1)}, bf16[80,2176]{1,0:T(8,128)(2,1)S(1)}, u32[]{:S(2)}, u32[]{:S(2)}) collective-permute-start(bf16[80,2176]{1,0:T(8,128)(2,1)S(1)} %collective-permute-done.4.refs_1_), channel_id=1, source_target_pairs={{0,4},{1,5},{2,6},{3,7},{8,0},{9,1},{10,2},{11,3},{16,8},{17,9},{1... | collective-permute-start | bytes 1044488 | tf_op jit(solution)/shard_map/ppermute | solution.py:300
  25.9 11.9 %collective-permute-start.5 = (bf16[96,2176]{1,0:T(8,128)(2,1)S(1)}, bf16[96,2176]{1,0:T(8,128)(2,1)S(1)}, u32[]{:S(2)}, u32[]{:S(2)}) collective-permute-start(bf16[96,2176]{1,0:T(8,128)(2,1)S(1)} %cut.6), channel_id=1, source_target_pairs={{0,2},{1,3},{2,0},{3,1},{4,6},{5,7},{6,4},{7,5},{8,10},{9,11},{10,... | collective-permute-start | bytes 1253384 | tf_op jit(solution)/shard_map/ppermute | solution.py:300
  34.0 8.8 %collective-permute-start.13 = (bf16[64,2176]{1,0:T(8,128)(2,1)S(1)}, bf16[64,2176]{1,0:T(8,128)(2,1)S(1)}, u32[]{:S(2)}, u32[]{:S(2)}) collective-permute-start(bf16[64,2176]{1,0:T(8,128)(2,1)S(1)} %cut.11), channel_id=1, source_target_pairs={{0,8},{1,9},{2,10},{3,11},{8,16},{9,17},{10,18},{11,19},{16,24},{1... | collective-permute-start | bytes 835592 | tf_op jit(solution)/shard_map/ppermute | solution.py:300
  35.6 7.2 %collective-permute-start.12 = (bf16[64,2176]{1,0:T(8,128)(2,1)S(1)}, bf16[64,2176]{1,0:T(8,128)(2,1)S(1)}, u32[]{:S(2)}, u32[]{:S(2)}) collective-permute-start(bf16[64,2176]{1,0:T(8,128)(2,1)S(1)} %cut.10), channel_id=1, source_target_pairs={{0,4},{1,5},{2,6},{3,7},{8,0},{9,1},{10,2},{11,3},{16,8},{17,9},{1... | collective-permute-start | bytes 835592 | tf_op jit(solution)/shard_map/ppermute | solution.py:300
  36.1 8.3 %collective-permute-start.11 = (bf16[64,2176]{1,0:T(8,128)(2,1)S(1)}, bf16[64,2176]{1,0:T(8,128)(2,1)S(1)}, u32[]{:S(2)}, u32[]{:S(2)}) collective-permute-start(bf16[64,2176]{1,0:T(8,128)(2,1)S(1)} %cut.9), channel_id=1, source_target_pairs={{0,2},{1,3},{2,0},{3,1},{4,6},{5,7},{6,4},{7,5},{8,10},{9,11},{10,... | collective-permute-start | bytes 835592 | tf_op jit(solution)/shard_map/ppermute | solution.py:300
  37.7 6.6 %collective-permute-start.6 = (bf16[16,2176]{1,0:T(8,128)(2,1)S(1)}, bf16[16,2176]{1,0:T(8,128)(2,1)S(1)}, u32[]{:S(2)}, u32[]{:S(2)}) collective-permute-start(bf16[16,2176]{1,0:T(8,128)(2,1)S(1)} %get-tuple-element.42), channel_id=1, source_target_pairs={{0,8},{1,9},{2,10},{3,11},{8,16},{9,17},{10,18},{11,19},{16,24},{1... | collective-permute-start | bytes 208904 | tf_op jit(solution)/shard_map/ppermute | solution.py:300
  39.4 5.0 %collective-permute-start.7 = (bf16[16,2176]{1,0:T(8,128)(2,1)S(1)}, bf16[16,2176]{1,0:T(8,128)(2,1)S(1)}, u32[]{:S(2)}, u32[]{:S(2)}) collective-permute-start(bf16[16,2176]{1,0:T(8,128)(2,1)S(1)} %get-tuple-element.43), channel_id=1, source_target_pairs={{0,4},{1,5},{2,6},{3,7},{8,0},{9,1},{10,2},{11,3},{16,8},{17,9},{1... | collective-permute-start | bytes 208904 | tf_op jit(solution)/shard_map/ppermute | solution.py:300
  47.0 13.2 %all-to-all-start = ((f32[32,8,128]{2,1,0:T(8,128)}), f32[32,8,128]{2,1,0:T(8,128)S(1)}, u32[]{:S(2)}, u32[]{:S(2)}) async-start(f32[32,8,128]{2,1,0:T(8,128)} %stats_last.1), calls=%async_computation | async-start | bytes 262144 | tf_op jit(solution)/shard_map/all_to_all | solution.py:348

commit v5 on v4

--- a/solution.py
+++ b/solution.py
@@ -1,4 +1,5 @@
 import functools
+import math
 
 import jax
 import jax.numpy as jnp
@@ -9,8 +10,9 @@
 
 AXES = ("req", "tp")
 LANES = 128
-STATS = 8
+STATS = 4
 DIGIT_BITS = 7
+CHUNKS = 1
 VMEM_BYTES = 10 * 1024 * 1024
 
 
@@ -56,6 +58,10 @@
 }
 
 
+def shard_index(turn, hops, n_req):
+    return hops if turn >= 0 or 2 * hops == n_req else n_req // 2 + hops
+
+
 def part_rows(part, rows):
     return sum(segments(rows)[1][j] for j in PARTS[part])
 
@@ -80,21 +86,27 @@
     rows, d = x_ref.shape
     tp = lax.axis_index("tp")
     core, plane = tp % 2, tp // 2
-    mine = pl.ds(pl.multiple_of(core * rows, rows), rows)
-    get_x = pltpu.make_async_copy(x_hbm.at[mine, :], x_ref, sems.at[0])
-    get_gain = pltpu.make_async_copy(gain_hbm, gain_ref, sems.at[1])
-    get_tid = pltpu.make_async_copy(tid_hbm, tid_ref, sems.at[2])
-    get_x.start()
+    size = rows // CHUNKS
+    get_gain = pltpu.make_async_copy(gain_hbm, gain_ref, sems.at[CHUNKS])
+    get_tid = pltpu.make_async_copy(tid_hbm, tid_ref, sems.at[CHUNKS + 1])
     get_gain.start()
     get_tid.start()
+    chunks = []
+    for k in range(CHUNKS):
+        there = pl.ds(pl.multiple_of(core * rows + k * size, size), size)
+        here = pl.ds(k * size, size)
+        chunks.append(pltpu.make_async_copy(x_hbm.at[there, :], x_ref.at[here, :], sems.at[k]))
+        chunks[k].start()
     get_tid.wait()
     target = jnp.where(core == 0, tid_ref[0:1, :], tid_ref[1:2, :])
     xn_ref[:, d:] = digits(jnp.broadcast_to(target, (8, rows)).T[:, :1])
     get_gain.wait()
-    get_x.wait()
-    feats = x_ref[...].astype(jnp.float32)
-    scale = lax.rsqrt(jnp.mean(feats * feats, axis=-1, keepdims=True) + 1e-06)
-    xn_ref[:, :d] = (feats * scale * gain_ref[...]).astype(jnp.bfloat16)
+    for k in range(CHUNKS):
+        chunks[k].wait()
+        here = pl.ds(k * size, size)
+        feats = x_ref[here, :].astype(jnp.float32)
+        scale = lax.rsqrt(jnp.mean(feats * feats, axis=-1, keepdims=True) + 1e-06)
+        xn_ref[here, :d] = (feats * scale * gain_ref[...]).astype(jnp.bfloat16)
     starts, sizes = segments(rows)
     for ref, flip in ((cw_ref, 0), (ccw_ref, 1)):
         down = plane != flip
@@ -119,7 +131,7 @@
             pltpu.VMEM((rows, d), jnp.bfloat16),
             pltpu.VMEM((1, d), jnp.float32),
             pltpu.VMEM((2, rows), jnp.int32),
-            pltpu.SemaphoreType.DMA((3,)),
+            pltpu.SemaphoreType.DMA((CHUNKS + 2,)),
         ],
         compiler_params=pltpu.CompilerParams(vmem_limit_bytes=VMEM_BYTES),
         name="norm",
@@ -151,7 +163,8 @@
     n = len(metas)
     piece_refs, (w0_ref, w1_ref), refs = refs[:n], refs[n : n + 2], refs[n + 2 :]
     if tail:
-        stat_refs, (packed_ref, x_s, l_s, t_s, out_ref) = refs[: len(earlier)], refs[len(earlier) :]
+        stat_refs, refs = refs[: len(earlier)], refs[len(earlier) :]
+        packed_ref, x_s, l_s, t_s, out_ref = refs
     else:
         out_ref, x_s, l_s, t_s = refs
     req, tp = lax.axis_index("req"), lax.axis_index("tp")
@@ -173,7 +186,7 @@
     column = lax.broadcasted_iota(jnp.int32, (1, vdev), 1)
     ids0 = (column + (req * n_tp + tp) * vdev).astype(jnp.float32)
     ids1 = (column + (req * n_tp + (tp ^ 1)) * vdev).astype(jnp.float32)
-    step = 16
+    step = math.gcd(total, 32)
 
     def body(i, _):
         here = pl.ds(pl.multiple_of(i * step, step), step)
@@ -186,12 +199,20 @@
         hit0 = jnp.where(ids0 == target, logits[:, :vdev], 0.0)
         hit1 = jnp.where(ids1 == target, logits[:, vdev:], 0.0)
         picked = jnp.sum(hit0 + hit1, axis=1, keepdims=True)
-        out_ref[here, :] = jnp.where(
-            lane == 0, top, jnp.where(lane == 1, weight_sum, jnp.where(lane == 2, weighted, picked))
-        )
+        values = jnp.where(lane == 3, picked, 0.0)
+        values = jnp.where(lane == 2, weighted, values)
+        values = jnp.where(lane == 1, weight_sum, values)
+        out_ref[here, :] = jnp.where(lane == 0, top, values)
         return 0
 
-    lax.fori_loop(0, total // step, body, 0, unroll=4)
+    lax.fori_loop(0, total // step, body, 0, unroll=total // step)
+    at = 0
+    for turn, hops, part in (p for parts in metas for p in parts):
+        here = pl.ds(at, part_rows(part, rows))
+        at += part_rows(part, rows)
+        if hops:
+            first = STATS * shard_index(turn, hops, n_req)
+            out_ref[here, :] = pltpu.roll(out_ref[here, :], first, 1)
     if tail:
         pack_stats(earlier + (metas,), (*stat_refs, out_ref), packed_ref, n_req, n_tp, rows)
 
@@ -200,29 +221,28 @@
     plane = lax.axis_index("tp") // 2
     place = ring_place(lax.axis_index("req"), n_req)
     _, sizes = segments(rows)
-    shards = {}
+    own, found = None, [[] for _ in sizes]
     for pieces, ref in zip(metas, stat_refs):
         at = 0
         for turn, hops, part in (p for parts in pieces for p in parts):
             for j in PARTS[part]:
-                shards.setdefault((turn, hops) if 2 * hops != n_req else (0, hops), []).append(
-                    (turn, j, ref[pl.ds(at, sizes[j]), :])
-                )
+                here = ref[pl.ds(at, sizes[j]), :]
                 at += sizes[j]
-    for (turn, hops), found in shards.items():
-        if turn == 0 and hops:
-            up = {j if t > 0 else 5 - j: v for t, j, v in found}
-        else:
-            up = {j: v for _, j, v in found}
-        ordered = jnp.concatenate([up[j] for j in range(6)], axis=0)
-        if hops:
-            flipped = jnp.concatenate([up[5 - j] for j in range(6)], axis=0)
-            down = plane != (0 if turn >= 0 else 1)
-            ordered = jnp.where(down, flipped, ordered)
-        source = ring_req((place - (turn or 1) * hops + n_req) % n_req, n_req)
-        packed = ordered.T[:STATS, :]
+                if hops:
+                    found[j if turn > 0 else 5 - j].append(here)
+                else:
+                    own = ref[...]
+    found = [functools.reduce(jnp.add, values) for values in found]
+    total = own + jnp.where(
+        plane == 0, jnp.concatenate(found, axis=0), jnp.concatenate(found[::-1], axis=0)
+    )
+    lanes = total.T
+    turns = [(0, 0)] + [(1, h) for h in range(1, n_req // 2 + 1)]
+    for turn, hops in turns + [(-1, h) for h in range(1, n_req // 2)]:
+        source = ring_req((place - turn * hops + n_req) % n_req, n_req)
+        k = STATS * shard_index(turn, hops, n_req)
         for t in range(n_tp):
-            packed_ref[source * n_tp + t] = packed
+            packed_ref[source * n_tp + t] = lanes[k : k + STATS, :]
 
 
 def stats_of(pieces, metas, w0, w1, n_req, n_tp, rows, earlier=(), stats=(), tail=False):

time: 61.1 us -> 59.1 us (0.967)
  Pallas kernels: 16.1 us -> 13.4 us
  waiting for transfers between devices: 20.1 us -> 20.9 us
    pallas_call x6, Pallas kernels: 13.9 us -> 11.2 us  [stats_of(): pl.pallas_call(functools.partial(stats_kernel, metas, n_req, n_tp, rows,...]
    ppermute x14, waiting for transfers between devices: 12.5 us -> 14.1 us  [send(): return lax.ppermute(value, AXES, pairs)]
    all_to_all x1, waiting for transfers between devices: 7.58 us -> 6.76 us  [per_device(): received = lax.all_to_all(packed, AXES, 0, 0, tiled=True)]
  transfers between devices with their start and end apart: 15 -> 15, of which waited for: 6 -> 7; matrix products, arithmetic and copies ran while one was open for 0% -> 0% of each run, Pallas kernels for 19% -> 16%
where the time goes in v5:
time: 59.1 us; the launch traced here: 58.8 us
  starting transfers between devices  21.3 us (36%)
  waiting for transfers between devices  20.9 us (35%)
  Pallas kernels  13.4 us (23%)
  local copies, waits for them, and re-layouts  1.89 us (3%)
  between operations  1.34 us (2%)
    ppermute x14, starting transfers between devices, send(): return lax.ppermute(value, AXES, pairs)  16.5 us
    ppermute x14, waiting for transfers between devices, send(): return lax.ppermute(value, AXES, pairs)  14.1 us
    pallas_call x6, Pallas kernels, stats_of(): pl.pallas_call(functools.partial(stats_kernel, metas, n_req, n_tp, rows,...  11.2 us
    all_to_all x1, waiting for transfers between devices, per_device(): received = lax.all_to_all(packed, AXES, 0, 0, tiled=True)  6.76 us
    all_to_all x1, starting transfers between devices, per_device(): received = lax.all_to_all(packed, AXES, 0, 0, tiled=True)  4.88 us
    unnamed x4, local copies, waits for them, and re-layouts  1.89 us
    pallas_call x1, Pallas kernels, norm_rows(): pl.pallas_call(norm_kernel, out_shape=[jax.ShapeDtypeStruct(s, jnp.bfloat...  1.4 us
  transfers between devices with their start and end apart: 15, of which 7 were waited for; matrix products, arithmetic and copies ran while one was open for 0% of the time, Pallas kernels for 16%

profile of v5, /device:TPU:0, one launch (start us, length us, event | category | flops | bytes accessed | tf_op | source)
XLA Modules:
  0.0 58.8 jit_solution(7956397747447944267)
XLA Ops:
  0.6 1.4 %norm.1 = (bf16[128,2176]{1,0:T(8,128)(2,1)S(1)}, bf16[80,2176]{1,0:T(8,128)(2,1)S(1)}, bf16[80,2176]{1,0:T(8,128)(2,1)S(1)}) custom-call(bf16[256,2048]{1,0:T(8,128)(2,1)} %x_hbm.1, f32[1,2048]{1,0:T(1,128)} %bitcast.6, s32[2,128]{1,0:T(2,128)} %bitcast.7), custom_call_target="tpu_custom_call" | custom-call | tf_op jit(solution)/shard_map/norm/pallas_call | solution.py:126
  2.0 0.5 collective-permute-start.1
  2.6 2.6 %collective-permute-start = (bf16[80,2176]{1,0:T(8,128)(2,1)S(1)}, bf16[80,2176]{1,0:T(8,128)(2,1)S(1)}, u32[]{:S(2)}, u32[]{:S(2)}) collective-permute-start(bf16[80,2176]{1,0:T(8,128)(2,1)S(1)} %get-tuple-element.31), channel_id=1, source_target_pairs={{0,8},{1,9},{2,10},{3,11},{8,16},{9,17},{10,18},{11,19},{16,24},{1... | collective-permute-start | bytes 1044488 | tf_op jit(solution)/shard_map/ppermute | solution.py:320
  5.2 0.0 collective-permute-start.3
  5.2 2.9 %collective-permute-done.1.refs_2_.refs_3_.refs_4_ = bf16[2048,768]{1,0:T(8,128)(2,1)S(1)} collective-permute-done((bf16[2048,768]{1,0:T(8,128)(2,1)}, bf16[2048,768]{1,0:T(8,128)(2,1)S(1)}, u32[]{:S(2)}, u32[]{:S(2)}) %collective-permute-start.1) | collective-permute-done | bytes 3145760 | tf_op jit(solution)/shard_map/ppermute | solution.py:320
  8.1 1.9 %copy-done = bf16[2048,768]{1,0:T(8,128)(2,1)S(1)} copy-done((bf16[2048,768]{1,0:T(8,128)(2,1)S(1)}, bf16[2048,768]{1,0:T(8,128)(2,1)}, u32[]{:S(2)}) %copy-start) | copy-done | bytes 3145752
  9.9 1.3 %stats.5.refs_5_ = f32[128,128]{1,0:T(8,128)S(1)} custom-call(bf16[128,2176]{1,0:T(8,128)(2,1)S(1)} %get-tuple-element.33.refs_0_, bf16[2048,768]{1,0:T(8,128)(2,1)S(1)} %copy-done, bf16[2048,768]{1,0:T(8,128)(2,1)S(1)} %collective-permute-done.1.refs_2_.refs_3_.refs_4_), custom_call_target="tpu_custom_call" | custom-call | flops 805306368 | bytes 6291456 | tf_op jit(solution)/shard_map/stats/pallas_call | solution.py:252
  11.3 2.6 %collective-permute-done.refs_0_ = bf16[80,2176]{1,0:T(8,128)(2,1)S(1)} collective-permute-done((bf16[80,2176]{1,0:T(8,128)(2,1)S(1)}, bf16[80,2176]{1,0:T(8,128)(2,1)S(1)}, u32[]{:S(2)}, u32[]{:S(2)}) %collective-permute-start) | collective-permute-done | bytes 348192 | tf_op jit(solution)/shard_map/ppermute | solution.py:320
  13.9 1.8 %collective-permute-start.2 = (bf16[80,2176]{1,0:T(8,128)(2,1)S(1)}, bf16[80,2176]{1,0:T(8,128)(2,1)S(1)}, u32[]{:S(2)}, u32[]{:S(2)}) collective-permute-start(bf16[80,2176]{1,0:T(8,128)(2,1)S(1)} %collective-permute-done.refs_0_), channel_id=1, source_target_pairs={{0,8},{1,9},{2,10},{3,11},{8,16},{9,17},{10,18},{11,19},{16,24},{1... | collective-permute-start | bytes 1044488 | tf_op jit(solution)/shard_map/ppermute | solution.py:320
  15.7 0.2 collective-permute-start.4
  15.9 1.8 %collective-permute-start.9 = (bf16[96,2176]{1,0:T(8,128)(2,1)S(1)}, bf16[96,2176]{1,0:T(8,128)(2,1)S(1)}, u32[]{:S(2)}, u32[]{:S(2)}) collective-permute-start(bf16[96,2176]{1,0:T(8,128)(2,1)S(1)} %cut.8), channel_id=1, source_target_pairs={{0,2},{1,3},{2,0},{3,1},{4,6},{5,7},{6,4},{7,5},{8,10},{9,11},{10,... | collective-permute-start | bytes 1253384 | tf_op jit(solution)/shard_map/ppermute | solution.py:320
  17.8 1.6 %stats.6.refs_6_ = f32[160,128]{1,0:T(8,128)S(1)} custom-call(bf16[80,2176]{1,0:T(8,128)(2,1)S(1)} %collective-permute-done.refs_0_, bf16[80,2176]{1,0:T(8,128)(2,1)S(1)} %collective-permute-done.3.refs_1_, bf16[2048,768]{1,0:T(8,128)(2,1)S(1)} %copy-done.1, bf16[2048,768]{1,0:T(8,128)(2,1)S(1)} %collective-permute-done.1.refs_2_.refs_3_.refs_4_), custom_call_target="tpu_custom_call" | custom-call | flops 1006632960 | bytes 6291456 | tf_op jit(solution)/shard_map/stats/pallas_call | solution.py:252
  19.4 4.4 %collective-permute-done.2.refs_0_ = bf16[80,2176]{1,0:T(8,128)(2,1)S(1)} collective-permute-done((bf16[80,2176]{1,0:T(8,128)(2,1)S(1)}, bf16[80,2176]{1,0:T(8,128)(2,1)S(1)}, u32[]{:S(2)}, u32[]{:S(2)}) %collective-permute-start.2) | collective-permute-done | bytes 348192 | tf_op jit(solution)/shard_map/ppermute | solution.py:320
  23.8 1.6 %collective-permute-start.8 = (bf16[80,2176]{1,0:T(8,128)(2,1)S(1)}, bf16[80,2176]{1,0:T(8,128)(2,1)S(1)}, u32[]{:S(2)}, u32[]{:S(2)}) collective-permute-start(bf16[80,2176]{1,0:T(8,128)(2,1)S(1)} %collective-permute-done.2.refs_0_), channel_id=1, source_target_pairs={{0,8},{1,9},{2,10},{3,11},{8,16},{9,17},{10,18},{11,19},{16,24},{1... | collective-permute-start | bytes 1044488 | tf_op jit(solution)/shard_map/ppermute | solution.py:320
  25.4 0.4 collective-permute-start.10
  25.8 1.6 %collective-permute-start.5 = (bf16[96,2176]{1,0:T(8,128)(2,1)S(1)}, bf16[96,2176]{1,0:T(8,128)(2,1)S(1)}, u32[]{:S(2)}, u32[]{:S(2)}) collective-permute-start(bf16[96,2176]{1,0:T(8,128)(2,1)S(1)} %cut.6), channel_id=1, source_target_pairs={{0,2},{1,3},{2,0},{3,1},{4,6},{5,7},{6,4},{7,5},{8,10},{9,11},{10,... | collective-permute-start | bytes 1253384 | tf_op jit(solution)/shard_map/ppermute | solution.py:320
  27.5 2.3 %stats.7.refs_7_ = f32[256,128]{1,0:T(8,128)S(1)} custom-call(bf16[80,2176]{1,0:T(8,128)(2,1)S(1)} %collective-permute-done.2.refs_0_, bf16[80,2176]{1,0:T(8,128)(2,1)S(1)} %collective-permute-done.4.refs_1_, bf16[96,2176]{1,0:T(8,128)(2,1)S(1)} %collective-permute-done.9.refs_2_, bf16[2048,768]{1,0:T(8,128)(2,1)S(1)} %copy-done.1, ...), custom_call_target="tpu_custom_call" | custom-call | flops 1610612736 | bytes 6291456 | tf_op jit(solution)/shard_map/stats/pallas_call | solution.py:252
  29.8 3.0 %collective-permute-done.8.refs_0_ = bf16[80,2176]{1,0:T(8,128)(2,1)S(1)} collective-permute-done((bf16[80,2176]{1,0:T(8,128)(2,1)S(1)}, bf16[80,2176]{1,0:T(8,128)(2,1)S(1)}, u32[]{:S(2)}, u32[]{:S(2)}) %collective-permute-start.8) | collective-permute-done | bytes 348192 | tf_op jit(solution)/shard_map/ppermute | solution.py:320
  32.8 1.1 %collective-permute-done.10.refs_1_.refs_0_ = bf16[80,2176]{1,0:T(8,128)(2,1)S(1)} collective-permute-done((bf16[80,2176]{1,0:T(8,128)(2,1)S(1)}, bf16[80,2176]{1,0:T(8,128)(2,1)S(1)}, u32[]{:S(2)}, u32[]{:S(2)}) %collective-permute-start.10) | collective-permute-done | bytes 348192 | tf_op jit(solution)/shard_map/ppermute | solution.py:320
  33.9 1.6 %collective-permute-start.13 = (bf16[64,2176]{1,0:T(8,128)(2,1)S(1)}, bf16[64,2176]{1,0:T(8,128)(2,1)S(1)}, u32[]{:S(2)}, u32[]{:S(2)}) collective-permute-start(bf16[64,2176]{1,0:T(8,128)(2,1)S(1)} %cut.11), channel_id=1, source_target_pairs={{0,8},{1,9},{2,10},{3,11},{8,16},{9,17},{10,18},{11,19},{16,24},{1... | collective-permute-start | bytes 835592 | tf_op jit(solution)/shard_map/ppermute | solution.py:320
  35.6 0.5 collective-permute-start.12
  36.1 1.6 %collective-permute-start.11 = (bf16[64,2176]{1,0:T(8,128)(2,1)S(1)}, bf16[64,2176]{1,0:T(8,128)(2,1)S(1)}, u32[]{:S(2)}, u32[]{:S(2)}) collective-permute-start(bf16[64,2176]{1,0:T(8,128)(2,1)S(1)} %cut.9), channel_id=1, source_target_pairs={{0,2},{1,3},{2,0},{3,1},{4,6},{5,7},{6,4},{7,5},{8,10},{9,11},{10,... | collective-permute-start | bytes 835592 | tf_op jit(solution)/shard_map/ppermute | solution.py:320
  37.7 1.6 %collective-permute-start.6 = (bf16[16,2176]{1,0:T(8,128)(2,1)S(1)}, bf16[16,2176]{1,0:T(8,128)(2,1)S(1)}, u32[]{:S(2)}, u32[]{:S(2)}) collective-permute-start(bf16[16,2176]{1,0:T(8,128)(2,1)S(1)} %get-tuple-element.42), channel_id=1, source_target_pairs={{0,8},{1,9},{2,10},{3,11},{8,16},{9,17},{10,18},{11,19},{16,24},{1... | collective-permute-start | bytes 208904 | tf_op jit(solution)/shard_map/ppermute | solution.py:320
  39.4 0.4 collective-permute-start.7
  39.8 2.3 %stats.8.refs_8_ = f32[256,128]{1,0:T(8,128)S(1)} custom-call(bf16[80,2176]{1,0:T(8,128)(2,1)S(1)} %collective-permute-done.8.refs_0_, bf16[80,2176]{1,0:T(8,128)(2,1)S(1)} %collective-permute-done.10.refs_1_.refs_0_, bf16[96,2176]{1,0:T(8,128)(2,1)S(1)} %collective-permute-done.5.refs_0_.refs_2_, bf16[2048,768]{1,0:T(8,128)(2,1)S(1)} %copy-done.1, ...), custom_call_target="tpu_custom_call" | custom-call | flops 1610612736 | bytes 6291456 | tf_op jit(solution)/shard_map/stats/pallas_call | solution.py:252
  42.1 0.1 collective-permute-done.12.refs_1_
  42.2 1.4 %stats.9.refs_9_ = f32[128,128]{1,0:T(8,128)S(1)} custom-call(bf16[64,2176]{1,0:T(8,128)(2,1)S(1)} %collective-permute-done.13.refs_0_, bf16[64,2176]{1,0:T(8,128)(2,1)S(1)} %collective-permute-done.12.refs_1_, bf16[2048,768]{1,0:T(8,128)(2,1)S(1)} %copy-done.1, bf16[2048,768]{1,0:T(8,128)(2,1)S(1)} %collective-permute-done.1.refs_2_.refs_3_.refs_4_), custom_call_target="tpu_custom_call" | custom-call | flops 805306368 | bytes 6291456 | tf_op jit(solution)/shard_map/stats/pallas_call | solution.py:252
  43.6 0.0 collective-permute-done.7.refs_1_
  43.7 2.2 %stats_last.1 = f32[32,4,128]{2,1,0:T(4,128)} custom-call(bf16[16,2176]{1,0:T(8,128)(2,1)S(1)} %collective-permute-done.6.refs_0_, bf16[16,2176]{1,0:T(8,128)(2,1)S(1)} %collective-permute-done.7.refs_1_, bf16[64,2176]{1,0:T(8,128)(2,1)S(1)} %collective-permute-done.11.refs_2_, bf16[2048,768]{1,0:T(8,128)(2,1)S(1)} %copy-done.1, ...), custom_call_target="tpu_custom_call" | custom-call | flops 603979776 | bytes 6291456 | tf_op jit(solution)/shard_map/stats_last/pallas_call | solution.py:252
  45.8 4.9 %all-to-all-start = ((f32[32,4,128]{2,1,0:T(4,128)}), f32[32,4,128]{2,1,0:T(4,128)S(1)}, u32[]{:S(2)}, u32[]{:S(2)}) async-start(f32[32,4,128]{2,1,0:T(4,128)} %stats_last.1), calls=%async_computation | async-start | bytes 131072 | tf_op jit(solution)/shard_map/all_to_all | solution.py:368
  51.4 6.8 %all-to-all-done.r_ref = f32[32,4,128]{2,1,0:T(4,128)S(1)} async-done(((f32[32,4,128]{2,1,0:T(4,128)}), f32[32,4,128]{2,1,0:T(4,128)S(1)}, u32[]{:S(2)}, u32[]{:S(2)}) %all-to-all-start) | async-done | bytes 65568 | tf_op jit(solution)/shard_map/all_to_all | solution.py:368
  58.1 0.7 %finish.1 = (f32[2,128]{1,0:T(2,128)}, f32[2,128]{1,0:T(2,128)}, f32[1,1]{1,0:T(1,128)}, f32[1,1]{1,0:T(1,128)}) custom-call(f32[32,4,128]{2,1,0:T(4,128)S(1)} %all-to-all-done.r_ref, s32[1]{0:T(128)S(6)} %copy.9.len_ref), custom_call_target="tpu_custom_call" | custom-call | tf_op jit(solution)/shard_map/finish/pallas_call | solution.py:296
  (16 shorter events, 0.2 us)
Async XLA Ops:
  2.0 6.0 %collective-permute-start.1 = (bf16[2048,768]{1,0:T(8,128)(2,1)}, bf16[2048,768]{1,0:T(8,128)(2,1)S(1)}, u32[]{:S(2)}, u32[]{:S(2)}) collective-permute-start(bf16[2048,768]{1,0:T(8,128)(2,1)} %refs_3_.5), channel_id=1, source_target_pairs={{0,1},{1,0},{2,3},{3,2},{4,5},{5,4},{6,7},{7,6},{8,9},{9,8},{10,11... | collective-permute-start | bytes 9437192 | tf_op jit(solution)/shard_map/ppermute | solution.py:320
  2.6 11.3 %collective-permute-start = (bf16[80,2176]{1,0:T(8,128)(2,1)S(1)}, bf16[80,2176]{1,0:T(8,128)(2,1)S(1)}, u32[]{:S(2)}, u32[]{:S(2)}) collective-permute-start(bf16[80,2176]{1,0:T(8,128)(2,1)S(1)} %get-tuple-element.31), channel_id=1, source_target_pairs={{0,8},{1,9},{2,10},{3,11},{8,16},{9,17},{10,18},{11,19},{16,24},{1... | collective-permute-start | bytes 1044488 | tf_op jit(solution)/shard_map/ppermute | solution.py:320
  5.2 10.5 %collective-permute-start.3 = (bf16[80,2176]{1,0:T(8,128)(2,1)S(1)}, bf16[80,2176]{1,0:T(8,128)(2,1)S(1)}, u32[]{:S(2)}, u32[]{:S(2)}) collective-permute-start(bf16[80,2176]{1,0:T(8,128)(2,1)S(1)} %get-tuple-element.36), channel_id=1, source_target_pairs={{0,4},{1,5},{2,6},{3,7},{8,0},{9,1},{10,2},{11,3},{16,8},{17,9},{1... | collective-permute-start | bytes 1044488 | tf_op jit(solution)/shard_map/ppermute | solution.py:320
  8.1 1.9 %copy-start = (bf16[2048,768]{1,0:T(8,128)(2,1)S(1)}, bf16[2048,768]{1,0:T(8,128)(2,1)}, u32[]{:S(2)}) copy-start(bf16[2048,768]{1,0:T(8,128)(2,1)} %refs_3_.5) | copy-start | bytes 9437188
  9.9 7.8 %copy-start.1 = (bf16[2048,768]{1,0:T(8,128)(2,1)S(1)}, bf16[2048,768]{1,0:T(8,128)(2,1)}, u32[]{:S(2)}) copy-start(bf16[2048,768]{1,0:T(8,128)(2,1)} %refs_3_.5) | copy-start | bytes 9437188
  13.9 9.9 %collective-permute-start.2 = (bf16[80,2176]{1,0:T(8,128)(2,1)S(1)}, bf16[80,2176]{1,0:T(8,128)(2,1)S(1)}, u32[]{:S(2)}, u32[]{:S(2)}) collective-permute-start(bf16[80,2176]{1,0:T(8,128)(2,1)S(1)} %collective-permute-done.refs_0_), channel_id=1, source_target_pairs={{0,8},{1,9},{2,10},{3,11},{8,16},{9,17},{10,18},{11,19},{16,24},{1... | collective-permute-start | bytes 1044488 | tf_op jit(solution)/shard_map/ppermute | solution.py:320
  15.7 9.7 %collective-permute-start.4 = (bf16[80,2176]{1,0:T(8,128)(2,1)S(1)}, bf16[80,2176]{1,0:T(8,128)(2,1)S(1)}, u32[]{:S(2)}, u32[]{:S(2)}) collective-permute-start(bf16[80,2176]{1,0:T(8,128)(2,1)S(1)} %collective-permute-done.3.refs_1_), channel_id=1, source_target_pairs={{0,4},{1,5},{2,6},{3,7},{8,0},{9,1},{10,2},{11,3},{16,8},{17,9},{1... | collective-permute-start | bytes 1044488 | tf_op jit(solution)/shard_map/ppermute | solution.py:320
  15.9 11.5 %collective-permute-start.9 = (bf16[96,2176]{1,0:T(8,128)(2,1)S(1)}, bf16[96,2176]{1,0:T(8,128)(2,1)S(1)}, u32[]{:S(2)}, u32[]{:S(2)}) collective-permute-start(bf16[96,2176]{1,0:T(8,128)(2,1)S(1)} %cut.8), channel_id=1, source_target_pairs={{0,2},{1,3},{2,0},{3,1},{4,6},{5,7},{6,4},{7,5},{8,10},{9,11},{10,... | collective-permute-start | bytes 1253384 | tf_op jit(solution)/shard_map/ppermute | solution.py:320
  23.8 9.1 %collective-permute-start.8 = (bf16[80,2176]{1,0:T(8,128)(2,1)S(1)}, bf16[80,2176]{1,0:T(8,128)(2,1)S(1)}, u32[]{:S(2)}, u32[]{:S(2)}) collective-permute-start(bf16[80,2176]{1,0:T(8,128)(2,1)S(1)} %collective-permute-done.2.refs_0_), channel_id=1, source_target_pairs={{0,8},{1,9},{2,10},{3,11},{8,16},{9,17},{10,18},{11,19},{16,24},{1... | collective-permute-start | bytes 1044488 | tf_op jit(solution)/shard_map/ppermute | solution.py:320
  25.4 8.5 %collective-permute-start.10 = (bf16[80,2176]{1,0:T(8,128)(2,1)S(1)}, bf16[80,2176]{1,0:T(8,128)(2,1)S(1)}, u32[]{:S(2)}, u32[]{:S(2)}) collective-permute-start(bf16[80,2176]{1,0:T(8,128)(2,1)S(1)} %collective-permute-done.4.refs_1_), channel_id=1, source_target_pairs={{0,4},{1,5},{2,6},{3,7},{8,0},{9,1},{10,2},{11,3},{16,8},{17,9},{1... | collective-permute-start | bytes 1044488 | tf_op jit(solution)/shard_map/ppermute | solution.py:320
  25.8 11.9 %collective-permute-start.5 = (bf16[96,2176]{1,0:T(8,128)(2,1)S(1)}, bf16[96,2176]{1,0:T(8,128)(2,1)S(1)}, u32[]{:S(2)}, u32[]{:S(2)}) collective-permute-start(bf16[96,2176]{1,0:T(8,128)(2,1)S(1)} %cut.6), channel_id=1, source_target_pairs={{0,2},{1,3},{2,0},{3,1},{4,6},{5,7},{6,4},{7,5},{8,10},{9,11},{10,... | collective-permute-start | bytes 1253384 | tf_op jit(solution)/shard_map/ppermute | solution.py:320
  33.9 8.2 %collective-permute-start.13 = (bf16[64,2176]{1,0:T(8,128)(2,1)S(1)}, bf16[64,2176]{1,0:T(8,128)(2,1)S(1)}, u32[]{:S(2)}, u32[]{:S(2)}) collective-permute-start(bf16[64,2176]{1,0:T(8,128)(2,1)S(1)} %cut.11), channel_id=1, source_target_pairs={{0,8},{1,9},{2,10},{3,11},{8,16},{9,17},{10,18},{11,19},{16,24},{1... | collective-permute-start | bytes 835592 | tf_op jit(solution)/shard_map/ppermute | solution.py:320
  35.6 6.6 %collective-permute-start.12 = (bf16[64,2176]{1,0:T(8,128)(2,1)S(1)}, bf16[64,2176]{1,0:T(8,128)(2,1)S(1)}, u32[]{:S(2)}, u32[]{:S(2)}) collective-permute-start(bf16[64,2176]{1,0:T(8,128)(2,1)S(1)} %cut.10), channel_id=1, source_target_pairs={{0,4},{1,5},{2,6},{3,7},{8,0},{9,1},{10,2},{11,3},{16,8},{17,9},{1... | collective-permute-start | bytes 835592 | tf_op jit(solution)/shard_map/ppermute | solution.py:320
  36.1 7.5 %collective-permute-start.11 = (bf16[64,2176]{1,0:T(8,128)(2,1)S(1)}, bf16[64,2176]{1,0:T(8,128)(2,1)S(1)}, u32[]{:S(2)}, u32[]{:S(2)}) collective-permute-start(bf16[64,2176]{1,0:T(8,128)(2,1)S(1)} %cut.9), channel_id=1, source_target_pairs={{0,2},{1,3},{2,0},{3,1},{4,6},{5,7},{6,4},{7,5},{8,10},{9,11},{10,... | collective-permute-start | bytes 835592 | tf_op jit(solution)/shard_map/ppermute | solution.py:320
  37.7 5.9 %collective-permute-start.6 = (bf16[16,2176]{1,0:T(8,128)(2,1)S(1)}, bf16[16,2176]{1,0:T(8,128)(2,1)S(1)}, u32[]{:S(2)}, u32[]{:S(2)}) collective-permute-start(bf16[16,2176]{1,0:T(8,128)(2,1)S(1)} %get-tuple-element.42), channel_id=1, source_target_pairs={{0,8},{1,9},{2,10},{3,11},{8,16},{9,17},{10,18},{11,19},{16,24},{1... | collective-permute-start | bytes 208904 | tf_op jit(solution)/shard_map/ppermute | solution.py:320
  39.4 4.3 %collective-permute-start.7 = (bf16[16,2176]{1,0:T(8,128)(2,1)S(1)}, bf16[16,2176]{1,0:T(8,128)(2,1)S(1)}, u32[]{:S(2)}, u32[]{:S(2)}) collective-permute-start(bf16[16,2176]{1,0:T(8,128)(2,1)S(1)} %get-tuple-element.43), channel_id=1, source_target_pairs={{0,4},{1,5},{2,6},{3,7},{8,0},{9,1},{10,2},{11,3},{16,8},{17,9},{1... | collective-permute-start | bytes 208904 | tf_op jit(solution)/shard_map/ppermute | solution.py:320
  45.8 12.3 %all-to-all-start = ((f32[32,4,128]{2,1,0:T(4,128)}), f32[32,4,128]{2,1,0:T(4,128)S(1)}, u32[]{:S(2)}, u32[]{:S(2)}) async-start(f32[32,4,128]{2,1,0:T(4,128)} %stats_last.1), calls=%async_computation | async-start | bytes 131072 | tf_op jit(solution)/shard_map/all_to_all | solution.py:368

commit v6 on v5

--- a/solution.py
+++ b/solution.py
@@ -12,7 +12,8 @@
 LANES = 128
 STATS = 4
 DIGIT_BITS = 7
-CHUNKS = 1
+NOTHING = -1e30
+EARLY_ROWS = 32
 VMEM_BYTES = 10 * 1024 * 1024
 
 
@@ -82,31 +83,72 @@
     return jnp.sum(ext.astype(jnp.float32) * weight, axis=1, keepdims=True)
 
 
-def norm_kernel(x_hbm, gain_hbm, tid_hbm, xn_ref, cw_ref, ccw_ref, x_ref, gain_ref, tid_ref, sems):
+def row_stats(logits, target, ids):
+    lane = lax.broadcasted_iota(jnp.int32, (1, LANES), 1)
+    top = jnp.max(logits, axis=1, keepdims=True)
+    shifted = jnp.exp(logits - top)
+    weight_sum = jnp.sum(shifted, axis=1, keepdims=True)
+    weighted = jnp.sum(shifted * logits, axis=1, keepdims=True)
+    width = logits.shape[1] // len(ids)
+    hits = [
+        jnp.where(part == target, logits[:, k * width : (k + 1) * width], 0.0)
+        for k, part in enumerate(ids)
+    ]
+    picked = jnp.sum(functools.reduce(jnp.add, hits), axis=1, keepdims=True)
+    values = jnp.where(lane == 3, picked, 0.0)
+    values = jnp.where(lane == 2, weighted, values)
+    values = jnp.where(lane == 1, weight_sum, values)
+    return jnp.where(lane == 0, top, values)
+
+
+def vocab_ids(vdev, owner):
+    column = lax.broadcasted_iota(jnp.int32, (1, vdev), 1)
+    return (column + owner * vdev).astype(jnp.float32)
+
+
+def norm_kernel(
+    n_tp, x_hbm, gain_hbm, tid_hbm, head_hbm, xn_ref, cw_ref, ccw_ref, early_ref,
+    x_ref, gain_ref, tid_ref, head_ref, sems,
+):
     rows, d = x_ref.shape
-    tp = lax.axis_index("tp")
+    vdev = head_ref.shape[1]
+    req, tp = lax.axis_index("req"), lax.axis_index("tp")
     core, plane = tp % 2, tp // 2
-    size = rows // CHUNKS
-    get_gain = pltpu.make_async_copy(gain_hbm, gain_ref, sems.at[CHUNKS])
-    get_tid = pltpu.make_async_copy(tid_hbm, tid_ref, sems.at[CHUNKS + 1])
+    mine = pl.ds(pl.multiple_of(core * rows, rows), rows)
+    get_x = pltpu.make_async_copy(x_hbm.at[mine, :], x_ref, sems.at[0])
+    get_gain = pltpu.make_async_copy(gain_hbm, gain_ref, sems.at[1])
+    get_tid = pltpu.make_async_copy(tid_hbm, tid_ref, sems.at[2])
+    get_x.start()
     get_gain.start()
     get_tid.start()
-    chunks = []
-    for k in range(CHUNKS):
-        there = pl.ds(pl.multiple_of(core * rows + k * size, size), size)
-        here = pl.ds(k * size, size)
-        chunks.append(pltpu.make_async_copy(x_hbm.at[there, :], x_ref.at[here, :], sems.at[k]))
-        chunks[k].start()
     get_tid.wait()
     target = jnp.where(core == 0, tid_ref[0:1, :], tid_ref[1:2, :])
-    xn_ref[:, d:] = digits(jnp.broadcast_to(target, (8, rows)).T[:, :1])
+    target = jnp.broadcast_to(target, (8, rows)).T[:, :1]
+    xn_ref[:, d:] = digits(target)
     get_gain.wait()
-    for k in range(CHUNKS):
-        chunks[k].wait()
-        here = pl.ds(k * size, size)
-        feats = x_ref[here, :].astype(jnp.float32)
-        scale = lax.rsqrt(jnp.mean(feats * feats, axis=-1, keepdims=True) + 1e-06)
-        xn_ref[here, :d] = (feats * scale * gain_ref[...]).astype(jnp.bfloat16)
+    get_x.wait()
+    feats = x_ref[...].astype(jnp.float32)
+    scale = lax.rsqrt(jnp.mean(feats * feats, axis=-1, keepdims=True) + 1e-06)
+    xn_ref[:, :d] = (feats * scale * gain_ref[...]).astype(jnp.bfloat16)
+
+    @pl.when(core == 0)
+    def _():
+        lane = lax.broadcasted_iota(jnp.int32, (rows, LANES), 1)
+        early_ref[...] = jnp.where(lane == 0, NOTHING, 0.0)
+
+    @pl.when(core == 1)
+    def _():
+        get_head = pltpu.make_async_copy(head_hbm, head_ref, sems.at[3])
+        get_head.start()
+        get_head.wait()
+        ids = [vocab_ids(vdev, req * n_tp + tp)]
+        for k in range(0, rows, EARLY_ROWS):
+            logits = jnp.dot(
+                xn_ref[k : k + EARLY_ROWS, :d], head_ref[...], preferred_element_type=jnp.float32
+            )
+            wanted = undigits(xn_ref[k : k + EARLY_ROWS, d:])
+            early_ref[k : k + EARLY_ROWS, :] = row_stats(logits, wanted, ids)
+
     starts, sizes = segments(rows)
     for ref, flip in ((cw_ref, 0), (ccw_ref, 1)):
         down = plane != flip
@@ -117,21 +159,22 @@
             at += sizes[j]
 
 
-def norm_rows(hidden, norm_gain, target_ids, rows):
+def norm_rows(hidden, norm_gain, target_ids, head, n_tp, rows):
     d = hidden.shape[1]
     wide = d + LANES
     message = (part_rows("most", rows), wide)
-    shapes = [(rows, wide), message, message]
-    hbm_operands = (hidden, norm_gain.reshape(1, d), target_ids.reshape(2, rows))
+    hbm_operands = (hidden, norm_gain.reshape(1, d), target_ids.reshape(2, rows), head)
     return pl.pallas_call(
-        norm_kernel,
-        out_shape=[jax.ShapeDtypeStruct(s, jnp.bfloat16) for s in shapes],
-        in_specs=[pl.BlockSpec(memory_space=pl.ANY)] * 3,
+        functools.partial(norm_kernel, n_tp),
+        out_shape=[jax.ShapeDtypeStruct(s, jnp.bfloat16) for s in [(rows, wide), message, message]]
+        + [jax.ShapeDtypeStruct((rows, LANES), jnp.float32)],
+        in_specs=[pl.BlockSpec(memory_space=pl.ANY)] * 4,
         scratch_shapes=[
             pltpu.VMEM((rows, d), jnp.bfloat16),
             pltpu.VMEM((1, d), jnp.float32),
             pltpu.VMEM((2, rows), jnp.int32),
-            pltpu.SemaphoreType.DMA((CHUNKS + 2,)),
+            pltpu.VMEM(head.shape, head.dtype),
+            pltpu.SemaphoreType.DMA((4,)),
         ],
         compiler_params=pltpu.CompilerParams(vmem_limit_bytes=VMEM_BYTES),
         name="norm",
@@ -159,9 +202,11 @@
     )(*arrays)
 
 
-def stats_kernel(metas, n_req, n_tp, rows, earlier, tail, *refs):
+def stats_kernel(metas, n_req, n_tp, rows, earlier, tail, first, *refs):
     n = len(metas)
     piece_refs, (w0_ref, w1_ref), refs = refs[:n], refs[n : n + 2], refs[n + 2 :]
+    if first:
+        early_ref, refs = refs[0], refs[1:]
     if tail:
         stat_refs, refs = refs[: len(earlier)], refs[len(earlier) :]
         packed_ref, x_s, l_s, t_s, out_ref = refs
@@ -179,33 +224,33 @@
         t_s[here, :] = undigits(ref[:, d:])
         at += ref.shape[0]
 
+    own = tp % 2 == 0 if first else True
+    ids = [vocab_ids(vdev, req * n_tp + tp), vocab_ids(vdev, req * n_tp + (tp ^ 1))]
     x = x_s[...]
-    l_s[:, :vdev] = jnp.dot(x, w0_ref[...], preferred_element_type=jnp.float32)
     l_s[:, vdev:] = jnp.dot(x, w1_ref[...], preferred_element_type=jnp.float32)
-
-    column = lax.broadcasted_iota(jnp.int32, (1, vdev), 1)
-    ids0 = (column + (req * n_tp + tp) * vdev).astype(jnp.float32)
-    ids1 = (column + (req * n_tp + (tp ^ 1)) * vdev).astype(jnp.float32)
+    if first:
+
+        @pl.when(own)
+        def _():
+            l_s[:, :vdev] = jnp.dot(x_s[...], w0_ref[...], preferred_element_type=jnp.float32)
+
+        @pl.when(jnp.logical_not(own))
+        def _():
+            l_s[:, :vdev] = jnp.full((total, vdev), NOTHING, jnp.float32)
+
+        ids[0] = jnp.where(own, ids[0], -1.0)
+    else:
+        l_s[:, :vdev] = jnp.dot(x, w0_ref[...], preferred_element_type=jnp.float32)
     step = math.gcd(total, 32)
 
     def body(i, _):
         here = pl.ds(pl.multiple_of(i * step, step), step)
-        logits = l_s[here, :]
-        target = t_s[here, :]
-        top = jnp.max(logits, axis=1, keepdims=True)
-        shifted = jnp.exp(logits - top)
-        weight_sum = jnp.sum(shifted, axis=1, keepdims=True)
-        weighted = jnp.sum(shifted * logits, axis=1, keepdims=True)
-        hit0 = jnp.where(ids0 == target, logits[:, :vdev], 0.0)
-        hit1 = jnp.where(ids1 == target, logits[:, vdev:], 0.0)
-        picked = jnp.sum(hit0 + hit1, axis=1, keepdims=True)
-        values = jnp.where(lane == 3, picked, 0.0)
-        values = jnp.where(lane == 2, weighted, values)
-        values = jnp.where(lane == 1, weight_sum, values)
-        out_ref[here, :] = jnp.where(lane == 0, top, values)
+        out_ref[here, :] = row_stats(l_s[here, :], t_s[here, :], ids)
         return 0
 
     lax.fori_loop(0, total // step, body, 0, unroll=total // step)
+    if first:
+        out_ref[...] = merged(out_ref[...], early_ref[...])
     at = 0
     for turn, hops, part in (p for parts in metas for p in parts):
         here = pl.ds(at, part_rows(part, rows))
@@ -215,6 +260,13 @@
             out_ref[here, :] = pltpu.roll(out_ref[here, :], first, 1)
     if tail:
         pack_stats(earlier + (metas,), (*stat_refs, out_ref), packed_ref, n_req, n_tp, rows)
+
+
+def merged(one, two):
+    lane = lax.broadcasted_iota(jnp.int32, (1, LANES), 1)
+    top = jnp.maximum(one[:, :1], two[:, :1])
+    scaled = one * jnp.exp(one[:, :1] - top) + two * jnp.exp(two[:, :1] - top)
+    return jnp.where(lane == 0, top, jnp.where(lane == 3, one + two, scaled))
 
 
 def pack_stats(metas, stat_refs, packed_ref, n_req, n_tp, rows):
@@ -245,12 +297,16 @@
             packed_ref[source * n_tp + t] = lanes[k : k + STATS, :]
 
 
-def stats_of(pieces, metas, w0, w1, n_req, n_tp, rows, earlier=(), stats=(), tail=False):
+def stats_of(
+    pieces, metas, w0, w1, n_req, n_tp, rows, early=(), earlier=(), stats=(), tail=False
+):
     d, vdev = w0.shape
     total = sum(p.shape[0] for p in pieces)
     row_stats = (total, LANES)
     return pl.pallas_call(
-        functools.partial(stats_kernel, metas, n_req, n_tp, rows, earlier, tail),
+        functools.partial(
+            stats_kernel, metas, n_req, n_tp, rows, earlier, tail, len(early) > 0
+        ),
         out_shape=jax.ShapeDtypeStruct(
             (n_req * n_tp, STATS, rows) if tail else row_stats, jnp.float32
         ),
@@ -265,7 +321,7 @@
             flops=4 * total * d * vdev, bytes_accessed=4 * d * vdev, transcendentals=2 * total * vdev
         ),
         name="stats_last" if tail else "stats",
-    )(*pieces, w0, w1, *stats)
+    )(*pieces, w0, w1, *early, *stats)
 
 
 def final_kernel(n_parts, r_ref, len_ref, lp_ref, ent_ref, mean_ref, top_ref):
@@ -319,25 +375,26 @@
     def send(value, pairs):
         return lax.ppermute(value, AXES, pairs)
 
-    def work(items):
+    def work(items, early=()):
         pieces, meta = zip(*items)
-        stats.append(stats_of(pieces, meta, head, other_head, *sizes))
+        stats.append(stats_of(pieces, meta, head, other_head, *sizes, early=early))
         metas.append(meta)
 
     def after(value):
         value, stats[-1] = lax.optimization_barrier((value, stats[-1]))
         return value
 
-    xn, to_cw, to_ccw = norm_rows(hidden_states, norm_gain, target_ids, rows)
-    swapped, xn = lax.optimization_barrier((head, xn))
-    other_head = send(swapped, other_core)
+    other_head = send(head, other_core)
+    xn, to_cw, to_ccw, early = norm_rows(
+        hidden_states, norm_gain, target_ids, head, n_tp, rows
+    )
     items = [(xn, ((0, 0, "all"),))]
     for hops in range(1, n_req // 2):
         next_to_last = 2 * hops + 2 == n_req
         cw, ccw = send(to_cw, cw_pairs), send(to_ccw, ccw_pairs)
         if hops > 1:
             y_next = send(y_message, other_y)
-        work(items)
+        work(items, () if stats else (early,))
         cw, ccw = after(cw), after(ccw)
         items = [(cw, ((1, hops, "most"),)), (ccw, ((-1, hops, "most"),))]
         if hops > 1:

time: 59.1 us -> 57.2 us (0.968)
  local copies, waits for them, and re-layouts: 1.89 us -> 0.01 us
  waiting for transfers between devices: 20.9 us -> 19.2 us
  Pallas kernels: 13.4 us -> 14.3 us
  starting transfers between devices: 21.3 us -> 22.2 us
    unnamed x4 -> x2, local copies, waits for them, and re-layouts: 1.89 us -> 0.01 us
    ppermute x14, waiting for transfers between devices: 14.1 us -> 12.5 us  [send(): return lax.ppermute(value, AXES, pairs)]
    pallas_call x6, Pallas kernels: 11.2 us -> 11.8 us  [stats_of(): pl.pallas_call(functools.partial(stats_kernel, metas, n_req, n_tp, rows,...]
    ppermute x14, starting transfers between devices: 16.5 us -> 17.1 us  [send(): return lax.ppermute(value, AXES, pairs)]
  transfers between devices with their start and end apart: 15 -> 15, of which waited for: 7 -> 10; matrix products, arithmetic and copies ran while one was open for 0% -> 0% of each run, Pallas kernels for 16% -> 20%
where the time goes in v6:
time: 57.2 us; the launch traced here: 57 us
  starting transfers between devices  22.2 us (39%)
  waiting for transfers between devices  19.2 us (34%)
  Pallas kernels  14.3 us (25%)
  between operations  1.35 us (2%)
    ppermute x14, starting transfers between devices, send(): return lax.ppermute(value, AXES, pairs)  17.1 us
    ppermute x14, waiting for transfers between devices, send(): return lax.ppermute(value, AXES, pairs)  12.5 us
    pallas_call x6, Pallas kernels, stats_of(): pl.pallas_call(functools.partial(stats_kernel, metas, n_req, n_tp, rows,...  11.8 us
    all_to_all x1, waiting for transfers between devices, per_device(): received = lax.all_to_all(packed, AXES, 0, 0, tiled=True)  6.76 us
    all_to_all x1, starting transfers between devices, per_device(): received = lax.all_to_all(packed, AXES, 0, 0, tiled=True)  5.04 us
    pallas_call x1, Pallas kernels, norm_rows(): pl.pallas_call(functools.partial(norm_kernel, n_tp), out_shape=[jax.Shape...  1.62 us
  transfers between devices with their start and end apart: 15, of which 10 were waited for; matrix products, arithmetic and copies ran while one was open for 0% of the time, Pallas kernels for 20%

profile of v6, /device:TPU:0, one launch (start us, length us, event | category | flops | bytes accessed | tf_op | source)
XLA Modules:
  0.0 57.0 jit_solution(14173629460661058402)
XLA Ops:
  0.6 0.5 collective-permute-start.1
  1.2 1.6 %norm.1 = (bf16[128,2176]{1,0:T(8,128)(2,1)S(1)}, bf16[80,2176]{1,0:T(8,128)(2,1)S(1)}, bf16[80,2176]{1,0:T(8,128)(2,1)S(1)}, f32[128,128]{1,0:T(8,128)S(1)}) custom-call(bf16[256,2048]{1,0:T(8,128)(2,1)} %x_hbm.1, f32[1,2048]{1,0:T(1,128)} %bitcast.6, s32[2,128]{1,0:T(2,128)} %bitcast.7, bf16[2048,768]{1,0:T(8,128)(2,1)} %refs_3_.5), custom_call_target="tpu_custom_call" | custom-call | tf_op jit(solution)/shard_map/norm/pallas_call | solution.py:167
  2.8 2.5 %collective-permute-start = (bf16[80,2176]{1,0:T(8,128)(2,1)S(1)}, bf16[80,2176]{1,0:T(8,128)(2,1)S(1)}, u32[]{:S(2)}, u32[]{:S(2)}) collective-permute-start(bf16[80,2176]{1,0:T(8,128)(2,1)S(1)} %get-tuple-element.30), channel_id=1, source_target_pairs={{0,8},{1,9},{2,10},{3,11},{8,16},{9,17},{10,18},{11,19},{16,24},{1... | collective-permute-start | bytes 1044488 | tf_op jit(solution)/shard_map/ppermute | solution.py:376
  5.3 0.0 collective-permute-start.3
  5.3 1.3 %collective-permute-done.1.refs_2_.refs_3_.refs_4_ = bf16[2048,768]{1,0:T(8,128)(2,1)S(1)} collective-permute-done((bf16[2048,768]{1,0:T(8,128)(2,1)}, bf16[2048,768]{1,0:T(8,128)(2,1)S(1)}, u32[]{:S(2)}, u32[]{:S(2)}) %collective-permute-start.1) | collective-permute-done | bytes 3145760 | tf_op jit(solution)/shard_map/ppermute | solution.py:376
  6.7 1.9 %stats.5.refs_5_ = f32[128,128]{1,0:T(8,128)S(1)} custom-call(bf16[128,2176]{1,0:T(8,128)(2,1)S(1)} %get-tuple-element.31.refs_0_, bf16[2048,768]{1,0:T(8,128)(2,1)S(1)} %copy-done, bf16[2048,768]{1,0:T(8,128)(2,1)S(1)} %collective-permute-done.1.refs_2_.refs_3_.refs_4_, f32[128,128]{1,0:T(8,128)S(1)} %get-tuple-element.32.refs_3_), custom_call_target="tpu_custom_call" | custom-call | flops 805306368 | bytes 6291456 | tf_op jit(solution)/shard_map/stats/pallas_call | solution.py:306
  8.6 1.9 %collective-permute-done.refs_0_ = bf16[80,2176]{1,0:T(8,128)(2,1)S(1)} collective-permute-done((bf16[80,2176]{1,0:T(8,128)(2,1)S(1)}, bf16[80,2176]{1,0:T(8,128)(2,1)S(1)}, u32[]{:S(2)}, u32[]{:S(2)}) %collective-permute-start) | collective-permute-done | bytes 348192 | tf_op jit(solution)/shard_map/ppermute | solution.py:376
  10.5 2.1 %collective-permute-start.2 = (bf16[80,2176]{1,0:T(8,128)(2,1)S(1)}, bf16[80,2176]{1,0:T(8,128)(2,1)S(1)}, u32[]{:S(2)}, u32[]{:S(2)}) collective-permute-start(bf16[80,2176]{1,0:T(8,128)(2,1)S(1)} %collective-permute-done.refs_0_), channel_id=1, source_target_pairs={{0,8},{1,9},{2,10},{3,11},{8,16},{9,17},{10,18},{11,19},{16,24},{1... | collective-permute-start | bytes 1044488 | tf_op jit(solution)/shard_map/ppermute | solution.py:376
  12.6 0.1 collective-permute-done.3.refs_1_
  12.7 0.0 collective-permute-start.4
  12.7 2.0 %collective-permute-start.9 = (bf16[96,2176]{1,0:T(8,128)(2,1)S(1)}, bf16[96,2176]{1,0:T(8,128)(2,1)S(1)}, u32[]{:S(2)}, u32[]{:S(2)}) collective-permute-start(bf16[96,2176]{1,0:T(8,128)(2,1)S(1)} %cut.8), channel_id=1, source_target_pairs={{0,2},{1,3},{2,0},{3,1},{4,6},{5,7},{6,4},{7,5},{8,10},{9,11},{10,... | collective-permute-start | bytes 1253384 | tf_op jit(solution)/shard_map/ppermute | solution.py:376
  14.8 1.7 %stats.6.refs_6_ = f32[160,128]{1,0:T(8,128)S(1)} custom-call(bf16[80,2176]{1,0:T(8,128)(2,1)S(1)} %collective-permute-done.refs_0_, bf16[80,2176]{1,0:T(8,128)(2,1)S(1)} %collective-permute-done.3.refs_1_, bf16[2048,768]{1,0:T(8,128)(2,1)S(1)} %copy-done, bf16[2048,768]{1,0:T(8,128)(2,1)S(1)} %collective-permute-done.1.refs_2_.refs_3_.refs_4_), custom_call_target="tpu_custom_call" | custom-call | flops 1006632960 | bytes 6291456 | tf_op jit(solution)/shard_map/stats/pallas_call | solution.py:306
  16.4 2.4 %collective-permute-done.2.refs_0_ = bf16[80,2176]{1,0:T(8,128)(2,1)S(1)} collective-permute-done((bf16[80,2176]{1,0:T(8,128)(2,1)S(1)}, bf16[80,2176]{1,0:T(8,128)(2,1)S(1)}, u32[]{:S(2)}, u32[]{:S(2)}) %collective-permute-start.2) | collective-permute-done | bytes 348192 | tf_op jit(solution)/shard_map/ppermute | solution.py:376
  18.8 2.1 %collective-permute-start.8 = (bf16[80,2176]{1,0:T(8,128)(2,1)S(1)}, bf16[80,2176]{1,0:T(8,128)(2,1)S(1)}, u32[]{:S(2)}, u32[]{:S(2)}) collective-permute-start(bf16[80,2176]{1,0:T(8,128)(2,1)S(1)} %collective-permute-done.2.refs_0_), channel_id=1, source_target_pairs={{0,8},{1,9},{2,10},{3,11},{8,16},{9,17},{10,18},{11,19},{16,24},{1... | collective-permute-start | bytes 1044488 | tf_op jit(solution)/shard_map/ppermute | solution.py:376
  21.0 2.0 %collective-permute-start.5 = (bf16[96,2176]{1,0:T(8,128)(2,1)S(1)}, bf16[96,2176]{1,0:T(8,128)(2,1)S(1)}, u32[]{:S(2)}, u32[]{:S(2)}) collective-permute-start(bf16[96,2176]{1,0:T(8,128)(2,1)S(1)} %cut.6), channel_id=1, source_target_pairs={{0,2},{1,3},{2,0},{3,1},{4,6},{5,7},{6,4},{7,5},{8,10},{9,11},{10,... | collective-permute-start | bytes 1253384 | tf_op jit(solution)/shard_map/ppermute | solution.py:376
  23.0 2.3 %stats.7.refs_7_ = f32[256,128]{1,0:T(8,128)S(1)} custom-call(bf16[80,2176]{1,0:T(8,128)(2,1)S(1)} %collective-permute-done.2.refs_0_, bf16[80,2176]{1,0:T(8,128)(2,1)S(1)} %collective-permute-done.4.refs_1_, bf16[96,2176]{1,0:T(8,128)(2,1)S(1)} %collective-permute-done.9.refs_2_, bf16[2048,768]{1,0:T(8,128)(2,1)S(1)} %copy-done, ...), custom_call_target="tpu_custom_call" | custom-call | flops 1610612736 | bytes 6291456 | tf_op jit(solution)/shard_map/stats/pallas_call | solution.py:306
  25.4 2.0 %collective-permute-done.8.refs_0_ = bf16[80,2176]{1,0:T(8,128)(2,1)S(1)} collective-permute-done((bf16[80,2176]{1,0:T(8,128)(2,1)S(1)}, bf16[80,2176]{1,0:T(8,128)(2,1)S(1)}, u32[]{:S(2)}, u32[]{:S(2)}) %collective-permute-start.8) | collective-permute-done | bytes 348192 | tf_op jit(solution)/shard_map/ppermute | solution.py:376
  27.3 2.5 %collective-permute-done.10.refs_1_.refs_0_ = bf16[80,2176]{1,0:T(8,128)(2,1)S(1)} collective-permute-done((bf16[80,2176]{1,0:T(8,128)(2,1)S(1)}, bf16[80,2176]{1,0:T(8,128)(2,1)S(1)}, u32[]{:S(2)}, u32[]{:S(2)}) %collective-permute-start.10) | collective-permute-done | bytes 348192 | tf_op jit(solution)/shard_map/ppermute | solution.py:376
  29.9 1.6 %collective-permute-start.13 = (bf16[64,2176]{1,0:T(8,128)(2,1)S(1)}, bf16[64,2176]{1,0:T(8,128)(2,1)S(1)}, u32[]{:S(2)}, u32[]{:S(2)}) collective-permute-start(bf16[64,2176]{1,0:T(8,128)(2,1)S(1)} %cut.11), channel_id=1, source_target_pairs={{0,8},{1,9},{2,10},{3,11},{8,16},{9,17},{10,18},{11,19},{16,24},{1... | collective-permute-start | bytes 835592 | tf_op jit(solution)/shard_map/ppermute | solution.py:376
  31.6 0.5 collective-permute-start.12
  32.1 1.6 %collective-permute-start.11 = (bf16[64,2176]{1,0:T(8,128)(2,1)S(1)}, bf16[64,2176]{1,0:T(8,128)(2,1)S(1)}, u32[]{:S(2)}, u32[]{:S(2)}) collective-permute-start(bf16[64,2176]{1,0:T(8,128)(2,1)S(1)} %cut.9), channel_id=1, source_target_pairs={{0,2},{1,3},{2,0},{3,1},{4,6},{5,7},{6,4},{7,5},{8,10},{9,11},{10,... | collective-permute-start | bytes 835592 | tf_op jit(solution)/shard_map/ppermute | solution.py:376
  33.7 1.6 %collective-permute-start.6 = (bf16[16,2176]{1,0:T(8,128)(2,1)S(1)}, bf16[16,2176]{1,0:T(8,128)(2,1)S(1)}, u32[]{:S(2)}, u32[]{:S(2)}) collective-permute-start(bf16[16,2176]{1,0:T(8,128)(2,1)S(1)} %get-tuple-element.40), channel_id=1, source_target_pairs={{0,8},{1,9},{2,10},{3,11},{8,16},{9,17},{10,18},{11,19},{16,24},{1... | collective-permute-start | bytes 208904 | tf_op jit(solution)/shard_map/ppermute | solution.py:376
  35.3 0.4 collective-permute-start.7
  35.8 2.3 %stats.8.refs_8_ = f32[256,128]{1,0:T(8,128)S(1)} custom-call(bf16[80,2176]{1,0:T(8,128)(2,1)S(1)} %collective-permute-done.8.refs_0_, bf16[80,2176]{1,0:T(8,128)(2,1)S(1)} %collective-permute-done.10.refs_1_.refs_0_, bf16[96,2176]{1,0:T(8,128)(2,1)S(1)} %collective-permute-done.5.refs_0_.refs_2_, bf16[2048,768]{1,0:T(8,128)(2,1)S(1)} %copy-done, ...), custom_call_target="tpu_custom_call" | custom-call | flops 1610612736 | bytes 6291456 | tf_op jit(solution)/shard_map/stats/pallas_call | solution.py:306
  38.1 0.1 collective-permute-done.13.refs_0_
  38.2 2.0 %collective-permute-done.12.refs_1_ = bf16[64,2176]{1,0:T(8,128)(2,1)S(1)} collective-permute-done((bf16[64,2176]{1,0:T(8,128)(2,1)S(1)}, bf16[64,2176]{1,0:T(8,128)(2,1)S(1)}, u32[]{:S(2)}, u32[]{:S(2)}) %collective-permute-start.12) | collective-permute-done | bytes 278560 | tf_op jit(solution)/shard_map/ppermute | solution.py:376
  40.2 1.4 %stats.9.refs_9_ = f32[128,128]{1,0:T(8,128)S(1)} custom-call(bf16[64,2176]{1,0:T(8,128)(2,1)S(1)} %collective-permute-done.13.refs_0_, bf16[64,2176]{1,0:T(8,128)(2,1)S(1)} %collective-permute-done.12.refs_1_, bf16[2048,768]{1,0:T(8,128)(2,1)S(1)} %copy-done, bf16[2048,768]{1,0:T(8,128)(2,1)S(1)} %collective-permute-done.1.refs_2_.refs_3_.refs_4_), custom_call_target="tpu_custom_call" | custom-call | flops 805306368 | bytes 6291456 | tf_op jit(solution)/shard_map/stats/pallas_call | solution.py:306
  41.6 0.1 collective-permute-done.7.refs_1_
  41.7 2.2 %stats_last.1 = f32[32,4,128]{2,1,0:T(4,128)} custom-call(bf16[16,2176]{1,0:T(8,128)(2,1)S(1)} %collective-permute-done.6.refs_0_, bf16[16,2176]{1,0:T(8,128)(2,1)S(1)} %collective-permute-done.7.refs_1_, bf16[64,2176]{1,0:T(8,128)(2,1)S(1)} %collective-permute-done.11.refs_2_, bf16[2048,768]{1,0:T(8,128)(2,1)S(1)} %copy-done, ...), custom_call_target="tpu_custom_call" | custom-call | flops 603979776 | bytes 6291456 | tf_op jit(solution)/shard_map/stats_last/pallas_call | solution.py:306
  43.9 5.0 %all-to-all-start = ((f32[32,4,128]{2,1,0:T(4,128)}), f32[32,4,128]{2,1,0:T(4,128)S(1)}, u32[]{:S(2)}, u32[]{:S(2)}) async-start(f32[32,4,128]{2,1,0:T(4,128)} %stats_last.1), calls=%async_computation | async-start | bytes 131072 | tf_op jit(solution)/shard_map/all_to_all | solution.py:425
  49.6 6.8 %all-to-all-done.r_ref = f32[32,4,128]{2,1,0:T(4,128)S(1)} async-done(((f32[32,4,128]{2,1,0:T(4,128)}), f32[32,4,128]{2,1,0:T(4,128)S(1)}, u32[]{:S(2)}, u32[]{:S(2)}) %all-to-all-start) | async-done | bytes 65568 | tf_op jit(solution)/shard_map/all_to_all | solution.py:425
  56.3 0.7 %finish.1 = (f32[2,128]{1,0:T(2,128)}, f32[2,128]{1,0:T(2,128)}, f32[1,1]{1,0:T(1,128)}, f32[1,1]{1,0:T(1,128)}) custom-call(f32[32,4,128]{2,1,0:T(4,128)S(1)} %all-to-all-done.r_ref, s32[1]{0:T(128)S(6)} %copy.9.len_ref), custom_call_target="tpu_custom_call" | custom-call | tf_op jit(solution)/shard_map/finish/pallas_call | solution.py:352
  (14 shorter events, 0.1 us)
Async XLA Ops:
  0.6 6.0 %copy-start = (bf16[2048,768]{1,0:T(8,128)(2,1)S(1)}, bf16[2048,768]{1,0:T(8,128)(2,1)}, u32[]{:S(2)}) copy-start(bf16[2048,768]{1,0:T(8,128)(2,1)} %refs_3_.5) | copy-start | bytes 9437188
  0.6 6.0 %collective-permute-start.1 = (bf16[2048,768]{1,0:T(8,128)(2,1)}, bf16[2048,768]{1,0:T(8,128)(2,1)S(1)}, u32[]{:S(2)}, u32[]{:S(2)}) collective-permute-start(bf16[2048,768]{1,0:T(8,128)(2,1)} %refs_3_.5), channel_id=1, source_target_pairs={{0,1},{1,0},{2,3},{3,2},{4,5},{5,4},{6,7},{7,6},{8,9},{9,8},{10,11... | collective-permute-start | bytes 9437192 | tf_op jit(solution)/shard_map/ppermute | solution.py:376
  2.8 7.7 %collective-permute-start = (bf16[80,2176]{1,0:T(8,128)(2,1)S(1)}, bf16[80,2176]{1,0:T(8,128)(2,1)S(1)}, u32[]{:S(2)}, u32[]{:S(2)}) collective-permute-start(bf16[80,2176]{1,0:T(8,128)(2,1)S(1)} %get-tuple-element.30), channel_id=1, source_target_pairs={{0,8},{1,9},{2,10},{3,11},{8,16},{9,17},{10,18},{11,19},{16,24},{1... | collective-permute-start | bytes 1044488 | tf_op jit(solution)/shard_map/ppermute | solution.py:376
  5.3 7.4 %collective-permute-start.3 = (bf16[80,2176]{1,0:T(8,128)(2,1)S(1)}, bf16[80,2176]{1,0:T(8,128)(2,1)S(1)}, u32[]{:S(2)}, u32[]{:S(2)}) collective-permute-start(bf16[80,2176]{1,0:T(8,128)(2,1)S(1)} %get-tuple-element.34), channel_id=1, source_target_pairs={{0,4},{1,5},{2,6},{3,7},{8,0},{9,1},{10,2},{11,3},{16,8},{17,9},{1... | collective-permute-start | bytes 1044488 | tf_op jit(solution)/shard_map/ppermute | solution.py:376
  10.5 8.3 %collective-permute-start.2 = (bf16[80,2176]{1,0:T(8,128)(2,1)S(1)}, bf16[80,2176]{1,0:T(8,128)(2,1)S(1)}, u32[]{:S(2)}, u32[]{:S(2)}) collective-permute-start(bf16[80,2176]{1,0:T(8,128)(2,1)S(1)} %collective-permute-done.refs_0_), channel_id=1, source_target_pairs={{0,8},{1,9},{2,10},{3,11},{8,16},{9,17},{10,18},{11,19},{16,24},{1... | collective-permute-start | bytes 1044488 | tf_op jit(solution)/shard_map/ppermute | solution.py:376
  12.7 8.3 %collective-permute-start.4 = (bf16[80,2176]{1,0:T(8,128)(2,1)S(1)}, bf16[80,2176]{1,0:T(8,128)(2,1)S(1)}, u32[]{:S(2)}, u32[]{:S(2)}) collective-permute-start(bf16[80,2176]{1,0:T(8,128)(2,1)S(1)} %collective-permute-done.3.refs_1_), channel_id=1, source_target_pairs={{0,4},{1,5},{2,6},{3,7},{8,0},{9,1},{10,2},{11,3},{16,8},{17,9},{1... | collective-permute-start | bytes 1044488 | tf_op jit(solution)/shard_map/ppermute | solution.py:376
  12.7 10.3 %collective-permute-start.9 = (bf16[96,2176]{1,0:T(8,128)(2,1)S(1)}, bf16[96,2176]{1,0:T(8,128)(2,1)S(1)}, u32[]{:S(2)}, u32[]{:S(2)}) collective-permute-start(bf16[96,2176]{1,0:T(8,128)(2,1)S(1)} %cut.8), channel_id=1, source_target_pairs={{0,2},{1,3},{2,0},{3,1},{4,6},{5,7},{6,4},{7,5},{8,10},{9,11},{10,... | collective-permute-start | bytes 1253384 | tf_op jit(solution)/shard_map/ppermute | solution.py:376
  18.8 8.5 %collective-permute-start.8 = (bf16[80,2176]{1,0:T(8,128)(2,1)S(1)}, bf16[80,2176]{1,0:T(8,128)(2,1)S(1)}, u32[]{:S(2)}, u32[]{:S(2)}) collective-permute-start(bf16[80,2176]{1,0:T(8,128)(2,1)S(1)} %collective-permute-done.2.refs_0_), channel_id=1, source_target_pairs={{0,8},{1,9},{2,10},{3,11},{8,16},{9,17},{10,18},{11,19},{16,24},{1... | collective-permute-start | bytes 1044488 | tf_op jit(solution)/shard_map/ppermute | solution.py:376
  20.9 8.9 %collective-permute-start.10 = (bf16[80,2176]{1,0:T(8,128)(2,1)S(1)}, bf16[80,2176]{1,0:T(8,128)(2,1)S(1)}, u32[]{:S(2)}, u32[]{:S(2)}) collective-permute-start(bf16[80,2176]{1,0:T(8,128)(2,1)S(1)} %collective-permute-done.4.refs_1_), channel_id=1, source_target_pairs={{0,4},{1,5},{2,6},{3,7},{8,0},{9,1},{10,2},{11,3},{16,8},{17,9},{1... | collective-permute-start | bytes 1044488 | tf_op jit(solution)/shard_map/ppermute | solution.py:376
  21.0 12.7 %collective-permute-start.5 = (bf16[96,2176]{1,0:T(8,128)(2,1)S(1)}, bf16[96,2176]{1,0:T(8,128)(2,1)S(1)}, u32[]{:S(2)}, u32[]{:S(2)}) collective-permute-start(bf16[96,2176]{1,0:T(8,128)(2,1)S(1)} %cut.6), channel_id=1, source_target_pairs={{0,2},{1,3},{2,0},{3,1},{4,6},{5,7},{6,4},{7,5},{8,10},{9,11},{10,... | collective-permute-start | bytes 1253384 | tf_op jit(solution)/shard_map/ppermute | solution.py:376
  29.9 8.3 %collective-permute-start.13 = (bf16[64,2176]{1,0:T(8,128)(2,1)S(1)}, bf16[64,2176]{1,0:T(8,128)(2,1)S(1)}, u32[]{:S(2)}, u32[]{:S(2)}) collective-permute-start(bf16[64,2176]{1,0:T(8,128)(2,1)S(1)} %cut.11), channel_id=1, source_target_pairs={{0,8},{1,9},{2,10},{3,11},{8,16},{9,17},{10,18},{11,19},{16,24},{1... | collective-permute-start | bytes 835592 | tf_op jit(solution)/shard_map/ppermute | solution.py:376
  31.6 8.6 %collective-permute-start.12 = (bf16[64,2176]{1,0:T(8,128)(2,1)S(1)}, bf16[64,2176]{1,0:T(8,128)(2,1)S(1)}, u32[]{:S(2)}, u32[]{:S(2)}) collective-permute-start(bf16[64,2176]{1,0:T(8,128)(2,1)S(1)} %cut.10), channel_id=1, source_target_pairs={{0,4},{1,5},{2,6},{3,7},{8,0},{9,1},{10,2},{11,3},{16,8},{17,9},{1... | collective-permute-start | bytes 835592 | tf_op jit(solution)/shard_map/ppermute | solution.py:376
  32.1 9.6 %collective-permute-start.11 = (bf16[64,2176]{1,0:T(8,128)(2,1)S(1)}, bf16[64,2176]{1,0:T(8,128)(2,1)S(1)}, u32[]{:S(2)}, u32[]{:S(2)}) collective-permute-start(bf16[64,2176]{1,0:T(8,128)(2,1)S(1)} %cut.9), channel_id=1, source_target_pairs={{0,2},{1,3},{2,0},{3,1},{4,6},{5,7},{6,4},{7,5},{8,10},{9,11},{10,... | collective-permute-start | bytes 835592 | tf_op jit(solution)/shard_map/ppermute | solution.py:376
  33.7 7.9 %collective-permute-start.6 = (bf16[16,2176]{1,0:T(8,128)(2,1)S(1)}, bf16[16,2176]{1,0:T(8,128)(2,1)S(1)}, u32[]{:S(2)}, u32[]{:S(2)}) collective-permute-start(bf16[16,2176]{1,0:T(8,128)(2,1)S(1)} %get-tuple-element.40), channel_id=1, source_target_pairs={{0,8},{1,9},{2,10},{3,11},{8,16},{9,17},{10,18},{11,19},{16,24},{1... | collective-permute-start | bytes 208904 | tf_op jit(solution)/shard_map/ppermute | solution.py:376
  35.3 6.4 %collective-permute-start.7 = (bf16[16,2176]{1,0:T(8,128)(2,1)S(1)}, bf16[16,2176]{1,0:T(8,128)(2,1)S(1)}, u32[]{:S(2)}, u32[]{:S(2)}) collective-permute-start(bf16[16,2176]{1,0:T(8,128)(2,1)S(1)} %get-tuple-element.41), channel_id=1, source_target_pairs={{0,4},{1,5},{2,6},{3,7},{8,0},{9,1},{10,2},{11,3},{16,8},{17,9},{1... | collective-permute-start | bytes 208904 | tf_op jit(solution)/shard_map/ppermute | solution.py:376
  43.9 12.5 %all-to-all-start = ((f32[32,4,128]{2,1,0:T(4,128)}), f32[32,4,128]{2,1,0:T(4,128)S(1)}, u32[]{:S(2)}, u32[]{:S(2)}) async-start(f32[32,4,128]{2,1,0:T(4,128)} %stats_last.1), calls=%async_computation | async-start | bytes 131072 | tf_op jit(solution)/shard_map/all_to_all | solution.py:425

commit v7 on v6

--- a/solution.py
+++ b/solution.py
@@ -13,7 +13,7 @@
 STATS = 4
 DIGIT_BITS = 7
 NOTHING = -1e30
-EARLY_ROWS = 32
+EARLY_TILES = (32, 32, 16, 16, 16, 16)
 VMEM_BYTES = 10 * 1024 * 1024
 
 
@@ -45,17 +45,15 @@
 
 
 def segments(rows):
-    e = rows // 8
-    return (0, 2 * e, 3 * e, 4 * e, 5 * e, 6 * e), (2 * e, e, e, e, e, 2 * e)
+    e = rows // 4
+    return (0, e, 2 * e, 3 * e), (e, e, e, e)
 
 
 PARTS = {
-    "all": (0, 1, 2, 3, 4, 5),
-    "most": (0, 1, 2, 3),
-    "half": (0, 1, 2),
-    "y": (5, 4),
-    "y_last": (5,),
-    "c": (4,),
+    "all": (0, 1, 2, 3),
+    "half": (0, 1),
+    "c": (2,),
+    "y": (3,),
 }
 
 
@@ -142,19 +140,19 @@
         get_head.start()
         get_head.wait()
         ids = [vocab_ids(vdev, req * n_tp + tp)]
-        for k in range(0, rows, EARLY_ROWS):
-            logits = jnp.dot(
-                xn_ref[k : k + EARLY_ROWS, :d], head_ref[...], preferred_element_type=jnp.float32
-            )
-            wanted = undigits(xn_ref[k : k + EARLY_ROWS, d:])
-            early_ref[k : k + EARLY_ROWS, :] = row_stats(logits, wanted, ids)
+        k = 0
+        for size in EARLY_TILES:
+            here = pl.ds(k, size * rows // sum(EARLY_TILES))
+            k += here.size
+            logits = jnp.dot(xn_ref[here, :d], head_ref[...], preferred_element_type=jnp.float32)
+            early_ref[here, :] = row_stats(logits, undigits(xn_ref[here, d:]), ids)
 
     starts, sizes = segments(rows)
     for ref, flip in ((cw_ref, 0), (ccw_ref, 1)):
         down = plane != flip
         at = 0
-        for j in PARTS["most"]:
-            start = pl.multiple_of(jnp.where(down, starts[5 - j], starts[j]), 16)
+        for j in PARTS["half"]:
+            start = pl.multiple_of(jnp.where(down, starts[3 - j], starts[j]), 16)
             ref[pl.ds(at, sizes[j]), :] = xn_ref[pl.ds(start, sizes[j]), :]
             at += sizes[j]
 
@@ -162,7 +160,7 @@
 def norm_rows(hidden, norm_gain, target_ids, head, n_tp, rows):
     d = hidden.shape[1]
     wide = d + LANES
-    message = (part_rows("most", rows), wide)
+    message = (part_rows("half", rows), wide)
     hbm_operands = (hidden, norm_gain.reshape(1, d), target_ids.reshape(2, rows), head)
     return pl.pallas_call(
         functools.partial(norm_kernel, n_tp),
@@ -281,7 +279,7 @@
                 here = ref[pl.ds(at, sizes[j]), :]
                 at += sizes[j]
                 if hops:
-                    found[j if turn > 0 else 5 - j].append(here)
+                    found[j if turn > 0 else 3 - j].append(here)
                 else:
                     own = ref[...]
     found = [functools.reduce(jnp.add, values) for values in found]
@@ -368,8 +366,7 @@
     cw_pairs, ccw_pairs = ring_pairs(n_req, n_tp, 1), ring_pairs(n_req, n_tp, -1)
     other_core, other_y = tp_pairs(n_req, n_tp, 1), tp_pairs(n_req, n_tp, 2)
     sizes = (n_req, n_tp, rows)
-    y_rows, c_rows, half = (part_rows(part, rows) for part in ("y", "c", "half"))
-    y_last_rows = part_rows("y_last", rows)
+    part = part_rows("y", rows)
     metas, stats = [], []
 
     def send(value, pairs):
@@ -389,35 +386,41 @@
         hidden_states, norm_gain, target_ids, head, n_tp, rows
     )
     items = [(xn, ((0, 0, "all"),))]
-    for hops in range(1, n_req // 2):
-        next_to_last = 2 * hops + 2 == n_req
-        cw, ccw = send(to_cw, cw_pairs), send(to_ccw, ccw_pairs)
-        if hops > 1:
+    cw, ccw, late = to_cw, to_ccw, []
+    for hops in range(1, n_req // 2 + 1):
+        next_cw, next_ccw = send(cw, cw_pairs), send(ccw, ccw_pairs)
+        others = []
+        both = [(0, 0, part), (1, 0, part)]
+        if hops == 2:
+            (c_both,) = cut((cw, ccw), [[(0, part, part), (1, part, part)]])
+            c_both = send(c_both, other_y)
+            others = [(c_both, ((1, 1, "c"), (-1, 1, "c")))]
+        elif hops > 2:
+            (y_message,) = cut((cw, ccw), [both])
             y_next = send(y_message, other_y)
+            if hops == 3:
+                c_cw, c_ccw = cut((c_both,), [[both[0]], [(0, part, part)]])
+            else:
+                c_cw, c_ccw, _ = lax.optimization_barrier((c_cw, c_ccw, y_message))
+            c_cw, c_ccw = send(c_cw, cw_pairs), send(c_ccw, ccw_pairs)
+            others = late + [
+                (c_cw, ((1, hops - 1, "c"),)),
+                (c_ccw, ((-1, hops - 1, "c"),)),
+                (y_next, ((1, hops - 1, "y"), (-1, hops - 1, "y"))),
+            ]
+            late = []
         work(items, () if stats else (early,))
-        cw, ccw = after(cw), after(ccw)
-        items = [(cw, ((1, hops, "most"),)), (ccw, ((-1, hops, "most"),))]
-        if hops > 1:
-            items.append((y_next, ((1, hops - 1, "y"), (-1, hops - 1, "y"))))
-        if next_to_last:
-            (to_cw,), (to_ccw,) = cut((cw,), [[(0, 0, half)]]), cut((ccw,), [[(0, 0, half)]])
-        else:
-            to_cw, to_ccw = cw, ccw
-        count = y_last_rows if next_to_last else y_rows
-        (y_message,) = cut((cw, ccw), [[(0, 0, count), (1, 0, count)]])
-    hops = n_req // 2
-    c_cw, c_ccw = cut((y_next,), [[(0, y_rows - c_rows, c_rows)], [(0, 2 * y_rows - c_rows, c_rows)]])
-    cw, ccw = send(to_cw, cw_pairs), send(to_ccw, ccw_pairs)
-    y_next = send(y_message, other_y)
-    c_cw, c_ccw = send(c_cw, cw_pairs), send(c_ccw, ccw_pairs)
-    work(items)
-    cw, ccw = after(cw), after(ccw)
-    work([(cw, ((1, hops, "half"),)), (ccw, ((-1, hops, "half"),))])
-    items = [
-        (c_cw, ((1, hops - 1, "c"),)),
-        (c_ccw, ((-1, hops - 1, "c"),)),
-        (y_next, ((1, hops - 1, "y_last"), (-1, hops - 1, "y_last"))),
-    ]
+        if hops == 2:
+            (y_message,) = cut((cw, ccw), [both])
+            late = [(send(y_message, other_y), ((1, 1, "y"), (-1, 1, "y")))]
+        cw, ccw = after(next_cw), after(next_ccw)
+        items = [(cw, ((1, hops, "half"),)), (ccw, ((-1, hops, "half"),))]
+        if 2 * hops == n_req:
+            work(items)
+            items = []
+        items += others
+        if hops == 2:
+            items, late = items + late, []
     pieces, meta = zip(*items)
     packed = stats_of(
         pieces, meta, head, other_head, *sizes, earlier=tuple(metas), stats=stats, tail=True

time: 57.2 us -> 55.7 us (0.974)
  waiting for transfers between devices: 19.2 us -> 15.9 us
  starting transfers between devices: 22.2 us -> 24.4 us
    ppermute x14 -> x17, waiting for transfers between devices: 12.5 us -> 9.17 us  [send(): return lax.ppermute(value, AXES, pairs)]
    ppermute x14 -> x17, starting transfers between devices: 17.1 us -> 18.3 us  [send(): return lax.ppermute(value, AXES, pairs)]
    all_to_all x1, starting transfers between devices: 5.04 us -> 6.1 us  [per_device(): received = lax.all_to_all(packed, AXES, 0, 0, tiled=True)]
  transfers between devices with their start and end apart: 15 -> 18, of which waited for: 10 -> 7; matrix products, arithmetic and copies ran while one was open for 0% -> 0% of each run, Pallas kernels for 20% -> 20%
where the time goes in v7:
time: 55.7 us; the launch traced here: 55.5 us
  starting transfers between devices  24.4 us (44%)
  waiting for transfers between devices  15.9 us (29%)
  Pallas kernels  13.8 us (25%)
  between operations  1.37 us (2%)
    ppermute x17, starting transfers between devices, send(): return lax.ppermute(value, AXES, pairs)  18.3 us
    pallas_call x6, Pallas kernels, stats_of(): pl.pallas_call(functools.partial(stats_kernel, metas, n_req, n_tp, rows,...  11.4 us
    ppermute x17, waiting for transfers between devices, send(): return lax.ppermute(value, AXES, pairs)  9.17 us
    all_to_all x1, waiting for transfers between devices, per_device(): received = lax.all_to_all(packed, AXES, 0, 0, tiled=True)  6.76 us
    all_to_all x1, starting transfers between devices, per_device(): received = lax.all_to_all(packed, AXES, 0, 0, tiled=True)  6.1 us
    pallas_call x1, Pallas kernels, norm_rows(): pl.pallas_call(functools.partial(norm_kernel, n_tp), out_shape=[jax.Shape...  1.61 us
  transfers between devices with their start and end apart: 18, of which 7 were waited for; matrix products, arithmetic and copies ran while one was open for 0% of the time, Pallas kernels for 20%

profile of v7, /device:TPU:0, one launch (start us, length us, event | category | flops | bytes accessed | tf_op | source)
XLA Modules:
  0.0 55.5 jit_solution(9925859618828031721)
XLA Ops:
  0.6 0.5 collective-permute-start.1
  1.2 1.6 %norm.1 = (bf16[128,2176]{1,0:T(8,128)(2,1)S(1)}, bf16[64,2176]{1,0:T(8,128)(2,1)S(1)}, bf16[64,2176]{1,0:T(8,128)(2,1)S(1)}, f32[128,128]{1,0:T(8,128)S(1)}) custom-call(bf16[256,2048]{1,0:T(8,128)(2,1)} %x_hbm.1, f32[1,2048]{1,0:T(1,128)} %bitcast.6, s32[2,128]{1,0:T(2,128)} %bitcast.7, bf16[2048,768]{1,0:T(8,128)(2,1)} %refs_3_.1), custom_call_target="tpu_custom_call" | custom-call | tf_op jit(solution)/shard_map/norm/pallas_call | solution.py:165
  2.8 2.5 %collective-permute-start = (bf16[64,2176]{1,0:T(8,128)(2,1)S(1)}, bf16[64,2176]{1,0:T(8,128)(2,1)S(1)}, u32[]{:S(2)}, u32[]{:S(2)}) collective-permute-start(bf16[64,2176]{1,0:T(8,128)(2,1)S(1)} %get-tuple-element.32), channel_id=1, source_target_pairs={{0,8},{1,9},{2,10},{3,11},{8,16},{9,17},{10,18},{11,19},{16,24},{1... | collective-permute-start | bytes 835592 | tf_op jit(solution)/shard_map/ppermute | solution.py:373
  5.3 1.3 %collective-permute-done.1.refs_2_.refs_3_.refs_5_.refs_6_.refs_4_ = bf16[2048,768]{1,0:T(8,128)(2,1)S(1)} collective-permute-done((bf16[2048,768]{1,0:T(8,128)(2,1)}, bf16[2048,768]{1,0:T(8,128)(2,1)S(1)}, u32[]{:S(2)}, u32[]{:S(2)}) %collective-permute-start.1) | collective-permute-done | bytes 3145760 | tf_op jit(solution)/shard_map/ppermute | solution.py:373
  6.7 1.9 %stats.5.refs_5_ = f32[128,128]{1,0:T(8,128)S(1)} custom-call(bf16[128,2176]{1,0:T(8,128)(2,1)S(1)} %get-tuple-element.33.refs_0_, bf16[2048,768]{1,0:T(8,128)(2,1)S(1)} %copy-done, bf16[2048,768]{1,0:T(8,128)(2,1)S(1)} %collective-permute-done.1.refs_2_.refs_3_.refs_5_.refs_6_.refs_4_, f32[128,128]{1,0:T(8,128)S(1)} %get-tuple-element.34.refs_3_), custom_call_target="tpu_custom_call" | custom-call | flops 805306368 | bytes 6291456 | tf_op jit(solution)/shard_map/stats/pallas_call | solution.py:304
  8.6 1.2 %collective-permute-done.refs_0_ = bf16[64,2176]{1,0:T(8,128)(2,1)S(1)} collective-permute-done((bf16[64,2176]{1,0:T(8,128)(2,1)S(1)}, bf16[64,2176]{1,0:T(8,128)(2,1)S(1)}, u32[]{:S(2)}, u32[]{:S(2)}) %collective-permute-start) | collective-permute-done | bytes 278560 | tf_op jit(solution)/shard_map/ppermute | solution.py:373
  9.8 2.1 %collective-permute-start.6 = (bf16[64,2176]{1,0:T(8,128)(2,1)S(1)}, bf16[64,2176]{1,0:T(8,128)(2,1)S(1)}, u32[]{:S(2)}, u32[]{:S(2)}) collective-permute-start(bf16[64,2176]{1,0:T(8,128)(2,1)S(1)} %collective-permute-done.refs_0_), channel_id=1, source_target_pairs={{0,8},{1,9},{2,10},{3,11},{8,16},{9,17},{10,18},{11,19},{16,24},{1... | collective-permute-start | bytes 835592 | tf_op jit(solution)/shard_map/ppermute | solution.py:373
  11.9 2.0 %collective-permute-start.3 = (bf16[64,2176]{1,0:T(8,128)(2,1)S(1)}, bf16[64,2176]{1,0:T(8,128)(2,1)S(1)}, u32[]{:S(2)}, u32[]{:S(2)}) collective-permute-start(bf16[64,2176]{1,0:T(8,128)(2,1)S(1)} %cut.5), channel_id=1, source_target_pairs={{0,2},{1,3},{2,0},{3,1},{4,6},{5,7},{6,4},{7,5},{8,10},{9,11},{10,... | collective-permute-start | bytes 835592 | tf_op jit(solution)/shard_map/ppermute | solution.py:373
  14.0 0.1 collective-permute-start.9
  14.1 1.4 %stats.6.refs_6_ = f32[128,128]{1,0:T(8,128)S(1)} custom-call(bf16[64,2176]{1,0:T(8,128)(2,1)S(1)} %collective-permute-done.refs_0_, bf16[64,2176]{1,0:T(8,128)(2,1)S(1)} %collective-permute-done.2.refs_1_, bf16[2048,768]{1,0:T(8,128)(2,1)S(1)} %copy-done, bf16[2048,768]{1,0:T(8,128)(2,1)S(1)} %collective-permute-done.1.refs_2_.refs_3_.refs_5_.refs_6_.refs_4_), custom_call_target="tpu_custom_call" | custom-call | flops 805306368 | bytes 6291456 | tf_op jit(solution)/shard_map/stats/pallas_call | solution.py:304
  15.5 2.0 %collective-permute-done.6.refs_0_ = bf16[64,2176]{1,0:T(8,128)(2,1)S(1)} collective-permute-done((bf16[64,2176]{1,0:T(8,128)(2,1)S(1)}, bf16[64,2176]{1,0:T(8,128)(2,1)S(1)}, u32[]{:S(2)}, u32[]{:S(2)}) %collective-permute-start.6) | collective-permute-done | bytes 278560 | tf_op jit(solution)/shard_map/ppermute | solution.py:373
  17.4 1.8 %collective-permute-start.7 = (bf16[64,2176]{1,0:T(8,128)(2,1)S(1)}, bf16[64,2176]{1,0:T(8,128)(2,1)S(1)}, u32[]{:S(2)}, u32[]{:S(2)}) collective-permute-start(bf16[64,2176]{1,0:T(8,128)(2,1)S(1)} %collective-permute-done.6.refs_0_), channel_id=1, source_target_pairs={{0,8},{1,9},{2,10},{3,11},{8,16},{9,17},{10,18},{11,19},{16,24},{1... | collective-permute-start | bytes 835592 | tf_op jit(solution)/shard_map/ppermute | solution.py:373
  19.3 0.0 collective-permute-done.8.refs_1_
  19.3 0.2 collective-permute-start.10
  19.5 1.9 %collective-permute-start.4 = (bf16[32,2176]{1,0:T(8,128)(2,1)S(1)}, bf16[32,2176]{1,0:T(8,128)(2,1)S(1)}, u32[]{:S(2)}, u32[]{:S(2)}) collective-permute-start(bf16[32,2176]{1,0:T(8,128)(2,1)S(1)} %get-tuple-element.39), channel_id=1, source_target_pairs={{0,8},{1,9},{2,10},{3,11},{8,16},{9,17},{10,18},{11,19},{16,24},{1... | collective-permute-start | bytes 417800 | tf_op jit(solution)/shard_map/ppermute | solution.py:373
  21.4 0.2 collective-permute-start.5
  21.6 1.5 %collective-permute-done.9.refs_3_ = bf16[64,2176]{1,0:T(8,128)(2,1)S(1)} collective-permute-done((bf16[64,2176]{1,0:T(8,128)(2,1)S(1)}, bf16[64,2176]{1,0:T(8,128)(2,1)S(1)}, u32[]{:S(2)}, u32[]{:S(2)}) %collective-permute-start.9) | collective-permute-done | bytes 278560 | tf_op jit(solution)/shard_map/ppermute | solution.py:373
  23.1 2.4 %collective-permute-start.16 = (bf16[64,2176]{1,0:T(8,128)(2,1)S(1)}, bf16[64,2176]{1,0:T(8,128)(2,1)S(1)}, u32[]{:S(2)}, u32[]{:S(2)}) collective-permute-start(bf16[64,2176]{1,0:T(8,128)(2,1)S(1)} %cut.9), channel_id=1, source_target_pairs={{0,2},{1,3},{2,0},{3,1},{4,6},{5,7},{6,4},{7,5},{8,10},{9,11},{10,... | collective-permute-start | bytes 835592 | tf_op jit(solution)/shard_map/ppermute | solution.py:373
  25.6 2.3 %stats.7.refs_7_ = f32[256,128]{1,0:T(8,128)S(1)} custom-call(bf16[64,2176]{1,0:T(8,128)(2,1)S(1)} %collective-permute-done.6.refs_0_, bf16[64,2176]{1,0:T(8,128)(2,1)S(1)} %collective-permute-done.8.refs_1_, bf16[64,2176]{1,0:T(8,128)(2,1)S(1)} %collective-permute-done.3.refs_0_.refs_2_, bf16[64,2176]{1,0:T(8,128)(2,1)S(1)} %collective-permute-done.9.refs_3_, ...), custom_call_target="tpu_custom_call" | custom-call | flops 1610612736 | bytes 6291456 | tf_op jit(solution)/shard_map/stats/pallas_call | solution.py:304
  27.9 1.6 %collective-permute-start.15 = (bf16[64,2176]{1,0:T(8,128)(2,1)S(1)}, bf16[64,2176]{1,0:T(8,128)(2,1)S(1)}, u32[]{:S(2)}, u32[]{:S(2)}) collective-permute-start(bf16[64,2176]{1,0:T(8,128)(2,1)S(1)} %collective-permute-done.7.refs_0_), channel_id=1, source_target_pairs={{0,8},{1,9},{2,10},{3,11},{8,16},{9,17},{10,18},{11,19},{16,24},{1... | collective-permute-start | bytes 835592 | tf_op jit(solution)/shard_map/ppermute | solution.py:373
  29.5 0.5 collective-permute-start.14
  30.0 0.1 collective-permute-start.13
  30.1 2.0 %collective-permute-start.11 = (bf16[32,2176]{1,0:T(8,128)(2,1)S(1)}, bf16[32,2176]{1,0:T(8,128)(2,1)S(1)}, u32[]{:S(2)}, u32[]{:S(2)}) collective-permute-start(bf16[32,2176]{1,0:T(8,128)(2,1)S(1)} %collective-permute-done.4.refs_2_), channel_id=1, source_target_pairs={{0,8},{1,9},{2,10},{3,11},{8,16},{9,17},{10,18},{11,19},{16,24},{1... | collective-permute-start | bytes 417800 | tf_op jit(solution)/shard_map/ppermute | solution.py:373
  32.1 0.3 collective-permute-start.12
  32.4 2.3 %stats.8.refs_8_ = f32[256,128]{1,0:T(8,128)S(1)} custom-call(bf16[64,2176]{1,0:T(8,128)(2,1)S(1)} %collective-permute-done.7.refs_0_, bf16[64,2176]{1,0:T(8,128)(2,1)S(1)} %collective-permute-done.10.refs_1_, bf16[32,2176]{1,0:T(8,128)(2,1)S(1)} %collective-permute-done.4.refs_2_, bf16[32,2176]{1,0:T(8,128)(2,1)S(1)} %collective-permute-done.5.refs_3_, ...), custom_call_target="tpu_custom_call" | custom-call | flops 1610612736 | bytes 6291456 | tf_op jit(solution)/shard_map/stats/pallas_call | solution.py:304
  34.7 1.6 %collective-permute-done.14.refs_1_ = bf16[64,2176]{1,0:T(8,128)(2,1)S(1)} collective-permute-done((bf16[64,2176]{1,0:T(8,128)(2,1)S(1)}, bf16[64,2176]{1,0:T(8,128)(2,1)S(1)}, u32[]{:S(2)}, u32[]{:S(2)}) %collective-permute-start.14) | collective-permute-done | bytes 278560 | tf_op jit(solution)/shard_map/ppermute | solution.py:373
  36.3 1.4 %stats.9.refs_9_ = f32[128,128]{1,0:T(8,128)S(1)} custom-call(bf16[64,2176]{1,0:T(8,128)(2,1)S(1)} %collective-permute-done.15.refs_0_, bf16[64,2176]{1,0:T(8,128)(2,1)S(1)} %collective-permute-done.14.refs_1_, bf16[2048,768]{1,0:T(8,128)(2,1)S(1)} %copy-done, bf16[2048,768]{1,0:T(8,128)(2,1)S(1)} %collective-permute-done.1.refs_2_.refs_3_.refs_5_.refs_6_.refs_4_), custom_call_target="tpu_custom_call" | custom-call | flops 805306368 | bytes 6291456 | tf_op jit(solution)/shard_map/stats/pallas_call | solution.py:304
  37.6 1.6 %collective-permute-done.12.refs_1_ = bf16[32,2176]{1,0:T(8,128)(2,1)S(1)} collective-permute-done((bf16[32,2176]{1,0:T(8,128)(2,1)S(1)}, bf16[32,2176]{1,0:T(8,128)(2,1)S(1)}, u32[]{:S(2)}, u32[]{:S(2)}) %collective-permute-start.12) | collective-permute-done | bytes 139296 | tf_op jit(solution)/shard_map/ppermute | solution.py:373
  39.3 2.1 %stats_last.1 = f32[32,4,128]{2,1,0:T(4,128)} custom-call(bf16[32,2176]{1,0:T(8,128)(2,1)S(1)} %collective-permute-done.11.refs_0_, bf16[32,2176]{1,0:T(8,128)(2,1)S(1)} %collective-permute-done.12.refs_1_, bf16[64,2176]{1,0:T(8,128)(2,1)S(1)} %collective-permute-done.13.refs_2_, bf16[2048,768]{1,0:T(8,128)(2,1)S(1)} %copy-done, ...), custom_call_target="tpu_custom_call" | custom-call | flops 805306368 | bytes 6291456 | tf_op jit(solution)/shard_map/stats_last/pallas_call | solution.py:304
  41.3 6.1 %all-to-all-start = ((f32[32,4,128]{2,1,0:T(4,128)}), f32[32,4,128]{2,1,0:T(4,128)S(1)}, u32[]{:S(2)}, u32[]{:S(2)}) async-start(f32[32,4,128]{2,1,0:T(4,128)} %stats_last.1), calls=%async_computation | async-start | bytes 131072 | tf_op jit(solution)/shard_map/all_to_all | solution.py:428
  48.1 6.8 %all-to-all-done.r_ref = f32[32,4,128]{2,1,0:T(4,128)S(1)} async-done(((f32[32,4,128]{2,1,0:T(4,128)}), f32[32,4,128]{2,1,0:T(4,128)S(1)}, u32[]{:S(2)}, u32[]{:S(2)}) %all-to-all-start) | async-done | bytes 65568 | tf_op jit(solution)/shard_map/all_to_all | solution.py:428
  54.8 0.7 %finish.1 = (f32[2,128]{1,0:T(2,128)}, f32[2,128]{1,0:T(2,128)}, f32[1,1]{1,0:T(1,128)}, f32[1,1]{1,0:T(1,128)}) custom-call(f32[32,4,128]{2,1,0:T(4,128)S(1)} %all-to-all-done.r_ref, s32[1]{0:T(128)S(6)} %copy.9.len_ref), custom_call_target="tpu_custom_call" | custom-call | tf_op jit(solution)/shard_map/finish/pallas_call | solution.py:350
  (19 shorter events, 0.1 us)
Async XLA Ops:
  0.6 6.0 %copy-start = (bf16[2048,768]{1,0:T(8,128)(2,1)S(1)}, bf16[2048,768]{1,0:T(8,128)(2,1)}, u32[]{:S(2)}) copy-start(bf16[2048,768]{1,0:T(8,128)(2,1)} %refs_3_.1) | copy-start | bytes 9437188
  0.6 6.0 %collective-permute-start.1 = (bf16[2048,768]{1,0:T(8,128)(2,1)}, bf16[2048,768]{1,0:T(8,128)(2,1)S(1)}, u32[]{:S(2)}, u32[]{:S(2)}) collective-permute-start(bf16[2048,768]{1,0:T(8,128)(2,1)} %refs_3_.1), channel_id=1, source_target_pairs={{0,1},{1,0},{2,3},{3,2},{4,5},{5,4},{6,7},{7,6},{8,9},{9,8},{10,11... | collective-permute-start | bytes 9437192 | tf_op jit(solution)/shard_map/ppermute | solution.py:373
  2.8 7.0 %collective-permute-start = (bf16[64,2176]{1,0:T(8,128)(2,1)S(1)}, bf16[64,2176]{1,0:T(8,128)(2,1)S(1)}, u32[]{:S(2)}, u32[]{:S(2)}) collective-permute-start(bf16[64,2176]{1,0:T(8,128)(2,1)S(1)} %get-tuple-element.32), channel_id=1, source_target_pairs={{0,8},{1,9},{2,10},{3,11},{8,16},{9,17},{10,18},{11,19},{16,24},{1... | collective-permute-start | bytes 835592 | tf_op jit(solution)/shard_map/ppermute | solution.py:373
  5.3 6.6 %collective-permute-start.2 = (bf16[64,2176]{1,0:T(8,128)(2,1)S(1)}, bf16[64,2176]{1,0:T(8,128)(2,1)S(1)}, u32[]{:S(2)}, u32[]{:S(2)}) collective-permute-start(bf16[64,2176]{1,0:T(8,128)(2,1)S(1)} %get-tuple-element.36), channel_id=1, source_target_pairs={{0,4},{1,5},{2,6},{3,7},{8,0},{9,1},{10,2},{11,3},{16,8},{17,9},{1... | collective-permute-start | bytes 835592 | tf_op jit(solution)/shard_map/ppermute | solution.py:373
  9.8 7.7 %collective-permute-start.6 = (bf16[64,2176]{1,0:T(8,128)(2,1)S(1)}, bf16[64,2176]{1,0:T(8,128)(2,1)S(1)}, u32[]{:S(2)}, u32[]{:S(2)}) collective-permute-start(bf16[64,2176]{1,0:T(8,128)(2,1)S(1)} %collective-permute-done.refs_0_), channel_id=1, source_target_pairs={{0,8},{1,9},{2,10},{3,11},{8,16},{9,17},{10,18},{11,19},{16,24},{1... | collective-permute-start | bytes 835592 | tf_op jit(solution)/shard_map/ppermute | solution.py:373
  11.9 7.4 %collective-permute-start.8 = (bf16[64,2176]{1,0:T(8,128)(2,1)S(1)}, bf16[64,2176]{1,0:T(8,128)(2,1)S(1)}, u32[]{:S(2)}, u32[]{:S(2)}) collective-permute-start(bf16[64,2176]{1,0:T(8,128)(2,1)S(1)} %collective-permute-done.2.refs_1_), channel_id=1, source_target_pairs={{0,4},{1,5},{2,6},{3,7},{8,0},{9,1},{10,2},{11,3},{16,8},{17,9},{1... | collective-permute-start | bytes 835592 | tf_op jit(solution)/shard_map/ppermute | solution.py:373
  11.9 7.6 %collective-permute-start.3 = (bf16[64,2176]{1,0:T(8,128)(2,1)S(1)}, bf16[64,2176]{1,0:T(8,128)(2,1)S(1)}, u32[]{:S(2)}, u32[]{:S(2)}) collective-permute-start(bf16[64,2176]{1,0:T(8,128)(2,1)S(1)} %cut.5), channel_id=1, source_target_pairs={{0,2},{1,3},{2,0},{3,1},{4,6},{5,7},{6,4},{7,5},{8,10},{9,11},{10,... | collective-permute-start | bytes 835592 | tf_op jit(solution)/shard_map/ppermute | solution.py:373
  14.0 9.2 %collective-permute-start.9 = (bf16[64,2176]{1,0:T(8,128)(2,1)S(1)}, bf16[64,2176]{1,0:T(8,128)(2,1)S(1)}, u32[]{:S(2)}, u32[]{:S(2)}) collective-permute-start(bf16[64,2176]{1,0:T(8,128)(2,1)S(1)} %cut.7), channel_id=1, source_target_pairs={{0,2},{1,3},{2,0},{3,1},{4,6},{5,7},{6,4},{7,5},{8,10},{9,11},{10,... | collective-permute-start | bytes 835592 | tf_op jit(solution)/shard_map/ppermute | solution.py:373
  17.4 10.4 %collective-permute-start.7 = (bf16[64,2176]{1,0:T(8,128)(2,1)S(1)}, bf16[64,2176]{1,0:T(8,128)(2,1)S(1)}, u32[]{:S(2)}, u32[]{:S(2)}) collective-permute-start(bf16[64,2176]{1,0:T(8,128)(2,1)S(1)} %collective-permute-done.6.refs_0_), channel_id=1, source_target_pairs={{0,8},{1,9},{2,10},{3,11},{8,16},{9,17},{10,18},{11,19},{16,24},{1... | collective-permute-start | bytes 835592 | tf_op jit(solution)/shard_map/ppermute | solution.py:373
  19.3 10.2 %collective-permute-start.10 = (bf16[64,2176]{1,0:T(8,128)(2,1)S(1)}, bf16[64,2176]{1,0:T(8,128)(2,1)S(1)}, u32[]{:S(2)}, u32[]{:S(2)}) collective-permute-start(bf16[64,2176]{1,0:T(8,128)(2,1)S(1)} %collective-permute-done.8.refs_1_), channel_id=1, source_target_pairs={{0,4},{1,5},{2,6},{3,7},{8,0},{9,1},{10,2},{11,3},{16,8},{17,9},{1... | collective-permute-start | bytes 835592 | tf_op jit(solution)/shard_map/ppermute | solution.py:373
  19.5 10.4 %collective-permute-start.4 = (bf16[32,2176]{1,0:T(8,128)(2,1)S(1)}, bf16[32,2176]{1,0:T(8,128)(2,1)S(1)}, u32[]{:S(2)}, u32[]{:S(2)}) collective-permute-start(bf16[32,2176]{1,0:T(8,128)(2,1)S(1)} %get-tuple-element.39), channel_id=1, source_target_pairs={{0,8},{1,9},{2,10},{3,11},{8,16},{9,17},{10,18},{11,19},{16,24},{1... | collective-permute-start | bytes 417800 | tf_op jit(solution)/shard_map/ppermute | solution.py:373
  21.4 8.7 %collective-permute-start.5 = (bf16[32,2176]{1,0:T(8,128)(2,1)S(1)}, bf16[32,2176]{1,0:T(8,128)(2,1)S(1)}, u32[]{:S(2)}, u32[]{:S(2)}) collective-permute-start(bf16[32,2176]{1,0:T(8,128)(2,1)S(1)} %get-tuple-element.40), channel_id=1, source_target_pairs={{0,4},{1,5},{2,6},{3,7},{8,0},{9,1},{10,2},{11,3},{16,8},{17,9},{1... | collective-permute-start | bytes 417800 | tf_op jit(solution)/shard_map/ppermute | solution.py:373
  23.1 9.0 %collective-permute-start.16 = (bf16[64,2176]{1,0:T(8,128)(2,1)S(1)}, bf16[64,2176]{1,0:T(8,128)(2,1)S(1)}, u32[]{:S(2)}, u32[]{:S(2)}) collective-permute-start(bf16[64,2176]{1,0:T(8,128)(2,1)S(1)} %cut.9), channel_id=1, source_target_pairs={{0,2},{1,3},{2,0},{3,1},{4,6},{5,7},{6,4},{7,5},{8,10},{9,11},{10,... | collective-permute-start | bytes 835592 | tf_op jit(solution)/shard_map/ppermute | solution.py:373
  27.9 6.8 %collective-permute-start.15 = (bf16[64,2176]{1,0:T(8,128)(2,1)S(1)}, bf16[64,2176]{1,0:T(8,128)(2,1)S(1)}, u32[]{:S(2)}, u32[]{:S(2)}) collective-permute-start(bf16[64,2176]{1,0:T(8,128)(2,1)S(1)} %collective-permute-done.7.refs_0_), channel_id=1, source_target_pairs={{0,8},{1,9},{2,10},{3,11},{8,16},{9,17},{10,18},{11,19},{16,24},{1... | collective-permute-start | bytes 835592 | tf_op jit(solution)/shard_map/ppermute | solution.py:373
  29.5 6.8 %collective-permute-start.14 = (bf16[64,2176]{1,0:T(8,128)(2,1)S(1)}, bf16[64,2176]{1,0:T(8,128)(2,1)S(1)}, u32[]{:S(2)}, u32[]{:S(2)}) collective-permute-start(bf16[64,2176]{1,0:T(8,128)(2,1)S(1)} %collective-permute-done.10.refs_1_), channel_id=1, source_target_pairs={{0,4},{1,5},{2,6},{3,7},{8,0},{9,1},{10,2},{11,3},{16,8},{17,9},{1... | collective-permute-start | bytes 835592 | tf_op jit(solution)/shard_map/ppermute | solution.py:373
  30.0 9.3 %collective-permute-start.13 = (bf16[64,2176]{1,0:T(8,128)(2,1)S(1)}, bf16[64,2176]{1,0:T(8,128)(2,1)S(1)}, u32[]{:S(2)}, u32[]{:S(2)}) collective-permute-start(bf16[64,2176]{1,0:T(8,128)(2,1)S(1)} %cut.8), channel_id=1, source_target_pairs={{0,2},{1,3},{2,0},{3,1},{4,6},{5,7},{6,4},{7,5},{8,10},{9,11},{10,... | collective-permute-start | bytes 835592 | tf_op jit(solution)/shard_map/ppermute | solution.py:373
  30.1 7.5 %collective-permute-start.11 = (bf16[32,2176]{1,0:T(8,128)(2,1)S(1)}, bf16[32,2176]{1,0:T(8,128)(2,1)S(1)}, u32[]{:S(2)}, u32[]{:S(2)}) collective-permute-start(bf16[32,2176]{1,0:T(8,128)(2,1)S(1)} %collective-permute-done.4.refs_2_), channel_id=1, source_target_pairs={{0,8},{1,9},{2,10},{3,11},{8,16},{9,17},{10,18},{11,19},{16,24},{1... | collective-permute-start | bytes 417800 | tf_op jit(solution)/shard_map/ppermute | solution.py:373
  32.1 7.1 %collective-permute-start.12 = (bf16[32,2176]{1,0:T(8,128)(2,1)S(1)}, bf16[32,2176]{1,0:T(8,128)(2,1)S(1)}, u32[]{:S(2)}, u32[]{:S(2)}) collective-permute-start(bf16[32,2176]{1,0:T(8,128)(2,1)S(1)} %collective-permute-done.5.refs_3_), channel_id=1, source_target_pairs={{0,4},{1,5},{2,6},{3,7},{8,0},{9,1},{10,2},{11,3},{16,8},{17,9},{1... | collective-permute-start | bytes 417800 | tf_op jit(solution)/shard_map/ppermute | solution.py:373
  41.3 13.5 %all-to-all-start = ((f32[32,4,128]{2,1,0:T(4,128)}), f32[32,4,128]{2,1,0:T(4,128)S(1)}, u32[]{:S(2)}, u32[]{:S(2)}) async-start(f32[32,4,128]{2,1,0:T(4,128)} %stats_last.1), calls=%async_computation | async-start | bytes 131072 | tf_op jit(solution)/shard_map/all_to_all | solution.py:428

commit v8 on v7

--- a/solution.py
+++ b/solution.py
@@ -129,11 +129,6 @@
     scale = lax.rsqrt(jnp.mean(feats * feats, axis=-1, keepdims=True) + 1e-06)
     xn_ref[:, :d] = (feats * scale * gain_ref[...]).astype(jnp.bfloat16)
 
-    @pl.when(core == 0)
-    def _():
-        lane = lax.broadcasted_iota(jnp.int32, (rows, LANES), 1)
-        early_ref[...] = jnp.where(lane == 0, NOTHING, 0.0)
-
     @pl.when(core == 1)
     def _():
         get_head = pltpu.make_async_copy(head_hbm, head_ref, sems.at[3])
@@ -248,7 +243,11 @@
 
     lax.fori_loop(0, total // step, body, 0, unroll=total // step)
     if first:
-        out_ref[...] = merged(out_ref[...], early_ref[...])
+
+        @pl.when(jnp.logical_not(own))
+        def _():
+            out_ref[...] = merged(out_ref[...], early_ref[...])
+
     at = 0
     for turn, hops, part in (p for parts in metas for p in parts):
         here = pl.ds(at, part_rows(part, rows))

time: 55.7 us -> 55.7 us (level)
  transfers between devices with their start and end apart: 18 -> 18, of which waited for: 7 -> 7; matrix products, arithmetic and copies ran while one was open for 0% -> 0% of each run, Pallas kernels for 20% -> 19%
where the time goes in v8:
time: 55.7 us; the launch traced here: 55.5 us
  starting transfers between devices  24.5 us (44%)
  waiting for transfers between devices  16.2 us (29%)
  Pallas kernels  13.4 us (24%)
  between operations  1.37 us (2%)
    ppermute x17, starting transfers between devices, send(): return lax.ppermute(value, AXES, pairs)  18.3 us
    pallas_call x6, Pallas kernels, stats_of(): pl.pallas_call(functools.partial(stats_kernel, metas, n_req, n_tp, rows,...  11 us
    ppermute x17, waiting for transfers between devices, send(): return lax.ppermute(value, AXES, pairs)  9.46 us
    all_to_all x1, waiting for transfers between devices, per_device(): received = lax.all_to_all(packed, AXES, 0, 0, tiled=True)  6.76 us
    all_to_all x1, starting transfers between devices, per_device(): received = lax.all_to_all(packed, AXES, 0, 0, tiled=True)  6.13 us
    pallas_call x1, Pallas kernels, norm_rows(): pl.pallas_call(functools.partial(norm_kernel, n_tp), out_shape=[jax.Shape...  1.6 us
  transfers between devices with their start and end apart: 18, of which 7 were waited for; matrix products, arithmetic and copies ran while one was open for 0% of the time, Pallas kernels for 19%

profile of v8, /device:TPU:0, one launch (start us, length us, event | category | flops | bytes accessed | tf_op | source)
XLA Modules:
  0.0 55.5 jit_solution(18226115597594766876)
XLA Ops:
  0.6 0.5 collective-permute-start.1
  1.2 1.6 %norm.1 = (bf16[128,2176]{1,0:T(8,128)(2,1)S(1)}, bf16[64,2176]{1,0:T(8,128)(2,1)S(1)}, bf16[64,2176]{1,0:T(8,128)(2,1)S(1)}, f32[128,128]{1,0:T(8,128)S(1)}) custom-call(bf16[256,2048]{1,0:T(8,128)(2,1)} %x_hbm.1, f32[1,2048]{1,0:T(1,128)} %bitcast.6, s32[2,128]{1,0:T(2,128)} %bitcast.7, bf16[2048,768]{1,0:T(8,128)(2,1)} %refs_3_.1), custom_call_target="tpu_custom_call" | custom-call | tf_op jit(solution)/shard_map/norm/pallas_call | solution.py:160
  2.8 2.5 %collective-permute-start = (bf16[64,2176]{1,0:T(8,128)(2,1)S(1)}, bf16[64,2176]{1,0:T(8,128)(2,1)S(1)}, u32[]{:S(2)}, u32[]{:S(2)}) collective-permute-start(bf16[64,2176]{1,0:T(8,128)(2,1)S(1)} %get-tuple-element.32), channel_id=1, source_target_pairs={{0,8},{1,9},{2,10},{3,11},{8,16},{9,17},{10,18},{11,19},{16,24},{1... | collective-permute-start | bytes 835592 | tf_op jit(solution)/shard_map/ppermute | solution.py:372
  5.3 0.0 collective-permute-start.2
  5.3 1.3 %collective-permute-done.1.refs_2_.refs_3_.refs_5_.refs_6_.refs_4_ = bf16[2048,768]{1,0:T(8,128)(2,1)S(1)} collective-permute-done((bf16[2048,768]{1,0:T(8,128)(2,1)}, bf16[2048,768]{1,0:T(8,128)(2,1)S(1)}, u32[]{:S(2)}, u32[]{:S(2)}) %collective-permute-start.1) | collective-permute-done | bytes 3145760 | tf_op jit(solution)/shard_map/ppermute | solution.py:372
  6.7 1.6 %stats.5.refs_5_ = f32[128,128]{1,0:T(8,128)S(1)} custom-call(bf16[128,2176]{1,0:T(8,128)(2,1)S(1)} %get-tuple-element.33.refs_0_, bf16[2048,768]{1,0:T(8,128)(2,1)S(1)} %copy-done, bf16[2048,768]{1,0:T(8,128)(2,1)S(1)} %collective-permute-done.1.refs_2_.refs_3_.refs_5_.refs_6_.refs_4_, f32[128,128]{1,0:T(8,128)S(1)} %get-tuple-element.34.refs_3_), custom_call_target="tpu_custom_call" | custom-call | flops 805306368 | bytes 6291456 | tf_op jit(solution)/shard_map/stats/pallas_call | solution.py:303
  8.2 1.5 %collective-permute-done.refs_0_ = bf16[64,2176]{1,0:T(8,128)(2,1)S(1)} collective-permute-done((bf16[64,2176]{1,0:T(8,128)(2,1)S(1)}, bf16[64,2176]{1,0:T(8,128)(2,1)S(1)}, u32[]{:S(2)}, u32[]{:S(2)}) %collective-permute-start) | collective-permute-done | bytes 278560 | tf_op jit(solution)/shard_map/ppermute | solution.py:372
  9.8 2.1 %collective-permute-start.6 = (bf16[64,2176]{1,0:T(8,128)(2,1)S(1)}, bf16[64,2176]{1,0:T(8,128)(2,1)S(1)}, u32[]{:S(2)}, u32[]{:S(2)}) collective-permute-start(bf16[64,2176]{1,0:T(8,128)(2,1)S(1)} %collective-permute-done.refs_0_), channel_id=1, source_target_pairs={{0,8},{1,9},{2,10},{3,11},{8,16},{9,17},{10,18},{11,19},{16,24},{1... | collective-permute-start | bytes 835592 | tf_op jit(solution)/shard_map/ppermute | solution.py:372
  11.9 2.0 %collective-permute-start.3 = (bf16[64,2176]{1,0:T(8,128)(2,1)S(1)}, bf16[64,2176]{1,0:T(8,128)(2,1)S(1)}, u32[]{:S(2)}, u32[]{:S(2)}) collective-permute-start(bf16[64,2176]{1,0:T(8,128)(2,1)S(1)} %cut.5), channel_id=1, source_target_pairs={{0,2},{1,3},{2,0},{3,1},{4,6},{5,7},{6,4},{7,5},{8,10},{9,11},{10,... | collective-permute-start | bytes 835592 | tf_op jit(solution)/shard_map/ppermute | solution.py:372
  13.9 0.1 collective-permute-start.9
  14.1 1.4 %stats.6.refs_6_ = f32[128,128]{1,0:T(8,128)S(1)} custom-call(bf16[64,2176]{1,0:T(8,128)(2,1)S(1)} %collective-permute-done.refs_0_, bf16[64,2176]{1,0:T(8,128)(2,1)S(1)} %collective-permute-done.2.refs_1_, bf16[2048,768]{1,0:T(8,128)(2,1)S(1)} %copy-done, bf16[2048,768]{1,0:T(8,128)(2,1)S(1)} %collective-permute-done.1.refs_2_.refs_3_.refs_5_.refs_6_.refs_4_), custom_call_target="tpu_custom_call" | custom-call | flops 805306368 | bytes 6291456 | tf_op jit(solution)/shard_map/stats/pallas_call | solution.py:303
  15.5 2.0 %collective-permute-done.6.refs_0_ = bf16[64,2176]{1,0:T(8,128)(2,1)S(1)} collective-permute-done((bf16[64,2176]{1,0:T(8,128)(2,1)S(1)}, bf16[64,2176]{1,0:T(8,128)(2,1)S(1)}, u32[]{:S(2)}, u32[]{:S(2)}) %collective-permute-start.6) | collective-permute-done | bytes 278560 | tf_op jit(solution)/shard_map/ppermute | solution.py:372
  17.4 1.8 %collective-permute-start.7 = (bf16[64,2176]{1,0:T(8,128)(2,1)S(1)}, bf16[64,2176]{1,0:T(8,128)(2,1)S(1)}, u32[]{:S(2)}, u32[]{:S(2)}) collective-permute-start(bf16[64,2176]{1,0:T(8,128)(2,1)S(1)} %collective-permute-done.6.refs_0_), channel_id=1, source_target_pairs={{0,8},{1,9},{2,10},{3,11},{8,16},{9,17},{10,18},{11,19},{16,24},{1... | collective-permute-start | bytes 835592 | tf_op jit(solution)/shard_map/ppermute | solution.py:372
  19.3 0.2 collective-permute-start.10
  19.5 1.9 %collective-permute-start.4 = (bf16[32,2176]{1,0:T(8,128)(2,1)S(1)}, bf16[32,2176]{1,0:T(8,128)(2,1)S(1)}, u32[]{:S(2)}, u32[]{:S(2)}) collective-permute-start(bf16[32,2176]{1,0:T(8,128)(2,1)S(1)} %get-tuple-element.39), channel_id=1, source_target_pairs={{0,8},{1,9},{2,10},{3,11},{8,16},{9,17},{10,18},{11,19},{16,24},{1... | collective-permute-start | bytes 417800 | tf_op jit(solution)/shard_map/ppermute | solution.py:372
  21.4 0.2 collective-permute-start.5
  21.6 1.5 %collective-permute-done.9.refs_3_ = bf16[64,2176]{1,0:T(8,128)(2,1)S(1)} collective-permute-done((bf16[64,2176]{1,0:T(8,128)(2,1)S(1)}, bf16[64,2176]{1,0:T(8,128)(2,1)S(1)}, u32[]{:S(2)}, u32[]{:S(2)}) %collective-permute-start.9) | collective-permute-done | bytes 278560 | tf_op jit(solution)/shard_map/ppermute | solution.py:372
  23.1 2.4 %collective-permute-start.16 = (bf16[64,2176]{1,0:T(8,128)(2,1)S(1)}, bf16[64,2176]{1,0:T(8,128)(2,1)S(1)}, u32[]{:S(2)}, u32[]{:S(2)}) collective-permute-start(bf16[64,2176]{1,0:T(8,128)(2,1)S(1)} %cut.9), channel_id=1, source_target_pairs={{0,2},{1,3},{2,0},{3,1},{4,6},{5,7},{6,4},{7,5},{8,10},{9,11},{10,... | collective-permute-start | bytes 835592 | tf_op jit(solution)/shard_map/ppermute | solution.py:372
  25.5 2.3 %stats.7.refs_7_ = f32[256,128]{1,0:T(8,128)S(1)} custom-call(bf16[64,2176]{1,0:T(8,128)(2,1)S(1)} %collective-permute-done.6.refs_0_, bf16[64,2176]{1,0:T(8,128)(2,1)S(1)} %collective-permute-done.8.refs_1_, bf16[64,2176]{1,0:T(8,128)(2,1)S(1)} %collective-permute-done.3.refs_0_.refs_2_, bf16[64,2176]{1,0:T(8,128)(2,1)S(1)} %collective-permute-done.9.refs_3_, ...), custom_call_target="tpu_custom_call" | custom-call | flops 1610612736 | bytes 6291456 | tf_op jit(solution)/shard_map/stats/pallas_call | solution.py:303
  27.9 1.6 %collective-permute-start.15 = (bf16[64,2176]{1,0:T(8,128)(2,1)S(1)}, bf16[64,2176]{1,0:T(8,128)(2,1)S(1)}, u32[]{:S(2)}, u32[]{:S(2)}) collective-permute-start(bf16[64,2176]{1,0:T(8,128)(2,1)S(1)} %collective-permute-done.7.refs_0_), channel_id=1, source_target_pairs={{0,8},{1,9},{2,10},{3,11},{8,16},{9,17},{10,18},{11,19},{16,24},{1... | collective-permute-start | bytes 835592 | tf_op jit(solution)/shard_map/ppermute | solution.py:372
  29.5 0.5 collective-permute-start.14
  29.9 0.1 collective-permute-start.13
  30.1 2.0 %collective-permute-start.11 = (bf16[32,2176]{1,0:T(8,128)(2,1)S(1)}, bf16[32,2176]{1,0:T(8,128)(2,1)S(1)}, u32[]{:S(2)}, u32[]{:S(2)}) collective-permute-start(bf16[32,2176]{1,0:T(8,128)(2,1)S(1)} %collective-permute-done.4.refs_2_), channel_id=1, source_target_pairs={{0,8},{1,9},{2,10},{3,11},{8,16},{9,17},{10,18},{11,19},{16,24},{1... | collective-permute-start | bytes 417800 | tf_op jit(solution)/shard_map/ppermute | solution.py:372
  32.1 0.3 collective-permute-start.12
  32.4 2.3 %stats.8.refs_8_ = f32[256,128]{1,0:T(8,128)S(1)} custom-call(bf16[64,2176]{1,0:T(8,128)(2,1)S(1)} %collective-permute-done.7.refs_0_, bf16[64,2176]{1,0:T(8,128)(2,1)S(1)} %collective-permute-done.10.refs_1_, bf16[32,2176]{1,0:T(8,128)(2,1)S(1)} %collective-permute-done.4.refs_2_, bf16[32,2176]{1,0:T(8,128)(2,1)S(1)} %collective-permute-done.5.refs_3_, ...), custom_call_target="tpu_custom_call" | custom-call | flops 1610612736 | bytes 6291456 | tf_op jit(solution)/shard_map/stats/pallas_call | solution.py:303
  34.7 1.5 %collective-permute-done.14.refs_1_ = bf16[64,2176]{1,0:T(8,128)(2,1)S(1)} collective-permute-done((bf16[64,2176]{1,0:T(8,128)(2,1)S(1)}, bf16[64,2176]{1,0:T(8,128)(2,1)S(1)}, u32[]{:S(2)}, u32[]{:S(2)}) %collective-permute-start.14) | collective-permute-done | bytes 278560 | tf_op jit(solution)/shard_map/ppermute | solution.py:372
  36.2 1.4 %stats.9.refs_9_ = f32[128,128]{1,0:T(8,128)S(1)} custom-call(bf16[64,2176]{1,0:T(8,128)(2,1)S(1)} %collective-permute-done.15.refs_0_, bf16[64,2176]{1,0:T(8,128)(2,1)S(1)} %collective-permute-done.14.refs_1_, bf16[2048,768]{1,0:T(8,128)(2,1)S(1)} %copy-done, bf16[2048,768]{1,0:T(8,128)(2,1)S(1)} %collective-permute-done.1.refs_2_.refs_3_.refs_5_.refs_6_.refs_4_), custom_call_target="tpu_custom_call" | custom-call | flops 805306368 | bytes 6291456 | tf_op jit(solution)/shard_map/stats/pallas_call | solution.py:303
  37.6 1.6 %collective-permute-done.12.refs_1_ = bf16[32,2176]{1,0:T(8,128)(2,1)S(1)} collective-permute-done((bf16[32,2176]{1,0:T(8,128)(2,1)S(1)}, bf16[32,2176]{1,0:T(8,128)(2,1)S(1)}, u32[]{:S(2)}, u32[]{:S(2)}) %collective-permute-start.12) | collective-permute-done | bytes 139296 | tf_op jit(solution)/shard_map/ppermute | solution.py:372
  39.2 2.1 %stats_last.1 = f32[32,4,128]{2,1,0:T(4,128)} custom-call(bf16[32,2176]{1,0:T(8,128)(2,1)S(1)} %collective-permute-done.11.refs_0_, bf16[32,2176]{1,0:T(8,128)(2,1)S(1)} %collective-permute-done.12.refs_1_, bf16[64,2176]{1,0:T(8,128)(2,1)S(1)} %collective-permute-done.13.refs_2_, bf16[2048,768]{1,0:T(8,128)(2,1)S(1)} %copy-done, ...), custom_call_target="tpu_custom_call" | custom-call | flops 805306368 | bytes 6291456 | tf_op jit(solution)/shard_map/stats_last/pallas_call | solution.py:303
  41.3 6.1 %all-to-all-start = ((f32[32,4,128]{2,1,0:T(4,128)}), f32[32,4,128]{2,1,0:T(4,128)S(1)}, u32[]{:S(2)}, u32[]{:S(2)}) async-start(f32[32,4,128]{2,1,0:T(4,128)} %stats_last.1), calls=%async_computation | async-start | bytes 131072 | tf_op jit(solution)/shard_map/all_to_all | solution.py:427
  48.1 6.8 %all-to-all-done.r_ref = f32[32,4,128]{2,1,0:T(4,128)S(1)} async-done(((f32[32,4,128]{2,1,0:T(4,128)}), f32[32,4,128]{2,1,0:T(4,128)S(1)}, u32[]{:S(2)}, u32[]{:S(2)}) %all-to-all-start) | async-done | bytes 65568 | tf_op jit(solution)/shard_map/all_to_all | solution.py:427
  54.8 0.7 %finish.1 = (f32[2,128]{1,0:T(2,128)}, f32[2,128]{1,0:T(2,128)}, f32[1,1]{1,0:T(1,128)}, f32[1,1]{1,0:T(1,128)}) custom-call(f32[32,4,128]{2,1,0:T(4,128)S(1)} %all-to-all-done.r_ref, s32[1]{0:T(128)S(6)} %copy.9.len_ref), custom_call_target="tpu_custom_call" | custom-call | tf_op jit(solution)/shard_map/finish/pallas_call | solution.py:349
  (19 shorter events, 0.1 us)
Async XLA Ops:
  0.6 6.0 %copy-start = (bf16[2048,768]{1,0:T(8,128)(2,1)S(1)}, bf16[2048,768]{1,0:T(8,128)(2,1)}, u32[]{:S(2)}) copy-start(bf16[2048,768]{1,0:T(8,128)(2,1)} %refs_3_.1) | copy-start | bytes 9437188
  0.6 6.0 %collective-permute-start.1 = (bf16[2048,768]{1,0:T(8,128)(2,1)}, bf16[2048,768]{1,0:T(8,128)(2,1)S(1)}, u32[]{:S(2)}, u32[]{:S(2)}) collective-permute-start(bf16[2048,768]{1,0:T(8,128)(2,1)} %refs_3_.1), channel_id=1, source_target_pairs={{0,1},{1,0},{2,3},{3,2},{4,5},{5,4},{6,7},{7,6},{8,9},{9,8},{10,11... | collective-permute-start | bytes 9437192 | tf_op jit(solution)/shard_map/ppermute | solution.py:372
  2.8 7.0 %collective-permute-start = (bf16[64,2176]{1,0:T(8,128)(2,1)S(1)}, bf16[64,2176]{1,0:T(8,128)(2,1)S(1)}, u32[]{:S(2)}, u32[]{:S(2)}) collective-permute-start(bf16[64,2176]{1,0:T(8,128)(2,1)S(1)} %get-tuple-element.32), channel_id=1, source_target_pairs={{0,8},{1,9},{2,10},{3,11},{8,16},{9,17},{10,18},{11,19},{16,24},{1... | collective-permute-start | bytes 835592 | tf_op jit(solution)/shard_map/ppermute | solution.py:372
  5.3 6.6 %collective-permute-start.2 = (bf16[64,2176]{1,0:T(8,128)(2,1)S(1)}, bf16[64,2176]{1,0:T(8,128)(2,1)S(1)}, u32[]{:S(2)}, u32[]{:S(2)}) collective-permute-start(bf16[64,2176]{1,0:T(8,128)(2,1)S(1)} %get-tuple-element.36), channel_id=1, source_target_pairs={{0,4},{1,5},{2,6},{3,7},{8,0},{9,1},{10,2},{11,3},{16,8},{17,9},{1... | collective-permute-start | bytes 835592 | tf_op jit(solution)/shard_map/ppermute | solution.py:372
  9.8 7.7 %collective-permute-start.6 = (bf16[64,2176]{1,0:T(8,128)(2,1)S(1)}, bf16[64,2176]{1,0:T(8,128)(2,1)S(1)}, u32[]{:S(2)}, u32[]{:S(2)}) collective-permute-start(bf16[64,2176]{1,0:T(8,128)(2,1)S(1)} %collective-permute-done.refs_0_), channel_id=1, source_target_pairs={{0,8},{1,9},{2,10},{3,11},{8,16},{9,17},{10,18},{11,19},{16,24},{1... | collective-permute-start | bytes 835592 | tf_op jit(solution)/shard_map/ppermute | solution.py:372
  11.9 7.4 %collective-permute-start.8 = (bf16[64,2176]{1,0:T(8,128)(2,1)S(1)}, bf16[64,2176]{1,0:T(8,128)(2,1)S(1)}, u32[]{:S(2)}, u32[]{:S(2)}) collective-permute-start(bf16[64,2176]{1,0:T(8,128)(2,1)S(1)} %collective-permute-done.2.refs_1_), channel_id=1, source_target_pairs={{0,4},{1,5},{2,6},{3,7},{8,0},{9,1},{10,2},{11,3},{16,8},{17,9},{1... | collective-permute-start | bytes 835592 | tf_op jit(solution)/shard_map/ppermute | solution.py:372
  11.9 7.6 %collective-permute-start.3 = (bf16[64,2176]{1,0:T(8,128)(2,1)S(1)}, bf16[64,2176]{1,0:T(8,128)(2,1)S(1)}, u32[]{:S(2)}, u32[]{:S(2)}) collective-permute-start(bf16[64,2176]{1,0:T(8,128)(2,1)S(1)} %cut.5), channel_id=1, source_target_pairs={{0,2},{1,3},{2,0},{3,1},{4,6},{5,7},{6,4},{7,5},{8,10},{9,11},{10,... | collective-permute-start | bytes 835592 | tf_op jit(solution)/shard_map/ppermute | solution.py:372
  13.9 9.2 %collective-permute-start.9 = (bf16[64,2176]{1,0:T(8,128)(2,1)S(1)}, bf16[64,2176]{1,0:T(8,128)(2,1)S(1)}, u32[]{:S(2)}, u32[]{:S(2)}) collective-permute-start(bf16[64,2176]{1,0:T(8,128)(2,1)S(1)} %cut.7), channel_id=1, source_target_pairs={{0,2},{1,3},{2,0},{3,1},{4,6},{5,7},{6,4},{7,5},{8,10},{9,11},{10,... | collective-permute-start | bytes 835592 | tf_op jit(solution)/shard_map/ppermute | solution.py:372
  17.4 10.4 %collective-permute-start.7 = (bf16[64,2176]{1,0:T(8,128)(2,1)S(1)}, bf16[64,2176]{1,0:T(8,128)(2,1)S(1)}, u32[]{:S(2)}, u32[]{:S(2)}) collective-permute-start(bf16[64,2176]{1,0:T(8,128)(2,1)S(1)} %collective-permute-done.6.refs_0_), channel_id=1, source_target_pairs={{0,8},{1,9},{2,10},{3,11},{8,16},{9,17},{10,18},{11,19},{16,24},{1... | collective-permute-start | bytes 835592 | tf_op jit(solution)/shard_map/ppermute | solution.py:372
  19.3 10.2 %collective-permute-start.10 = (bf16[64,2176]{1,0:T(8,128)(2,1)S(1)}, bf16[64,2176]{1,0:T(8,128)(2,1)S(1)}, u32[]{:S(2)}, u32[]{:S(2)}) collective-permute-start(bf16[64,2176]{1,0:T(8,128)(2,1)S(1)} %collective-permute-done.8.refs_1_), channel_id=1, source_target_pairs={{0,4},{1,5},{2,6},{3,7},{8,0},{9,1},{10,2},{11,3},{16,8},{17,9},{1... | collective-permute-start | bytes 835592 | tf_op jit(solution)/shard_map/ppermute | solution.py:372
  19.5 10.4 %collective-permute-start.4 = (bf16[32,2176]{1,0:T(8,128)(2,1)S(1)}, bf16[32,2176]{1,0:T(8,128)(2,1)S(1)}, u32[]{:S(2)}, u32[]{:S(2)}) collective-permute-start(bf16[32,2176]{1,0:T(8,128)(2,1)S(1)} %get-tuple-element.39), channel_id=1, source_target_pairs={{0,8},{1,9},{2,10},{3,11},{8,16},{9,17},{10,18},{11,19},{16,24},{1... | collective-permute-start | bytes 417800 | tf_op jit(solution)/shard_map/ppermute | solution.py:372
  21.4 8.7 %collective-permute-start.5 = (bf16[32,2176]{1,0:T(8,128)(2,1)S(1)}, bf16[32,2176]{1,0:T(8,128)(2,1)S(1)}, u32[]{:S(2)}, u32[]{:S(2)}) collective-permute-start(bf16[32,2176]{1,0:T(8,128)(2,1)S(1)} %get-tuple-element.40), channel_id=1, source_target_pairs={{0,4},{1,5},{2,6},{3,7},{8,0},{9,1},{10,2},{11,3},{16,8},{17,9},{1... | collective-permute-start | bytes 417800 | tf_op jit(solution)/shard_map/ppermute | solution.py:372
  23.1 9.0 %collective-permute-start.16 = (bf16[64,2176]{1,0:T(8,128)(2,1)S(1)}, bf16[64,2176]{1,0:T(8,128)(2,1)S(1)}, u32[]{:S(2)}, u32[]{:S(2)}) collective-permute-start(bf16[64,2176]{1,0:T(8,128)(2,1)S(1)} %cut.9), channel_id=1, source_target_pairs={{0,2},{1,3},{2,0},{3,1},{4,6},{5,7},{6,4},{7,5},{8,10},{9,11},{10,... | collective-permute-start | bytes 835592 | tf_op jit(solution)/shard_map/ppermute | solution.py:372
  27.9 6.8 %collective-permute-start.15 = (bf16[64,2176]{1,0:T(8,128)(2,1)S(1)}, bf16[64,2176]{1,0:T(8,128)(2,1)S(1)}, u32[]{:S(2)}, u32[]{:S(2)}) collective-permute-start(bf16[64,2176]{1,0:T(8,128)(2,1)S(1)} %collective-permute-done.7.refs_0_), channel_id=1, source_target_pairs={{0,8},{1,9},{2,10},{3,11},{8,16},{9,17},{10,18},{11,19},{16,24},{1... | collective-permute-start | bytes 835592 | tf_op jit(solution)/shard_map/ppermute | solution.py:372
  29.5 6.7 %collective-permute-start.14 = (bf16[64,2176]{1,0:T(8,128)(2,1)S(1)}, bf16[64,2176]{1,0:T(8,128)(2,1)S(1)}, u32[]{:S(2)}, u32[]{:S(2)}) collective-permute-start(bf16[64,2176]{1,0:T(8,128)(2,1)S(1)} %collective-permute-done.10.refs_1_), channel_id=1, source_target_pairs={{0,4},{1,5},{2,6},{3,7},{8,0},{9,1},{10,2},{11,3},{16,8},{17,9},{1... | collective-permute-start | bytes 835592 | tf_op jit(solution)/shard_map/ppermute | solution.py:372
  29.9 9.2 %collective-permute-start.13 = (bf16[64,2176]{1,0:T(8,128)(2,1)S(1)}, bf16[64,2176]{1,0:T(8,128)(2,1)S(1)}, u32[]{:S(2)}, u32[]{:S(2)}) collective-permute-start(bf16[64,2176]{1,0:T(8,128)(2,1)S(1)} %cut.8), channel_id=1, source_target_pairs={{0,2},{1,3},{2,0},{3,1},{4,6},{5,7},{6,4},{7,5},{8,10},{9,11},{10,... | collective-permute-start | bytes 835592 | tf_op jit(solution)/shard_map/ppermute | solution.py:372
  30.1 7.5 %collective-permute-start.11 = (bf16[32,2176]{1,0:T(8,128)(2,1)S(1)}, bf16[32,2176]{1,0:T(8,128)(2,1)S(1)}, u32[]{:S(2)}, u32[]{:S(2)}) collective-permute-start(bf16[32,2176]{1,0:T(8,128)(2,1)S(1)} %collective-permute-done.4.refs_2_), channel_id=1, source_target_pairs={{0,8},{1,9},{2,10},{3,11},{8,16},{9,17},{10,18},{11,19},{16,24},{1... | collective-permute-start | bytes 417800 | tf_op jit(solution)/shard_map/ppermute | solution.py:372
  32.1 7.1 %collective-permute-start.12 = (bf16[32,2176]{1,0:T(8,128)(2,1)S(1)}, bf16[32,2176]{1,0:T(8,128)(2,1)S(1)}, u32[]{:S(2)}, u32[]{:S(2)}) collective-permute-start(bf16[32,2176]{1,0:T(8,128)(2,1)S(1)} %collective-permute-done.5.refs_3_), channel_id=1, source_target_pairs={{0,4},{1,5},{2,6},{3,7},{8,0},{9,1},{10,2},{11,3},{16,8},{17,9},{1... | collective-permute-start | bytes 417800 | tf_op jit(solution)/shard_map/ppermute | solution.py:372
  41.3 13.6 %all-to-all-start = ((f32[32,4,128]{2,1,0:T(4,128)}), f32[32,4,128]{2,1,0:T(4,128)S(1)}, u32[]{:S(2)}, u32[]{:S(2)}) async-start(f32[32,4,128]{2,1,0:T(4,128)} %stats_last.1), calls=%async_computation | async-start | bytes 131072 | tf_op jit(solution)/shard_map/all_to_all | solution.py:427

commit v9 on v7

--- a/solution.py
+++ b/solution.py
@@ -13,7 +13,7 @@
 STATS = 4
 DIGIT_BITS = 7
 NOTHING = -1e30
-EARLY_TILES = (32, 32, 16, 16, 16, 16)
+EARLY_TILES = ((32, 16, 16, 16, 16, 16, 16), (32, 32, 16, 16, 16, 16))
 VMEM_BYTES = 10 * 1024 * 1024
 
 
@@ -134,18 +134,20 @@
         lane = lax.broadcasted_iota(jnp.int32, (rows, LANES), 1)
         early_ref[...] = jnp.where(lane == 0, NOTHING, 0.0)
 
-    @pl.when(core == 1)
-    def _():
+    def early(tiles):
         get_head = pltpu.make_async_copy(head_hbm, head_ref, sems.at[3])
         get_head.start()
         get_head.wait()
         ids = [vocab_ids(vdev, req * n_tp + tp)]
         k = 0
-        for size in EARLY_TILES:
-            here = pl.ds(k, size * rows // sum(EARLY_TILES))
+        for size in tiles:
+            here = pl.ds(k, size * rows // sum(tiles))
             k += here.size
             logits = jnp.dot(xn_ref[here, :d], head_ref[...], preferred_element_type=jnp.float32)
             early_ref[here, :] = row_stats(logits, undigits(xn_ref[here, d:]), ids)
+
+    for own_plane, tiles in enumerate(EARLY_TILES):
+        pl.when((core == 1) & (plane == own_plane))(functools.partial(early, tiles))
 
     starts, sizes = segments(rows)
     for ref, flip in ((cw_ref, 0), (ccw_ref, 1)):

time: 55.7 us -> 55.9 us (level)
  no operation moved by 1% of the time
where the time goes in v9:
time: 55.9 us; the launch traced here: 55.7 us
  starting transfers between devices  24.6 us (44%)
  waiting for transfers between devices  15.9 us (28%)
  Pallas kernels  13.8 us (25%)
  between operations  1.38 us (2%)
    ppermute x17, starting transfers between devices, send(): return lax.ppermute(value, AXES, pairs)  18.4 us
    pallas_call x6, Pallas kernels, stats_of(): pl.pallas_call(functools.partial(stats_kernel, metas, n_req, n_tp, rows,...  11.4 us
    ppermute x17, waiting for transfers between devices, send(): return lax.ppermute(value, AXES, pairs)  9.15 us
    all_to_all x1, waiting for transfers between devices, per_device(): received = lax.all_to_all(packed, AXES, 0, 0, tiled=True)  6.76 us
    all_to_all x1, starting transfers between devices, per_device(): received = lax.all_to_all(packed, AXES, 0, 0, tiled=True)  6.2 us
    pallas_call x1, Pallas kernels, norm_rows(): pl.pallas_call(functools.partial(norm_kernel, n_tp), out_shape=[jax.Shape...  1.61 us
  transfers between devices with their start and end apart: 18, of which 7 were waited for; matrix products, arithmetic and copies ran while one was open for 0% of the time, Pallas kernels for 20%

profile of v9, /device:TPU:0, one launch (start us, length us, event | category | flops | bytes accessed | tf_op | source)
XLA Modules:
  0.0 55.7 jit_solution(7938453690225205972)
XLA Ops:
  0.6 0.5 collective-permute-start.1
  1.2 1.6 %norm.1 = (bf16[128,2176]{1,0:T(8,128)(2,1)S(1)}, bf16[64,2176]{1,0:T(8,128)(2,1)S(1)}, bf16[64,2176]{1,0:T(8,128)(2,1)S(1)}, f32[128,128]{1,0:T(8,128)S(1)}) custom-call(bf16[256,2048]{1,0:T(8,128)(2,1)} %x_hbm.1, f32[1,2048]{1,0:T(1,128)} %bitcast.6, s32[2,128]{1,0:T(2,128)} %bitcast.7, bf16[2048,768]{1,0:T(8,128)(2,1)} %refs_3_.1), custom_call_target="tpu_custom_call" | custom-call | tf_op jit(solution)/shard_map/norm/pallas_call | solution.py:167
  2.8 2.5 %collective-permute-start = (bf16[64,2176]{1,0:T(8,128)(2,1)S(1)}, bf16[64,2176]{1,0:T(8,128)(2,1)S(1)}, u32[]{:S(2)}, u32[]{:S(2)}) collective-permute-start(bf16[64,2176]{1,0:T(8,128)(2,1)S(1)} %get-tuple-element.32), channel_id=1, source_target_pairs={{0,8},{1,9},{2,10},{3,11},{8,16},{9,17},{10,18},{11,19},{16,24},{1... | collective-permute-start | bytes 835592 | tf_op jit(solution)/shard_map/ppermute | solution.py:375
  5.3 0.0 collective-permute-start.2
  5.3 1.3 %collective-permute-done.1.refs_2_.refs_3_.refs_5_.refs_6_.refs_4_ = bf16[2048,768]{1,0:T(8,128)(2,1)S(1)} collective-permute-done((bf16[2048,768]{1,0:T(8,128)(2,1)}, bf16[2048,768]{1,0:T(8,128)(2,1)S(1)}, u32[]{:S(2)}, u32[]{:S(2)}) %collective-permute-start.1) | collective-permute-done | bytes 3145760 | tf_op jit(solution)/shard_map/ppermute | solution.py:375
  6.7 1.9 %stats.5.refs_5_ = f32[128,128]{1,0:T(8,128)S(1)} custom-call(bf16[128,2176]{1,0:T(8,128)(2,1)S(1)} %get-tuple-element.33.refs_0_, bf16[2048,768]{1,0:T(8,128)(2,1)S(1)} %copy-done, bf16[2048,768]{1,0:T(8,128)(2,1)S(1)} %collective-permute-done.1.refs_2_.refs_3_.refs_5_.refs_6_.refs_4_, f32[128,128]{1,0:T(8,128)S(1)} %get-tuple-element.34.refs_3_), custom_call_target="tpu_custom_call" | custom-call | flops 805306368 | bytes 6291456 | tf_op jit(solution)/shard_map/stats/pallas_call | solution.py:306
  8.6 1.2 %collective-permute-done.refs_0_ = bf16[64,2176]{1,0:T(8,128)(2,1)S(1)} collective-permute-done((bf16[64,2176]{1,0:T(8,128)(2,1)S(1)}, bf16[64,2176]{1,0:T(8,128)(2,1)S(1)}, u32[]{:S(2)}, u32[]{:S(2)}) %collective-permute-start) | collective-permute-done | bytes 278560 | tf_op jit(solution)/shard_map/ppermute | solution.py:375
  9.8 2.1 %collective-permute-start.6 = (bf16[64,2176]{1,0:T(8,128)(2,1)S(1)}, bf16[64,2176]{1,0:T(8,128)(2,1)S(1)}, u32[]{:S(2)}, u32[]{:S(2)}) collective-permute-start(bf16[64,2176]{1,0:T(8,128)(2,1)S(1)} %collective-permute-done.refs_0_), channel_id=1, source_target_pairs={{0,8},{1,9},{2,10},{3,11},{8,16},{9,17},{10,18},{11,19},{16,24},{1... | collective-permute-start | bytes 835592 | tf_op jit(solution)/shard_map/ppermute | solution.py:375
  11.9 2.0 %collective-permute-start.3 = (bf16[64,2176]{1,0:T(8,128)(2,1)S(1)}, bf16[64,2176]{1,0:T(8,128)(2,1)S(1)}, u32[]{:S(2)}, u32[]{:S(2)}) collective-permute-start(bf16[64,2176]{1,0:T(8,128)(2,1)S(1)} %cut.5), channel_id=1, source_target_pairs={{0,2},{1,3},{2,0},{3,1},{4,6},{5,7},{6,4},{7,5},{8,10},{9,11},{10,... | collective-permute-start | bytes 835592 | tf_op jit(solution)/shard_map/ppermute | solution.py:375
  14.0 0.1 collective-permute-start.9
  14.1 1.4 %stats.6.refs_6_ = f32[128,128]{1,0:T(8,128)S(1)} custom-call(bf16[64,2176]{1,0:T(8,128)(2,1)S(1)} %collective-permute-done.refs_0_, bf16[64,2176]{1,0:T(8,128)(2,1)S(1)} %collective-permute-done.2.refs_1_, bf16[2048,768]{1,0:T(8,128)(2,1)S(1)} %copy-done, bf16[2048,768]{1,0:T(8,128)(2,1)S(1)} %collective-permute-done.1.refs_2_.refs_3_.refs_5_.refs_6_.refs_4_), custom_call_target="tpu_custom_call" | custom-call | flops 805306368 | bytes 6291456 | tf_op jit(solution)/shard_map/stats/pallas_call | solution.py:306
  15.5 2.3 %collective-permute-done.6.refs_0_ = bf16[64,2176]{1,0:T(8,128)(2,1)S(1)} collective-permute-done((bf16[64,2176]{1,0:T(8,128)(2,1)S(1)}, bf16[64,2176]{1,0:T(8,128)(2,1)S(1)}, u32[]{:S(2)}, u32[]{:S(2)}) %collective-permute-start.6) | collective-permute-done | bytes 278560 | tf_op jit(solution)/shard_map/ppermute | solution.py:375
  17.7 1.8 %collective-permute-start.7 = (bf16[64,2176]{1,0:T(8,128)(2,1)S(1)}, bf16[64,2176]{1,0:T(8,128)(2,1)S(1)}, u32[]{:S(2)}, u32[]{:S(2)}) collective-permute-start(bf16[64,2176]{1,0:T(8,128)(2,1)S(1)} %collective-permute-done.6.refs_0_), channel_id=1, source_target_pairs={{0,8},{1,9},{2,10},{3,11},{8,16},{9,17},{10,18},{11,19},{16,24},{1... | collective-permute-start | bytes 835592 | tf_op jit(solution)/shard_map/ppermute | solution.py:375
  19.6 0.2 collective-permute-start.10
  19.8 1.9 %collective-permute-start.4 = (bf16[32,2176]{1,0:T(8,128)(2,1)S(1)}, bf16[32,2176]{1,0:T(8,128)(2,1)S(1)}, u32[]{:S(2)}, u32[]{:S(2)}) collective-permute-start(bf16[32,2176]{1,0:T(8,128)(2,1)S(1)} %get-tuple-element.39), channel_id=1, source_target_pairs={{0,8},{1,9},{2,10},{3,11},{8,16},{9,17},{10,18},{11,19},{16,24},{1... | collective-permute-start | bytes 417800 | tf_op jit(solution)/shard_map/ppermute | solution.py:375
  21.7 0.2 collective-permute-start.5
  21.9 1.2 %collective-permute-done.9.refs_3_ = bf16[64,2176]{1,0:T(8,128)(2,1)S(1)} collective-permute-done((bf16[64,2176]{1,0:T(8,128)(2,1)S(1)}, bf16[64,2176]{1,0:T(8,128)(2,1)S(1)}, u32[]{:S(2)}, u32[]{:S(2)}) %collective-permute-start.9) | collective-permute-done | bytes 278560 | tf_op jit(solution)/shard_map/ppermute | solution.py:375
  23.1 2.5 %collective-permute-start.16 = (bf16[64,2176]{1,0:T(8,128)(2,1)S(1)}, bf16[64,2176]{1,0:T(8,128)(2,1)S(1)}, u32[]{:S(2)}, u32[]{:S(2)}) collective-permute-start(bf16[64,2176]{1,0:T(8,128)(2,1)S(1)} %cut.9), channel_id=1, source_target_pairs={{0,2},{1,3},{2,0},{3,1},{4,6},{5,7},{6,4},{7,5},{8,10},{9,11},{10,... | collective-permute-start | bytes 835592 | tf_op jit(solution)/shard_map/ppermute | solution.py:375
  25.6 2.3 %stats.7.refs_7_ = f32[256,128]{1,0:T(8,128)S(1)} custom-call(bf16[64,2176]{1,0:T(8,128)(2,1)S(1)} %collective-permute-done.6.refs_0_, bf16[64,2176]{1,0:T(8,128)(2,1)S(1)} %collective-permute-done.8.refs_1_, bf16[64,2176]{1,0:T(8,128)(2,1)S(1)} %collective-permute-done.3.refs_0_.refs_2_, bf16[64,2176]{1,0:T(8,128)(2,1)S(1)} %collective-permute-done.9.refs_3_, ...), custom_call_target="tpu_custom_call" | custom-call | flops 1610612736 | bytes 6291456 | tf_op jit(solution)/shard_map/stats/pallas_call | solution.py:306
  27.9 1.6 %collective-permute-start.15 = (bf16[64,2176]{1,0:T(8,128)(2,1)S(1)}, bf16[64,2176]{1,0:T(8,128)(2,1)S(1)}, u32[]{:S(2)}, u32[]{:S(2)}) collective-permute-start(bf16[64,2176]{1,0:T(8,128)(2,1)S(1)} %collective-permute-done.7.refs_0_), channel_id=1, source_target_pairs={{0,8},{1,9},{2,10},{3,11},{8,16},{9,17},{10,18},{11,19},{16,24},{1... | collective-permute-start | bytes 835592 | tf_op jit(solution)/shard_map/ppermute | solution.py:375
  29.5 0.4 collective-permute-start.14
  30.0 0.1 collective-permute-start.13
  30.1 1.6 %collective-permute-start.11 = (bf16[32,2176]{1,0:T(8,128)(2,1)S(1)}, bf16[32,2176]{1,0:T(8,128)(2,1)S(1)}, u32[]{:S(2)}, u32[]{:S(2)}) collective-permute-start(bf16[32,2176]{1,0:T(8,128)(2,1)S(1)} %collective-permute-done.4.refs_2_), channel_id=1, source_target_pairs={{0,8},{1,9},{2,10},{3,11},{8,16},{9,17},{10,18},{11,19},{16,24},{1... | collective-permute-start | bytes 417800 | tf_op jit(solution)/shard_map/ppermute | solution.py:375
  31.7 0.7 %collective-permute-start.12 = (bf16[32,2176]{1,0:T(8,128)(2,1)S(1)}, bf16[32,2176]{1,0:T(8,128)(2,1)S(1)}, u32[]{:S(2)}, u32[]{:S(2)}) collective-permute-start(bf16[32,2176]{1,0:T(8,128)(2,1)S(1)} %collective-permute-done.5.refs_3_), channel_id=1, source_target_pairs={{0,4},{1,5},{2,6},{3,7},{8,0},{9,1},{10,2},{11,3},{16,8},{17,9},{1... | collective-permute-start | bytes 417800 | tf_op jit(solution)/shard_map/ppermute | solution.py:375
  32.4 2.3 %stats.8.refs_8_ = f32[256,128]{1,0:T(8,128)S(1)} custom-call(bf16[64,2176]{1,0:T(8,128)(2,1)S(1)} %collective-permute-done.7.refs_0_, bf16[64,2176]{1,0:T(8,128)(2,1)S(1)} %collective-permute-done.10.refs_1_, bf16[32,2176]{1,0:T(8,128)(2,1)S(1)} %collective-permute-done.4.refs_2_, bf16[32,2176]{1,0:T(8,128)(2,1)S(1)} %collective-permute-done.5.refs_3_, ...), custom_call_target="tpu_custom_call" | custom-call | flops 1610612736 | bytes 6291456 | tf_op jit(solution)/shard_map/stats/pallas_call | solution.py:306
  34.7 1.6 %collective-permute-done.14.refs_1_ = bf16[64,2176]{1,0:T(8,128)(2,1)S(1)} collective-permute-done((bf16[64,2176]{1,0:T(8,128)(2,1)S(1)}, bf16[64,2176]{1,0:T(8,128)(2,1)S(1)}, u32[]{:S(2)}, u32[]{:S(2)}) %collective-permute-start.14) | collective-permute-done | bytes 278560 | tf_op jit(solution)/shard_map/ppermute | solution.py:375
  36.3 1.4 %stats.9.refs_9_ = f32[128,128]{1,0:T(8,128)S(1)} custom-call(bf16[64,2176]{1,0:T(8,128)(2,1)S(1)} %collective-permute-done.15.refs_0_, bf16[64,2176]{1,0:T(8,128)(2,1)S(1)} %collective-permute-done.14.refs_1_, bf16[2048,768]{1,0:T(8,128)(2,1)S(1)} %copy-done, bf16[2048,768]{1,0:T(8,128)(2,1)S(1)} %collective-permute-done.1.refs_2_.refs_3_.refs_5_.refs_6_.refs_4_), custom_call_target="tpu_custom_call" | custom-call | flops 805306368 | bytes 6291456 | tf_op jit(solution)/shard_map/stats/pallas_call | solution.py:306
  37.7 1.6 %collective-permute-done.12.refs_1_ = bf16[32,2176]{1,0:T(8,128)(2,1)S(1)} collective-permute-done((bf16[32,2176]{1,0:T(8,128)(2,1)S(1)}, bf16[32,2176]{1,0:T(8,128)(2,1)S(1)}, u32[]{:S(2)}, u32[]{:S(2)}) %collective-permute-start.12) | collective-permute-done | bytes 139296 | tf_op jit(solution)/shard_map/ppermute | solution.py:375
  39.3 2.1 %stats_last.1 = f32[32,4,128]{2,1,0:T(4,128)} custom-call(bf16[32,2176]{1,0:T(8,128)(2,1)S(1)} %collective-permute-done.11.refs_0_, bf16[32,2176]{1,0:T(8,128)(2,1)S(1)} %collective-permute-done.12.refs_1_, bf16[64,2176]{1,0:T(8,128)(2,1)S(1)} %collective-permute-done.13.refs_2_, bf16[2048,768]{1,0:T(8,128)(2,1)S(1)} %copy-done, ...), custom_call_target="tpu_custom_call" | custom-call | flops 805306368 | bytes 6291456 | tf_op jit(solution)/shard_map/stats_last/pallas_call | solution.py:306
  41.3 6.2 %all-to-all-start = ((f32[32,4,128]{2,1,0:T(4,128)}), f32[32,4,128]{2,1,0:T(4,128)S(1)}, u32[]{:S(2)}, u32[]{:S(2)}) async-start(f32[32,4,128]{2,1,0:T(4,128)} %stats_last.1), calls=%async_computation | async-start | bytes 131072 | tf_op jit(solution)/shard_map/all_to_all | solution.py:430
  48.2 6.8 %all-to-all-done.r_ref = f32[32,4,128]{2,1,0:T(4,128)S(1)} async-done(((f32[32,4,128]{2,1,0:T(4,128)}), f32[32,4,128]{2,1,0:T(4,128)S(1)}, u32[]{:S(2)}, u32[]{:S(2)}) %all-to-all-start) | async-done | bytes 65568 | tf_op jit(solution)/shard_map/all_to_all | solution.py:430
  55.0 0.7 %finish.1 = (f32[2,128]{1,0:T(2,128)}, f32[2,128]{1,0:T(2,128)}, f32[1,1]{1,0:T(1,128)}, f32[1,1]{1,0:T(1,128)}) custom-call(f32[32,4,128]{2,1,0:T(4,128)S(1)} %all-to-all-done.r_ref, s32[1]{0:T(128)S(6)} %copy.9.len_ref), custom_call_target="tpu_custom_call" | custom-call | tf_op jit(solution)/shard_map/finish/pallas_call | solution.py:352
  (19 shorter events, 0.1 us)
Async XLA Ops:
  0.6 6.0 %copy-start = (bf16[2048,768]{1,0:T(8,128)(2,1)S(1)}, bf16[2048,768]{1,0:T(8,128)(2,1)}, u32[]{:S(2)}) copy-start(bf16[2048,768]{1,0:T(8,128)(2,1)} %refs_3_.1) | copy-start | bytes 9437188
  0.6 6.0 %collective-permute-start.1 = (bf16[2048,768]{1,0:T(8,128)(2,1)}, bf16[2048,768]{1,0:T(8,128)(2,1)S(1)}, u32[]{:S(2)}, u32[]{:S(2)}) collective-permute-start(bf16[2048,768]{1,0:T(8,128)(2,1)} %refs_3_.1), channel_id=1, source_target_pairs={{0,1},{1,0},{2,3},{3,2},{4,5},{5,4},{6,7},{7,6},{8,9},{9,8},{10,11... | collective-permute-start | bytes 9437192 | tf_op jit(solution)/shard_map/ppermute | solution.py:375
  2.8 7.0 %collective-permute-start = (bf16[64,2176]{1,0:T(8,128)(2,1)S(1)}, bf16[64,2176]{1,0:T(8,128)(2,1)S(1)}, u32[]{:S(2)}, u32[]{:S(2)}) collective-permute-start(bf16[64,2176]{1,0:T(8,128)(2,1)S(1)} %get-tuple-element.32), channel_id=1, source_target_pairs={{0,8},{1,9},{2,10},{3,11},{8,16},{9,17},{10,18},{11,19},{16,24},{1... | collective-permute-start | bytes 835592 | tf_op jit(solution)/shard_map/ppermute | solution.py:375
  5.3 6.6 %collective-permute-start.2 = (bf16[64,2176]{1,0:T(8,128)(2,1)S(1)}, bf16[64,2176]{1,0:T(8,128)(2,1)S(1)}, u32[]{:S(2)}, u32[]{:S(2)}) collective-permute-start(bf16[64,2176]{1,0:T(8,128)(2,1)S(1)} %get-tuple-element.36), channel_id=1, source_target_pairs={{0,4},{1,5},{2,6},{3,7},{8,0},{9,1},{10,2},{11,3},{16,8},{17,9},{1... | collective-permute-start | bytes 835592 | tf_op jit(solution)/shard_map/ppermute | solution.py:375
  9.8 8.0 %collective-permute-start.6 = (bf16[64,2176]{1,0:T(8,128)(2,1)S(1)}, bf16[64,2176]{1,0:T(8,128)(2,1)S(1)}, u32[]{:S(2)}, u32[]{:S(2)}) collective-permute-start(bf16[64,2176]{1,0:T(8,128)(2,1)S(1)} %collective-permute-done.refs_0_), channel_id=1, source_target_pairs={{0,8},{1,9},{2,10},{3,11},{8,16},{9,17},{10,18},{11,19},{16,24},{1... | collective-permute-start | bytes 835592 | tf_op jit(solution)/shard_map/ppermute | solution.py:375
  11.9 7.7 %collective-permute-start.8 = (bf16[64,2176]{1,0:T(8,128)(2,1)S(1)}, bf16[64,2176]{1,0:T(8,128)(2,1)S(1)}, u32[]{:S(2)}, u32[]{:S(2)}) collective-permute-start(bf16[64,2176]{1,0:T(8,128)(2,1)S(1)} %collective-permute-done.2.refs_1_), channel_id=1, source_target_pairs={{0,4},{1,5},{2,6},{3,7},{8,0},{9,1},{10,2},{11,3},{16,8},{17,9},{1... | collective-permute-start | bytes 835592 | tf_op jit(solution)/shard_map/ppermute | solution.py:375
  11.9 7.9 %collective-permute-start.3 = (bf16[64,2176]{1,0:T(8,128)(2,1)S(1)}, bf16[64,2176]{1,0:T(8,128)(2,1)S(1)}, u32[]{:S(2)}, u32[]{:S(2)}) collective-permute-start(bf16[64,2176]{1,0:T(8,128)(2,1)S(1)} %cut.5), channel_id=1, source_target_pairs={{0,2},{1,3},{2,0},{3,1},{4,6},{5,7},{6,4},{7,5},{8,10},{9,11},{10,... | collective-permute-start | bytes 835592 | tf_op jit(solution)/shard_map/ppermute | solution.py:375
  14.0 9.1 %collective-permute-start.9 = (bf16[64,2176]{1,0:T(8,128)(2,1)S(1)}, bf16[64,2176]{1,0:T(8,128)(2,1)S(1)}, u32[]{:S(2)}, u32[]{:S(2)}) collective-permute-start(bf16[64,2176]{1,0:T(8,128)(2,1)S(1)} %cut.7), channel_id=1, source_target_pairs={{0,2},{1,3},{2,0},{3,1},{4,6},{5,7},{6,4},{7,5},{8,10},{9,11},{10,... | collective-permute-start | bytes 835592 | tf_op jit(solution)/shard_map/ppermute | solution.py:375
  17.7 10.2 %collective-permute-start.7 = (bf16[64,2176]{1,0:T(8,128)(2,1)S(1)}, bf16[64,2176]{1,0:T(8,128)(2,1)S(1)}, u32[]{:S(2)}, u32[]{:S(2)}) collective-permute-start(bf16[64,2176]{1,0:T(8,128)(2,1)S(1)} %collective-permute-done.6.refs_0_), channel_id=1, source_target_pairs={{0,8},{1,9},{2,10},{3,11},{8,16},{9,17},{10,18},{11,19},{16,24},{1... | collective-permute-start | bytes 835592 | tf_op jit(solution)/shard_map/ppermute | solution.py:375
  19.6 9.9 %collective-permute-start.10 = (bf16[64,2176]{1,0:T(8,128)(2,1)S(1)}, bf16[64,2176]{1,0:T(8,128)(2,1)S(1)}, u32[]{:S(2)}, u32[]{:S(2)}) collective-permute-start(bf16[64,2176]{1,0:T(8,128)(2,1)S(1)} %collective-permute-done.8.refs_1_), channel_id=1, source_target_pairs={{0,4},{1,5},{2,6},{3,7},{8,0},{9,1},{10,2},{11,3},{16,8},{17,9},{1... | collective-permute-start | bytes 835592 | tf_op jit(solution)/shard_map/ppermute | solution.py:375
  19.8 10.2 %collective-permute-start.4 = (bf16[32,2176]{1,0:T(8,128)(2,1)S(1)}, bf16[32,2176]{1,0:T(8,128)(2,1)S(1)}, u32[]{:S(2)}, u32[]{:S(2)}) collective-permute-start(bf16[32,2176]{1,0:T(8,128)(2,1)S(1)} %get-tuple-element.39), channel_id=1, source_target_pairs={{0,8},{1,9},{2,10},{3,11},{8,16},{9,17},{10,18},{11,19},{16,24},{1... | collective-permute-start | bytes 417800 | tf_op jit(solution)/shard_map/ppermute | solution.py:375
  21.7 8.4 %collective-permute-start.5 = (bf16[32,2176]{1,0:T(8,128)(2,1)S(1)}, bf16[32,2176]{1,0:T(8,128)(2,1)S(1)}, u32[]{:S(2)}, u32[]{:S(2)}) collective-permute-start(bf16[32,2176]{1,0:T(8,128)(2,1)S(1)} %get-tuple-element.40), channel_id=1, source_target_pairs={{0,4},{1,5},{2,6},{3,7},{8,0},{9,1},{10,2},{11,3},{16,8},{17,9},{1... | collective-permute-start | bytes 417800 | tf_op jit(solution)/shard_map/ppermute | solution.py:375
  23.1 8.6 %collective-permute-start.16 = (bf16[64,2176]{1,0:T(8,128)(2,1)S(1)}, bf16[64,2176]{1,0:T(8,128)(2,1)S(1)}, u32[]{:S(2)}, u32[]{:S(2)}) collective-permute-start(bf16[64,2176]{1,0:T(8,128)(2,1)S(1)} %cut.9), channel_id=1, source_target_pairs={{0,2},{1,3},{2,0},{3,1},{4,6},{5,7},{6,4},{7,5},{8,10},{9,11},{10,... | collective-permute-start | bytes 835592 | tf_op jit(solution)/shard_map/ppermute | solution.py:375
  27.9 6.8 %collective-permute-start.15 = (bf16[64,2176]{1,0:T(8,128)(2,1)S(1)}, bf16[64,2176]{1,0:T(8,128)(2,1)S(1)}, u32[]{:S(2)}, u32[]{:S(2)}) collective-permute-start(bf16[64,2176]{1,0:T(8,128)(2,1)S(1)} %collective-permute-done.7.refs_0_), channel_id=1, source_target_pairs={{0,8},{1,9},{2,10},{3,11},{8,16},{9,17},{10,18},{11,19},{16,24},{1... | collective-permute-start | bytes 835592 | tf_op jit(solution)/shard_map/ppermute | solution.py:375
  29.5 6.8 %collective-permute-start.14 = (bf16[64,2176]{1,0:T(8,128)(2,1)S(1)}, bf16[64,2176]{1,0:T(8,128)(2,1)S(1)}, u32[]{:S(2)}, u32[]{:S(2)}) collective-permute-start(bf16[64,2176]{1,0:T(8,128)(2,1)S(1)} %collective-permute-done.10.refs_1_), channel_id=1, source_target_pairs={{0,4},{1,5},{2,6},{3,7},{8,0},{9,1},{10,2},{11,3},{16,8},{17,9},{1... | collective-permute-start | bytes 835592 | tf_op jit(solution)/shard_map/ppermute | solution.py:375
  30.0 9.3 %collective-permute-start.13 = (bf16[64,2176]{1,0:T(8,128)(2,1)S(1)}, bf16[64,2176]{1,0:T(8,128)(2,1)S(1)}, u32[]{:S(2)}, u32[]{:S(2)}) collective-permute-start(bf16[64,2176]{1,0:T(8,128)(2,1)S(1)} %cut.8), channel_id=1, source_target_pairs={{0,2},{1,3},{2,0},{3,1},{4,6},{5,7},{6,4},{7,5},{8,10},{9,11},{10,... | collective-permute-start | bytes 835592 | tf_op jit(solution)/shard_map/ppermute | solution.py:375
  30.1 7.6 %collective-permute-start.11 = (bf16[32,2176]{1,0:T(8,128)(2,1)S(1)}, bf16[32,2176]{1,0:T(8,128)(2,1)S(1)}, u32[]{:S(2)}, u32[]{:S(2)}) collective-permute-start(bf16[32,2176]{1,0:T(8,128)(2,1)S(1)} %collective-permute-done.4.refs_2_), channel_id=1, source_target_pairs={{0,8},{1,9},{2,10},{3,11},{8,16},{9,17},{10,18},{11,19},{16,24},{1... | collective-permute-start | bytes 417800 | tf_op jit(solution)/shard_map/ppermute | solution.py:375
  31.7 7.6 %collective-permute-start.12 = (bf16[32,2176]{1,0:T(8,128)(2,1)S(1)}, bf16[32,2176]{1,0:T(8,128)(2,1)S(1)}, u32[]{:S(2)}, u32[]{:S(2)}) collective-permute-start(bf16[32,2176]{1,0:T(8,128)(2,1)S(1)} %collective-permute-done.5.refs_3_), channel_id=1, source_target_pairs={{0,4},{1,5},{2,6},{3,7},{8,0},{9,1},{10,2},{11,3},{16,8},{17,9},{1... | collective-permute-start | bytes 417800 | tf_op jit(solution)/shard_map/ppermute | solution.py:375
  41.3 13.6 %all-to-all-start = ((f32[32,4,128]{2,1,0:T(4,128)}), f32[32,4,128]{2,1,0:T(4,128)S(1)}, u32[]{:S(2)}, u32[]{:S(2)}) async-start(f32[32,4,128]{2,1,0:T(4,128)} %stats_last.1), calls=%async_computation | async-start | bytes 131072 | tf_op jit(solution)/shard_map/all_to_all | solution.py:430
